TPU v7x, 32 devices: a whole 2x2x4 slice. The times are simulated.
32 devices in a mesh: gx: 4 (over x, core), gy: 2 (over y), gz: 4 (over z).
Axes of the slice: x: 2, y: 2, z: 4, core: 2. Of those that a mesh axis runs over, the one named last changes fastest.
Arguments:
- cotangent: float32 [16, 128, 512], P('gx', 'gy', 'gz'), may hold values from -6 to 6
- fraction_x: float32 [16, 128, 512], P('gx', 'gy', 'gz'), may hold values from 0 to 1
- fraction_y: float32 [16, 128, 512], P('gx', 'gy', 'gz'), may hold values from 0 to 1
- fraction_z: float32 [16, 128, 512], P('gx', 'gy', 'gz'), may hold values from 0 to 1
- courant_x: float32 [16, 128, 512], P('gx', 'gy', 'gz'), may hold values from -0.3 to 0.3
- courant_y: float32 [16, 128, 512], P('gx', 'gy', 'gz'), may hold values from -0.3 to 0.3
- courant_z: float32 [16, 128, 512], P('gx', 'gy', 'gz'), may hold values from -0.3 to 0.3
- open_cells: int32 [16, 128, 512], P('gx', 'gy', 'gz'), may hold values 0 or 1
Outputs:
- adjoint_fraction: float32 [16, 128, 512], P('gx', 'gy', 'gz')
All inputs are finite; a program needn't handle non-finite values. No bound on the sum of `open_cells` on one device may be relied on, other than what follows from the above.
Results may differ from a plain program's by a relative error of at most 0.0003.
Values sent between devices are 32-bit elements; how exact they have to be, the bound alone decides.
No kernel may reach another device: no remote copies, remote signals or barrier semaphores. Data moves between devices by JAX's collectives and lax.ppermute only.
A program may use at most 64 MiB of HBM per device.

v0:
```python
import jax
import jax.numpy as jnp
from jax import lax
from jax.sharding import PartitionSpec as P

sharpness = 3.5


def padded_2(value, sides, width):
    for axis, dim in sides:
        size, length = (lax.axis_size(axis), value.shape[dim])
        up = [(i, (i + 1) % size) for i in range(size - 1)]
        down = [(j, i) for i, j in up]
        last = lax.slice_in_dim(value, length - width, length, axis=dim)
        first = lax.slice_in_dim(value, 0, width, axis=dim)
        before = lax.ppermute(last, axis, up)
        after = lax.ppermute(first, axis, down)
        value = jnp.concatenate([before, value, after], axis=dim)
    return value


def face_flux(padded, face_rates, along, count):
    before = lax.slice_in_dim(padded, 0, count + 1, axis=along)
    current = lax.slice_in_dim(padded, 1, count + 2, axis=along)
    after = lax.slice_in_dim(padded, 2, count + 3, axis=along)
    further = lax.slice_in_dim(padded, 3, count + 4, axis=along)
    forward = face_rates >= 0.0
    upwind = jnp.where(forward, current, after)
    behind = jnp.where(forward, before, further)
    ahead = jnp.where(forward, after, current)
    slope = jnp.tanh(sharpness * (ahead - behind))
    return face_rates * (upwind + 0.5 * upwind * (1.0 - upwind) * slope)


def change(padded, face_rates, along):
    count = padded.shape[along] - 4
    flux = face_flux(padded, face_rates, along, count)
    lower = lax.slice_in_dim(flux, 0, count, axis=along)
    upper = lax.slice_in_dim(flux, 1, count + 1, axis=along)
    cells = lax.slice_in_dim(padded, 2, count + 2, axis=along)
    rate_lower = lax.slice_in_dim(face_rates, 0, count, axis=along)
    rate_upper = lax.slice_in_dim(face_rates, 1, count + 1, axis=along)
    return lower - upper + cells * (rate_upper - rate_lower)


def pull_back(padded, face_rates, weighted, along):
    _, pullback = jax.vjp(lambda cells: change(cells, face_rates, along), padded)
    return pullback(weighted)[0]


def outer_rims(stacked, along, width):
    if along == 0:
        return padded_2(stacked, (("gx", 1),), width)
    if along == 1:
        return padded_2(stacked, (("gy", 2),), width)
    return padded_2(stacked, (("gz", 3),), width)


def return_rims(edges, along):
    if along == 0:
        return padded_2(edges, (("gx", 0),), 2)
    if along == 1:
        return padded_2(edges, (("gy", 1),), 2)
    return padded_2(edges, (("gz", 2),), 2)


def per_device(
    cotangent, fraction_x, fraction_y, fraction_z, courant_x, courant_y, courant_z, open_cells
):
    opened = open_cells.astype(jnp.float32)
    adjoint = cotangent
    for along, fraction, courant in (
        (2, fraction_z, courant_z),
        (1, fraction_y, courant_y),
        (0, fraction_x, courant_x),
    ):
        count = fraction.shape[along]
        stacked = jnp.stack([fraction, courant])
        weighted = opened * adjoint
        extended = outer_rims(stacked, along, 2)
        padded = extended[0]
        face_rates = lax.slice_in_dim(extended[1], 1, count + 2, axis=along)
        pulled = pull_back(padded, face_rates, weighted, along)
        inner = lax.slice_in_dim(pulled, 2, count + 2, axis=along)
        edges = jnp.concatenate(
            [
                lax.slice_in_dim(pulled, 0, 2, axis=along),
                lax.slice_in_dim(pulled, count + 2, count + 4, axis=along),
            ],
            axis=along,
        )
        arrived = return_rims(edges, along)
        front_pad = [(0, 0), (0, 0), (0, 0)]
        front_pad[along] = (0, count - 2)
        back_pad = [(0, 0), (0, 0), (0, 0)]
        back_pad[along] = (count - 2, 0)
        front = jnp.pad(lax.slice_in_dim(arrived, 0, 2, axis=along), front_pad)
        back = jnp.pad(lax.slice_in_dim(arrived, 6, 8, axis=along), back_pad)
        adjoint = adjoint + inner + front + back
    return adjoint


def solution(mesh):
    placed = (
        P("gx", "gy", "gz"),
        P("gx", "gy", "gz"),
        P("gx", "gy", "gz"),
        P("gx", "gy", "gz"),
        P("gx", "gy", "gz"),
        P("gx", "gy", "gz"),
        P("gx", "gy", "gz"),
        P("gx", "gy", "gz"),
    )
    return jax.shard_map(
        per_device, mesh=mesh, in_specs=placed, out_specs=P("gx", "gy", "gz"), check_vma=False
    )
```

profile of v0, /device:TPU:1, one launch (start us, length us, event | category | flops | bytes accessed | tf_op | source)
XLA Modules:
  0.0 52.8 jit_solution(11649862201137798813)
XLA Ops:
  0.0 1.3 %slice_maximum_fusion = (f32[2,4,64,2]{3,2,1,0:T(8,128)S(1)}, f32[2,4,64,2]{3,2,1,0:T(8,128)S(1)}) fusion(f32[1,4,64,128]{3,2,1,0:T(8,128)} %bitcast.97, f32[1,4,64,128]{3,2,1,0:T(8,128)} %bitcast.99), kind=kLoop, calls=%fused_computation.10 | loop fusion | flops 2048 | bytes 270336 | tf_op jit(solution)/shard_map/stack | solution.py:78
  1.3 4.0 %collective-permute-start = (f32[2,4,64,2]{3,2,1,0:T(8,128)S(1)}, f32[2,4,64,2]{3,2,1,0:T(8,128)S(1)}, u32[]{:S(2)}, u32[]{:S(2)}) collective-permute-start(f32[2,4,64,2]{3,2,1,0:T(8,128)S(1)} %get-tuple-element.41), channel_id=1, source_target_pairs={{0,1},{1,2},{2,3},{4,5},{5,6},{6,7},{8,9},{9,10},{10,11},{12,13},{... | collective-permute-start | bytes 12296 | tf_op jit(solution)/shard_map/ppermute | solution.py:16
  5.3 1.3 %collective-permute-start.1 = (f32[2,4,64,2]{3,2,1,0:T(8,128)S(1)}, f32[2,4,64,2]{3,2,1,0:T(8,128)S(1)}, u32[]{:S(2)}, u32[]{:S(2)}) collective-permute-start(f32[2,4,64,2]{3,2,1,0:T(8,128)S(1)} %get-tuple-element.42), channel_id=1, source_target_pairs={{1,0},{2,1},{3,2},{5,4},{6,5},{7,6},{9,8},{10,9},{11,10},{13,12},{... | collective-permute-start | bytes 12296 | tf_op jit(solution)/shard_map/ppermute | solution.py:17
  6.6 0.0 copy-start
  6.7 0.0 copy-start.1
  6.7 3.3 %collective-permute-start.4 = (f32[2,4,2,128]{3,2,1,0:T(2,128)S(1)}, f32[2,4,2,128]{3,2,1,0:T(2,128)S(1)}, u32[]{:S(2)}, u32[]{:S(2)}) collective-permute-start(f32[2,4,2,128]{3,2,1,0:T(2,128)S(1)} %get-tuple-element.43), channel_id=1, source_target_pairs={{0,4},{1,5},{2,6},{3,7},{8,12},{9,13},{10,14},{11,15},{16,20},{17,... | collective-permute-start | bytes 24584 | tf_op jit(solution)/shard_map/ppermute | solution.py:16
  10.0 1.3 %collective-permute-start.5 = (f32[2,4,2,128]{3,2,1,0:T(2,128)S(1)}, f32[2,4,2,128]{3,2,1,0:T(2,128)S(1)}, u32[]{:S(2)}, u32[]{:S(2)}) collective-permute-start(f32[2,4,2,128]{3,2,1,0:T(2,128)S(1)} %get-tuple-element.44), channel_id=1, source_target_pairs={{4,0},{5,1},{6,2},{7,3},{12,8},{13,9},{14,10},{15,11},{20,16},{21,... | collective-permute-start | bytes 24584 | tf_op jit(solution)/shard_map/ppermute | solution.py:17
  11.3 0.0 copy-done
  11.3 0.0 copy-start.3
  11.3 0.0 copy-start.4
  11.3 4.4 %collective-permute-start.8 = (f32[2,2,64,128]{3,2,1,0:T(8,128)S(1)}, f32[2,2,64,128]{3,2,1,0:T(8,128)S(1)}, u32[]{:S(2)}, u32[]{:S(2)}) collective-permute-start(f32[2,2,64,128]{3,2,1,0:T(8,128)S(1)} %get-tuple-element.45), channel_id=1, source_target_pairs={{0,8},{8,16},{16,24},{1,9},{9,17},{17,25},{2,10},{10,18},{18,26},{... | collective-permute-start | bytes 393224 | tf_op jit(solution)/shard_map/ppermute | solution.py:16
  15.7 0.0 collective-permute-done
  15.7 1.9 %collective-permute-start.9 = (f32[2,2,64,128]{3,2,1,0:T(8,128)S(1)}, f32[2,2,64,128]{3,2,1,0:T(8,128)S(1)}, u32[]{:S(2)}, u32[]{:S(2)}) collective-permute-start(f32[2,2,64,128]{3,2,1,0:T(8,128)S(1)} %get-tuple-element.46), channel_id=1, source_target_pairs={{8,0},{16,8},{24,16},{9,1},{17,9},{25,17},{10,2},{18,10},{26,18},{... | collective-permute-start | bytes 393224 | tf_op jit(solution)/shard_map/ppermute | solution.py:17
  17.7 0.0 collective-permute-done.1
  17.7 0.3 pad_maximum_fusion
  18.0 0.0 copy-start.2
  18.0 0.0 copy-start.5
  18.0 0.8 %copy-done.2 = s32[4,64,128]{2,1,0:T(8,128)S(1)} copy-done((s32[4,64,128]{2,1,0:T(8,128)S(1)}, s32[4,64,128]{2,1,0:T(8,128)}, u32[]{:S(2)}) %copy-start.2) | copy-done | bytes 131096
  18.9 0.1 copy-done.5
  18.9 0.1 fusion.23
  19.1 0.4 negate_select_fusion.1
  19.5 0.3 select_add_fusion.1
  19.9 0.1 select_add_fusion
  19.9 0.3 pad_add_fusion.1
  20.3 0.1 fusion.28
  20.4 4.3 %collective-permute-start.2 = (f32[4,64,2]{2,1,0:T(8,128)S(1)}, f32[4,64,2]{2,1,0:T(8,128)S(1)}, u32[]{:S(2)}, u32[]{:S(2)}) collective-permute-start(f32[4,64,2]{2,1,0:T(8,128)S(1)} %get-tuple-element.39), channel_id=1, source_target_pairs={{0,1},{1,2},{2,3},{4,5},{5,6},{6,7},{8,9},{9,10},{10,11},{12,13},{... | collective-permute-start | bytes 6152 | tf_op jit(solution)/shard_map/ppermute | solution.py:16
  24.7 0.0 collective-permute-done.4
  24.7 1.3 %collective-permute-start.3 = (f32[4,64,2]{2,1,0:T(8,128)S(1)}, f32[4,64,2]{2,1,0:T(8,128)S(1)}, u32[]{:S(2)}, u32[]{:S(2)}) collective-permute-start(f32[4,64,2]{2,1,0:T(8,128)S(1)} %get-tuple-element.40), channel_id=1, source_target_pairs={{1,0},{2,1},{3,2},{5,4},{6,5},{7,6},{9,8},{10,9},{11,10},{13,12},{... | collective-permute-start | bytes 6152 | tf_op jit(solution)/shard_map/ppermute | solution.py:17
  26.0 0.0 collective-permute-done.5
  26.1 0.5 %collective-permute-done.2 = f32[4,64,2]{2,1,0:T(8,128)S(1)} collective-permute-done((f32[4,64,2]{2,1,0:T(8,128)S(1)}, f32[4,64,2]{2,1,0:T(8,128)S(1)}, u32[]{:S(2)}, u32[]{:S(2)}) %collective-permute-start.2) | collective-permute-done | bytes 2080 | tf_op jit(solution)/shard_map/ppermute | solution.py:16
  26.6 3.8 %collective-permute-done.3 = f32[4,64,2]{2,1,0:T(8,128)S(1)} collective-permute-done((f32[4,64,2]{2,1,0:T(8,128)S(1)}, f32[4,64,2]{2,1,0:T(8,128)S(1)}, u32[]{:S(2)}, u32[]{:S(2)}) %collective-permute-start.3) | collective-permute-done | bytes 2080 | tf_op jit(solution)/shard_map/ppermute | solution.py:17
  30.4 0.1 fusion.20
  30.6 0.2 negate_select_fusion.5
  30.7 0.1 select_add_fusion.5
  30.9 4.3 %collective-permute-start.6 = (f32[4,2,128]{2,1,0:T(2,128)S(1)}, f32[4,2,128]{2,1,0:T(2,128)S(1)}, u32[]{:S(2)}, u32[]{:S(2)}) collective-permute-start(f32[4,2,128]{2,1,0:T(2,128)S(1)} %get-tuple-element.31), channel_id=1, source_target_pairs={{0,4},{1,5},{2,6},{3,7},{8,12},{9,13},{10,14},{11,15},{16,20},{17,... | collective-permute-start | bytes 12296 | tf_op jit(solution)/shard_map/ppermute | solution.py:16
  35.2 1.3 %collective-permute-start.7 = (f32[4,2,128]{2,1,0:T(2,128)S(1)}, f32[4,2,128]{2,1,0:T(2,128)S(1)}, u32[]{:S(2)}, u32[]{:S(2)}) collective-permute-start(f32[4,2,128]{2,1,0:T(2,128)S(1)} %get-tuple-element.32), channel_id=1, source_target_pairs={{4,0},{5,1},{6,2},{7,3},{12,8},{13,9},{14,10},{15,11},{20,16},{21,... | collective-permute-start | bytes 12296 | tf_op jit(solution)/shard_map/ppermute | solution.py:17
  36.5 0.1 pad_add_fusion.2
  36.6 0.0 collective-permute-done.8
  36.6 0.0 collective-permute-done.6
  36.6 3.0 %collective-permute-done.7 = f32[4,2,128]{2,1,0:T(2,128)S(1)} collective-permute-done((f32[4,2,128]{2,1,0:T(2,128)S(1)}, f32[4,2,128]{2,1,0:T(2,128)S(1)}, u32[]{:S(2)}, u32[]{:S(2)}) %collective-permute-start.7) | collective-permute-done | bytes 4128 | tf_op jit(solution)/shard_map/ppermute | solution.py:17
  39.7 0.0 collective-permute-done.9
  39.8 0.1 negate_select_fusion.3
  39.9 0.1 select_add_fusion.3
  40.1 6.4 %collective-permute-start.10 = (f32[2,64,128]{2,1,0:T(8,128)S(1)}, f32[2,64,128]{2,1,0:T(8,128)S(1)}, u32[]{:S(2)}, u32[]{:S(2)}) collective-permute-start(f32[2,64,128]{2,1,0:T(8,128)S(1)} %get-tuple-element.29), channel_id=1, source_target_pairs={{0,8},{8,16},{16,24},{1,9},{9,17},{17,25},{2,10},{10,18},{18,26},{... | collective-permute-start | bytes 196616 | tf_op jit(solution)/shard_map/ppermute | solution.py:16
  46.5 1.9 %collective-permute-start.11 = (f32[2,64,128]{2,1,0:T(8,128)S(1)}, f32[2,64,128]{2,1,0:T(8,128)S(1)}, u32[]{:S(2)}, u32[]{:S(2)}) collective-permute-start(f32[2,64,128]{2,1,0:T(8,128)S(1)} %get-tuple-element.30), channel_id=1, source_target_pairs={{8,0},{16,8},{24,16},{9,1},{17,9},{25,17},{10,2},{18,10},{26,18},{... | collective-permute-start | bytes 196616 | tf_op jit(solution)/shard_map/ppermute | solution.py:17
  48.5 0.0 collective-permute-done.10
  48.5 3.6 %collective-permute-done.11 = f32[2,64,128]{2,1,0:T(8,128)S(1)} collective-permute-done((f32[2,64,128]{2,1,0:T(8,128)S(1)}, f32[2,64,128]{2,1,0:T(8,128)S(1)}, u32[]{:S(2)}, u32[]{:S(2)}) %collective-permute-start.11) | collective-permute-done | bytes 65568 | tf_op jit(solution)/shard_map/ppermute | solution.py:17
  52.1 0.7 %fusion.15 = f32[4,64,128]{2,1,0:T(8,128)} fusion(f32[8,64,128]{2,1,0:T(8,128)S(1)} %pad_add_fusion, f32[2,64,128]{2,1,0:T(8,128)S(1)} %collective-permute-done.11, f32[2,64,128]{2,1,0:T(8,128)S(1)} %collective-permute-done.10, f32[4,2,128]{2,1,0:T(2,128)S(1)} %collective-permute-done.7, f32[4,2,128]{2,1,0:T(2,128)S(1)} %collective-permute-done.6, ...), kind=kLoop, calls=%fused_computation.63 | loop fusion | flops 196608 | bytes 663552 | tf_op jit(solution)/shard_map/add | solution.py:99
  (22 shorter events, 0.4 us)
Async XLA Ops:
  0.0 6.6 %copy-start.6 = (f32[4,64,128]{2,1,0:T(8,128)S(1)}, f32[4,64,128]{2,1,0:T(8,128)}, u32[]{:S(2)}) copy-start(f32[4,64,128]{2,1,0:T(8,128)} %param.13) | copy-start | bytes 393220
  0.0 6.6 %copy-start.7 = (f32[4,64,128]{2,1,0:T(8,128)S(1)}, f32[4,64,128]{2,1,0:T(8,128)}, u32[]{:S(2)}) copy-start(f32[4,64,128]{2,1,0:T(8,128)} %param.10) | copy-start | bytes 393220
  1.3 14.5 %collective-permute-start = (f32[2,4,64,2]{3,2,1,0:T(8,128)S(1)}, f32[2,4,64,2]{3,2,1,0:T(8,128)S(1)}, u32[]{:S(2)}, u32[]{:S(2)}) collective-permute-start(f32[2,4,64,2]{3,2,1,0:T(8,128)S(1)} %get-tuple-element.41), channel_id=1, source_target_pairs={{0,1},{1,2},{2,3},{4,5},{5,6},{6,7},{8,9},{9,10},{10,11},{12,13},{... | collective-permute-start | bytes 12296 | tf_op jit(solution)/shard_map/ppermute | solution.py:16
  5.3 12.3 %collective-permute-start.1 = (f32[2,4,64,2]{3,2,1,0:T(8,128)S(1)}, f32[2,4,64,2]{3,2,1,0:T(8,128)S(1)}, u32[]{:S(2)}, u32[]{:S(2)}) collective-permute-start(f32[2,4,64,2]{3,2,1,0:T(8,128)S(1)} %get-tuple-element.42), channel_id=1, source_target_pairs={{1,0},{2,1},{3,2},{5,4},{6,5},{7,6},{9,8},{10,9},{11,10},{13,12},{... | collective-permute-start | bytes 12296 | tf_op jit(solution)/shard_map/ppermute | solution.py:17
  6.6 4.6 %copy-start = (f32[4,64,128]{2,1,0:T(8,128)S(1)}, f32[4,64,128]{2,1,0:T(8,128)}, u32[]{:S(2)}) copy-start(f32[4,64,128]{2,1,0:T(8,128)} %param.12) | copy-start | bytes 393220
  6.7 4.6 %copy-start.1 = (f32[4,64,128]{2,1,0:T(8,128)S(1)}, f32[4,64,128]{2,1,0:T(8,128)}, u32[]{:S(2)}) copy-start(f32[4,64,128]{2,1,0:T(8,128)} %param.9) | copy-start | bytes 393220
  6.7 18.0 %collective-permute-start.4 = (f32[2,4,2,128]{3,2,1,0:T(2,128)S(1)}, f32[2,4,2,128]{3,2,1,0:T(2,128)S(1)}, u32[]{:S(2)}, u32[]{:S(2)}) collective-permute-start(f32[2,4,2,128]{3,2,1,0:T(2,128)S(1)} %get-tuple-element.43), channel_id=1, source_target_pairs={{0,4},{1,5},{2,6},{3,7},{8,12},{9,13},{10,14},{11,15},{16,20},{17,... | collective-permute-start | bytes 24584 | tf_op jit(solution)/shard_map/ppermute | solution.py:16
  10.0 16.0 %collective-permute-start.5 = (f32[2,4,2,128]{3,2,1,0:T(2,128)S(1)}, f32[2,4,2,128]{3,2,1,0:T(2,128)S(1)}, u32[]{:S(2)}, u32[]{:S(2)}) collective-permute-start(f32[2,4,2,128]{3,2,1,0:T(2,128)S(1)} %get-tuple-element.44), channel_id=1, source_target_pairs={{4,0},{5,1},{6,2},{7,3},{12,8},{13,9},{14,10},{15,11},{20,16},{21,... | collective-permute-start | bytes 24584 | tf_op jit(solution)/shard_map/ppermute | solution.py:17
  11.3 6.4 %copy-start.3 = (f32[4,64,128]{2,1,0:T(8,128)S(1)}, f32[4,64,128]{2,1,0:T(8,128)}, u32[]{:S(2)}) copy-start(f32[4,64,128]{2,1,0:T(8,128)} %param.14) | copy-start | bytes 393220
  11.3 6.4 %copy-start.4 = (f32[4,64,128]{2,1,0:T(8,128)S(1)}, f32[4,64,128]{2,1,0:T(8,128)}, u32[]{:S(2)}) copy-start(f32[4,64,128]{2,1,0:T(8,128)} %param.11) | copy-start | bytes 393220
  11.3 25.2 %collective-permute-start.8 = (f32[2,2,64,128]{3,2,1,0:T(8,128)S(1)}, f32[2,2,64,128]{3,2,1,0:T(8,128)S(1)}, u32[]{:S(2)}, u32[]{:S(2)}) collective-permute-start(f32[2,2,64,128]{3,2,1,0:T(8,128)S(1)} %get-tuple-element.45), channel_id=1, source_target_pairs={{0,8},{8,16},{16,24},{1,9},{9,17},{17,25},{2,10},{10,18},{18,26},{... | collective-permute-start | bytes 393224 | tf_op jit(solution)/shard_map/ppermute | solution.py:16
  15.7 24.0 %collective-permute-start.9 = (f32[2,2,64,128]{3,2,1,0:T(8,128)S(1)}, f32[2,2,64,128]{3,2,1,0:T(8,128)S(1)}, u32[]{:S(2)}, u32[]{:S(2)}) collective-permute-start(f32[2,2,64,128]{3,2,1,0:T(8,128)S(1)} %get-tuple-element.46), channel_id=1, source_target_pairs={{8,0},{16,8},{24,16},{9,1},{17,9},{25,17},{10,2},{18,10},{26,18},{... | collective-permute-start | bytes 393224 | tf_op jit(solution)/shard_map/ppermute | solution.py:17
  18.0 0.9 %copy-start.2 = (s32[4,64,128]{2,1,0:T(8,128)S(1)}, s32[4,64,128]{2,1,0:T(8,128)}, u32[]{:S(2)}) copy-start(s32[4,64,128]{2,1,0:T(8,128)} %param.15) | copy-start | bytes 393220
  18.0 1.0 %copy-start.5 = (f32[4,64,128]{2,1,0:T(8,128)S(1)}, f32[4,64,128]{2,1,0:T(8,128)}, u32[]{:S(2)}) copy-start(f32[4,64,128]{2,1,0:T(8,128)} %param.8) | copy-start | bytes 393220
  20.4 6.2 %collective-permute-start.2 = (f32[4,64,2]{2,1,0:T(8,128)S(1)}, f32[4,64,2]{2,1,0:T(8,128)S(1)}, u32[]{:S(2)}, u32[]{:S(2)}) collective-permute-start(f32[4,64,2]{2,1,0:T(8,128)S(1)} %get-tuple-element.39), channel_id=1, source_target_pairs={{0,1},{1,2},{2,3},{4,5},{5,6},{6,7},{8,9},{9,10},{10,11},{12,13},{... | collective-permute-start | bytes 6152 | tf_op jit(solution)/shard_map/ppermute | solution.py:16
  24.7 5.7 %collective-permute-start.3 = (f32[4,64,2]{2,1,0:T(8,128)S(1)}, f32[4,64,2]{2,1,0:T(8,128)S(1)}, u32[]{:S(2)}, u32[]{:S(2)}) collective-permute-start(f32[4,64,2]{2,1,0:T(8,128)S(1)} %get-tuple-element.40), channel_id=1, source_target_pairs={{1,0},{2,1},{3,2},{5,4},{6,5},{7,6},{9,8},{10,9},{11,10},{13,12},{... | collective-permute-start | bytes 6152 | tf_op jit(solution)/shard_map/ppermute | solution.py:17
  30.9 5.7 %collective-permute-start.6 = (f32[4,2,128]{2,1,0:T(2,128)S(1)}, f32[4,2,128]{2,1,0:T(2,128)S(1)}, u32[]{:S(2)}, u32[]{:S(2)}) collective-permute-start(f32[4,2,128]{2,1,0:T(2,128)S(1)} %get-tuple-element.31), channel_id=1, source_target_pairs={{0,4},{1,5},{2,6},{3,7},{8,12},{9,13},{10,14},{11,15},{16,20},{17,... | collective-permute-start | bytes 12296 | tf_op jit(solution)/shard_map/ppermute | solution.py:16
  35.2 4.5 %collective-permute-start.7 = (f32[4,2,128]{2,1,0:T(2,128)S(1)}, f32[4,2,128]{2,1,0:T(2,128)S(1)}, u32[]{:S(2)}, u32[]{:S(2)}) collective-permute-start(f32[4,2,128]{2,1,0:T(2,128)S(1)} %get-tuple-element.32), channel_id=1, source_target_pairs={{4,0},{5,1},{6,2},{7,3},{12,8},{13,9},{14,10},{15,11},{20,16},{21,... | collective-permute-start | bytes 12296 | tf_op jit(solution)/shard_map/ppermute | solution.py:17
  40.1 8.4 %collective-permute-start.10 = (f32[2,64,128]{2,1,0:T(8,128)S(1)}, f32[2,64,128]{2,1,0:T(8,128)S(1)}, u32[]{:S(2)}, u32[]{:S(2)}) collective-permute-start(f32[2,64,128]{2,1,0:T(8,128)S(1)} %get-tuple-element.29), channel_id=1, source_target_pairs={{0,8},{8,16},{16,24},{1,9},{9,17},{17,25},{2,10},{10,18},{18,26},{... | collective-permute-start | bytes 196616 | tf_op jit(solution)/shard_map/ppermute | solution.py:16
  46.5 5.6 %collective-permute-start.11 = (f32[2,64,128]{2,1,0:T(8,128)S(1)}, f32[2,64,128]{2,1,0:T(8,128)S(1)}, u32[]{:S(2)}, u32[]{:S(2)}) collective-permute-start(f32[2,64,128]{2,1,0:T(8,128)S(1)} %get-tuple-element.30), channel_id=1, source_target_pairs={{8,0},{16,8},{24,16},{9,1},{17,9},{25,17},{10,2},{18,10},{26,18},{... | collective-permute-start | bytes 196616 | tf_op jit(solution)/shard_map/ppermute | solution.py:17
where the time goes:
time: 53.2 us; the launch traced here: 52.8 us
  starting transfers between devices  35.6 us (67%)
  waiting for transfers between devices  11 us (21%)
  other arithmetic  4.63 us (9%)
  local copies, waits for them, and re-layouts  1.09 us (2%)
    ppermute x6, starting transfers between devices, padded_2(): before = lax.ppermute(last, axis, up)  26.6 us
    ppermute x6, waiting for transfers between devices, padded_2(): after = lax.ppermute(first, axis, down)  10.4 us
    ppermute x6, starting transfers between devices, padded_2(): after = lax.ppermute(first, axis, down)  9.01 us
    another operation x2, other arithmetic, per_device(): stacked = jnp.stack([fraction, courant])  1.28 us
  transfers between devices with their start and end apart: 12, of which 4 were waited for; matrix products, arithmetic and copies ran while one was open for 5% of the time, Pallas kernels for 0%

commit v1 on v0

v1 whole, which is shorter than its diff:
```python
import functools

import jax
import jax.numpy as jnp
from jax import lax
from jax.experimental import pallas as pl
from jax.experimental.pallas import tpu as pltpu
from jax.sharding import PartitionSpec as P

sharpness = 3.5
slot = 8
AXES = ("gx", "gy", "gz")


def pair_rounds(sizes, along):
    size = sizes[along]
    if size == 1:
        return []
    assert size % 2 == 0

    def perm(partner):
        pairs = []
        for i in range(sizes[0]):
            for j in range(sizes[1]):
                for k in range(sizes[2]):
                    a, b, c = partner(i, j, k)
                    pairs.append(
                        ((i * sizes[1] + j) * sizes[2] + k, (a * sizes[1] + b) * sizes[2] + c)
                    )
        return pairs

    def even(*at):
        at = list(at)
        at[along] ^= 1
        return at

    def odd(*at):
        at = list(at)
        if 0 < at[along] < size - 1:
            at[along] = (at[along] - 1) ^ 1
            at[along] += 1
        elif along != 0 and sizes[0] % 2 == 0:
            at[0] ^= 1
        else:
            at[along] = size - 1 - at[along]
        return at

    return [perm(even)] if size == 2 else [perm(even), perm(odd)]


def roles(axis, size):
    at = lax.axis_index(axis)
    return lax.rem(at, 2) == 0, at > 0, at < size - 1


def to_send(axis, size, up, down):
    if size == 1:
        return []
    even, _, _ = roles(axis, size)
    first = jnp.where(even, up, down)
    return [first] if size == 2 else [first, jnp.where(even, down, up)]


def received(axis, size, messages, like):
    if size == 1:
        return jnp.zeros_like(like), jnp.zeros_like(like)
    even, has_low, has_high = roles(axis, size)
    first, second = messages[0], messages[-1]
    low = jnp.where(even, second, first)
    high = jnp.where(even, first, second)
    return jnp.where(has_low, low, 0.0), jnp.where(has_high, high, 0.0)


def bend(a, difference):
    t = jnp.tanh(sharpness * difference)
    return t, 0.5 * sharpness * a * (1.0 - a) * (1.0 - t * t)


def lower_carry(w, c, a_far, a, b, w0, a0):
    _, g = bend(a, a0 - a_far)
    return ((w0 - w) * jnp.maximum(c, 0.0) - b) * g


def upper_carry(w, a, a_far, forth, w_last, a_last, c_last):
    _, g = bend(a, a_far - a_last)
    return (forth - (w - w_last) * jnp.minimum(c_last, 0.0)) * g


def sweep(g, w, a, c, prev, after, a_low, a_high, w_low, w_high, c_low, r_low, r_high):
    t, bent = bend(a, after(a, a_high) - prev(a, a_low))
    below = prev(c, c_low)
    forth = (after(w, w_high) - w) * jnp.maximum(c, 0.0)
    back = (w - prev(w, w_low)) * jnp.minimum(below, 0.0)
    apart = forth - back
    r = apart * bent
    own = g + w * (c - below) + (forth + back) + apart * ((0.5 - a) * t)
    return own + (prev(r, r_low) - after(r, r_high))


def shifts(shape, dim):
    at = lax.broadcasted_iota(jnp.int32, shape, dim)
    length = shape[dim]

    def prev(value, edge):
        return jnp.where(at == 0, edge, pltpu.roll(value, 1, dim))

    def after(value, edge):
        return jnp.where(at == length - 1, edge, pltpu.roll(value, length - 1, dim))

    return prev, after


def fold(planes, rows, lanes):
    per = lanes // (slot * planes)
    return per if per >= 1 and rows % (8 * per) == 0 else 1


def z_pack(size, cot, opened, a_ref, c_ref, *out):
    planes, rows, lanes = a_ref.shape
    per = fold(planes, rows, lanes)
    step = rows // per
    at = lax.broadcasted_iota(jnp.int32, (rows, lanes), 1)
    totals = [None] * len(out)
    for x in range(planes):
        w = cot[x] * opened[x].astype(jnp.float32)
        a, c = a_ref[x], c_ref[x]
        w1 = pltpu.roll(w, 1, 1)
        back = (w - w1) * jnp.minimum(pltpu.roll(c, 1, 1), 0.0)
        forth = (pltpu.roll(w, lanes - 1, 1) - w) * jnp.maximum(c, 0.0)
        up = jnp.where(
            at < 2,
            jnp.where(at == 0, w1, pltpu.roll(c, 2, 1)),
            jnp.where(at < 4, pltpu.roll(a, 4, 1), pltpu.roll(back, 5, 1)),
        )
        down = jnp.where(
            at == 0, w, jnp.where(at < 3, pltpu.roll(a, 1, 1), pltpu.roll(forth, 3, 1))
        )
        for n, message in enumerate(to_send("gz", size, up, down)):
            message = jnp.where(at < 5, message, 0.0)
            total = totals[n]
            for r in range(per):
                part = message[r * step : (r + 1) * step]
                move = slot * (x + planes * r)
                part = pltpu.roll(part, move, 1) if move else part
                total = part if total is None else total + part
            totals[n] = total
    for ref, total in zip(out, totals):
        ref[...] = total


def z_unpack(message, x, planes, rows, lanes):
    per = fold(planes, rows, lanes)
    parts = []
    for r in range(per):
        move = slot * (x + planes * r)
        parts.append(pltpu.roll(message, lanes - move, 1) if move else message)
    return jnp.concatenate(parts, axis=0)


def z_sweep(sizes, cot, opened, az, cz, ay, cy, *rest):
    n_in = min(sizes[2] - 1, 2)
    messages, (g_ref, *out) = [m[...] for m in rest[:n_in]], rest[n_in:]
    planes, rows, lanes = az.shape
    prev, after = shifts((rows, lanes), 1)
    low_all, high_all = received("gz", sizes[2], messages, az[0])
    tile = lax.broadcasted_iota(jnp.int32, (8, lanes), 0)
    for x in range(planes):
        mask = opened[x].astype(jnp.float32)
        g = cot[x]
        w, a, c = mask * g, az[x], cz[x]
        low = z_unpack(low_all, x, planes, rows, lanes)
        high = z_unpack(high_all, x, planes, rows, lanes)
        lo = [low[:, v : v + 1] for v in range(5)]
        hi = [high[:, v : v + 1] for v in range(4)]
        r_low = lower_carry(*lo, w[:, 0:1], a[:, 0:1])
        r_high = upper_carry(*hi, w[:, lanes - 1 :], a[:, lanes - 1 :], c[:, lanes - 1 :])
        g = sweep(g, w, a, c, prev, after, lo[3], hi[1], lo[0], hi[0], lo[1], r_low, r_high)
        g_ref[x] = g
        if not out:
            continue
        first, last = (mask * g)[:8], (mask * g)[rows - 8 :]
        a_first, a_last = ay[x, :8], ay[x, rows - 8 :]
        c_first, c_last = cy[x, :8], cy[x, rows - 8 :]
        back = (last - pltpu.roll(last, 1, 0)) * jnp.minimum(pltpu.roll(c_last, 1, 0), 0.0)
        forth = (pltpu.roll(first, 7, 0) - first) * jnp.maximum(c_first, 0.0)
        up = jnp.where(
            tile < 2,
            jnp.where(tile == 0, pltpu.roll(last, 1, 0), pltpu.roll(c_last, 2, 0)),
            jnp.where(tile < 4, pltpu.roll(a_last, 4, 0), pltpu.roll(back, 5, 0)),
        )
        down = jnp.where(
            tile == 0,
            first,
            jnp.where(tile < 3, pltpu.roll(a_first, 1, 0), pltpu.roll(forth, 3, 0)),
        )
        for ref, message in zip(out, to_send("gy", sizes[1], up, down)):
            ref[x] = message


def y_sweep(sizes, g_in, opened, ay, cy, ax, cx, *rest):
    n_in = min(sizes[1] - 1, 2)
    messages, (g_ref, *out) = rest[:n_in], rest[n_in:]
    planes, rows, lanes = ay.shape
    prev, after = shifts((rows, lanes), 0)
    ws = []
    for x in range(planes):
        mask = opened[x].astype(jnp.float32)
        g = g_in[x]
        w, a, c = mask * g, ay[x], cy[x]
        low, high = received("gy", sizes[1], [m[x] for m in messages], a[:8])
        lo = [low[v : v + 1] for v in range(5)]
        hi = [high[v : v + 1] for v in range(4)]
        r_low = lower_carry(*lo, w[0:1], a[0:1])
        r_high = upper_carry(*hi, w[rows - 1 :], a[rows - 1 :], c[rows - 1 :])
        g = sweep(g, w, a, c, prev, after, lo[3], hi[1], lo[0], hi[0], lo[1], r_low, r_high)
        g_ref[x] = g
        ws.append(mask * g)
    if out:
        back = (ws[-1] - ws[-2]) * jnp.minimum(cx[planes - 2], 0.0)
        forth = (ws[1] - ws[0]) * jnp.maximum(cx[0], 0.0)
        for v, (up, down) in enumerate(((ws[-1], ws[0]), (back, forth))):
            for ref, message in zip(out, to_send("gx", sizes[0], up, down)):
                ref[v] = message


def x_fields(sizes, ax, cx, *out):
    planes = ax.shape[0]
    pairs = ((ax[planes - 2], ax[0]), (ax[planes - 1], ax[1]), (cx[planes - 1], cx[0]))
    for v, (up, down) in enumerate(pairs):
        for ref, message in zip(out, to_send("gx", sizes[0], up, down)):
            ref[v] = message


def x_sweep(sizes, g_in, opened, ax, cx, *rest):
    n_in = min(sizes[0] - 1, 2)
    fields, late, (out,) = rest[:n_in], rest[n_in : 2 * n_in], rest[2 * n_in :]
    planes = ax.shape[0]
    like = ax[0]
    (f0, h0), (f1, h1), (c_low, _) = (
        received("gx", sizes[0], [m[v] for m in fields], like) for v in range(3)
    )
    (w_low, w_high), (back, forth) = (
        received("gx", sizes[0], [m[v] for m in late], like) for v in range(2)
    )
    g = [g_in[x] for x in range(planes)]
    w = [opened[x].astype(jnp.float32) * g[x] for x in range(planes)]
    a = [ax[x] for x in range(planes)]
    c = [cx[x] for x in range(planes)]
    last = planes - 1
    r = [lower_carry(w_low, c_low, f0, f1, back, w[0], a[0])]
    own = []
    for x in range(planes):
        below = c[x - 1] if x else c_low
        t, bent = bend(a[x], (a[x + 1] if x < last else h0) - (a[x - 1] if x else f1))
        forth_x = ((w[x + 1] if x < last else w_high) - w[x]) * jnp.maximum(c[x], 0.0)
        back_x = (w[x] - (w[x - 1] if x else w_low)) * jnp.minimum(below, 0.0)
        apart = forth_x - back_x
        r.append(apart * bent)
        own.append(
            g[x] + w[x] * (c[x] - below) + (forth_x + back_x) + apart * ((0.5 - a[x]) * t)
        )
    r.append(upper_carry(w_high, h0, h1, forth, w[last], a[last], c[last]))
    for x in range(planes):
        out[x] = own[x] + (r[x] - r[x + 2])


def call(body, out, *args, name):
    shapes = [jax.ShapeDtypeStruct(shape, jnp.float32) for shape in out]
    return pl.pallas_call(
        body,
        out_shape=shapes,
        in_specs=[pl.BlockSpec(memory_space=pltpu.VMEM)] * len(args),
        out_specs=[pl.BlockSpec(memory_space=pltpu.VMEM)] * len(shapes),
        compiler_params=pltpu.CompilerParams(vmem_limit_bytes=8 * 2**20),
        name=name,
    )(*args)


def per_device(sizes, cot, ax, ay, az, cx, cy, cz, opened):
    x_rounds, y_rounds, z_rounds = (pair_rounds(sizes, d) for d in range(3))
    block = az.shape
    planes, rows, lanes = block
    swap = lambda value, perm: lax.ppermute(value, AXES, perm)
    packed = (rows // fold(planes, rows, lanes), lanes)
    z_out = call(
        functools.partial(z_pack, sizes[2]),
        [packed] * len(z_rounds),
        cot, opened, az, cz,
        name="z_pack",
    )
    z_in = [swap(m, p) for m, p in zip(z_out, z_rounds)]
    fields = call(
        functools.partial(x_fields, sizes), [(3, rows, lanes)] * len(x_rounds), ax, cx, name="x_fields"
    )
    fields = [swap(m, p) for m, p in zip(fields, x_rounds)]
    g, *y_out = call(
        functools.partial(z_sweep, sizes),
        [block] + [(planes, 8, lanes)] * len(y_rounds),
        cot, opened, az, cz, ay, cy, *z_in,
        name="z_sweep",
    )
    y_in = [swap(m, p) for m, p in zip(y_out, y_rounds)]
    g, *x_out = call(
        functools.partial(y_sweep, sizes),
        [block] + [(2, rows, lanes)] * len(x_rounds),
        g, opened, ay, cy, ax, cx, *y_in,
        name="y_sweep",
    )
    x_in = [swap(m, p) for m, p in zip(x_out, x_rounds)]
    (g,) = call(
        functools.partial(x_sweep, sizes), [block], g, opened, ax, cx, *fields, *x_in, name="x_sweep"
    )
    return g


def solution(mesh):
    sizes = tuple(mesh.shape[axis] for axis in AXES)
    placed = P(*AXES)
    return jax.shard_map(
        functools.partial(per_device, sizes),
        mesh=mesh,
        in_specs=(placed,) * 8,
        out_specs=placed,
        check_vma=False,
    )
```

time: 53.2 us -> 23.1 us (0.43)
  the two profiles are of different devices: /device:TPU:1 before, /device:TPU:21 now
where the time goes in v1:
time: 23.1 us; the launch traced here: 22.9 us
  waiting for transfers between devices  8.3 us (36%)
  starting transfers between devices  7 us (30%)
  Pallas kernels  3.93 us (17%)
  local copies, waits for them, and re-layouts  3.67 us (16%)
    ppermute x7, waiting for transfers between devices, per_device(): swap = lambda value, perm: lax.ppermute(value, AXES, perm)  8.3 us
    ppermute x7, starting transfers between devices, per_device(): swap = lambda value, perm: lax.ppermute(value, AXES, perm)  7 us
    pallas_call x5, Pallas kernels, call(): pl.pallas_call(body, out_shape=shapes, in_specs=[pl.BlockSpec(memory_spac...  3.93 us
    unnamed x20, local copies, waits for them, and re-layouts  3.67 us
  transfers between devices with their start and end apart: 7, of which 5 were waited for; matrix products, arithmetic and copies ran while one was open for 0% of the time, Pallas kernels for 13%

profile of v1, /device:TPU:21, one launch (start us, length us, event | category | flops | bytes accessed | tf_op | source)
XLA Modules:
  0.0 22.9 jit_solution(13242834680587552931)
XLA Ops:
  0.0 0.0 copy-start
  0.0 0.0 copy-start.1
  0.0 0.9 %copy-done.1 = f32[4,64,128]{2,1,0:T(8,128)S(1)} copy-done((f32[4,64,128]{2,1,0:T(8,128)S(1)}, f32[4,64,128]{2,1,0:T(8,128)}, u32[]{:S(2)}) %copy-start.1) | copy-done | bytes 131096
  0.9 0.0 copy-start.3
  0.9 0.9 %copy-done.3 = f32[4,64,128]{2,1,0:T(8,128)S(1)} copy-done((f32[4,64,128]{2,1,0:T(8,128)S(1)}, f32[4,64,128]{2,1,0:T(8,128)}, u32[]{:S(2)}) %copy-start.3) | copy-done | bytes 131096
  1.8 0.0 copy-start.7
  1.9 0.7 %collective-permute-start.3 = (f32[3,64,128]{2,1,0:T(8,128)S(1)}, f32[3,64,128]{2,1,0:T(8,128)S(1)}, u32[]{:S(2)}, u32[]{:S(2)}) collective-permute-start(f32[3,64,128]{2,1,0:T(8,128)S(1)} %get-tuple-element.19), channel_id=1, source_target_pairs={{0,8},{1,9},{2,10},{3,11},{4,12},{5,13},{6,14},{7,15},{8,0},{9,1},... | collective-permute-start | bytes 294920 | tf_op jit(solution)/shard_map/ppermute | solution.py:283
  2.6 0.0 copy-start.5
  2.6 0.0 copy-start.6
  2.6 1.2 %collective-permute-start.4 = (f32[3,64,128]{2,1,0:T(8,128)S(1)}, f32[3,64,128]{2,1,0:T(8,128)S(1)}, u32[]{:S(2)}, u32[]{:S(2)}) collective-permute-start(f32[3,64,128]{2,1,0:T(8,128)S(1)} %get-tuple-element.20), channel_id=1, source_target_pairs={{0,24},{1,25},{2,26},{3,27},{4,28},{5,29},{6,30},{7,31},{8,16},{9,... | collective-permute-start | bytes 294920 | tf_op jit(solution)/shard_map/ppermute | solution.py:283
  3.8 0.0 copy-done
  3.8 0.0 copy-done.7
  3.8 0.0 copy-start.8
  3.8 0.9 %copy-done.8 = f32[4,64,128]{2,1,0:T(8,128)S(1)} copy-done((f32[4,64,128]{2,1,0:T(8,128)S(1)}, f32[4,64,128]{2,1,0:T(8,128)}, u32[]{:S(2)}) %copy-start.8) | copy-done | bytes 131096
  4.7 0.0 copy-start.9
  4.7 0.9 %copy-done.9 = f32[4,64,128]{2,1,0:T(8,128)S(1)} copy-done((f32[4,64,128]{2,1,0:T(8,128)S(1)}, f32[4,64,128]{2,1,0:T(8,128)}, u32[]{:S(2)}) %copy-start.9) | copy-done | bytes 131096
  5.6 0.7 %z_pack.1 = (f32[16,128]{1,0:T(8,128)S(1)}, f32[16,128]{1,0:T(8,128)S(1)}) custom-call(f32[4,64,128]{2,1,0:T(8,128)S(1)} %copy-done.7, s32[4,64,128]{2,1,0:T(8,128)S(1)} %copy-done, f32[4,64,128]{2,1,0:T(8,128)S(1)} %copy-done.8, f32[4,64,128]{2,1,0:T(8,128)S(1)} %copy-done.9), custom_call_target="tpu_custom_call" | custom-call | tf_op jit(solution)/shard_map/z_pack/pallas_call | solution.py:269
  6.3 1.3 %collective-permute-start = (f32[16,128]{1,0:T(8,128)S(1)}, f32[16,128]{1,0:T(8,128)S(1)}, u32[]{:S(2)}, u32[]{:S(2)}) collective-permute-start(f32[16,128]{1,0:T(8,128)S(1)} %get-tuple-element.14), channel_id=1, source_target_pairs={{0,1},{1,0},{2,3},{3,2},{4,5},{5,4},{6,7},{7,6},{8,9},{9,8},{10,11... | collective-permute-start | bytes 24584 | tf_op jit(solution)/shard_map/ppermute | solution.py:283
  7.6 0.0 copy-start.2
  7.6 0.0 copy-start.4
  7.6 0.0 collective-permute-start.1
  7.6 1.2 %collective-permute-done.rest_0_ = f32[16,128]{1,0:T(8,128)S(1)} collective-permute-done((f32[16,128]{1,0:T(8,128)S(1)}, f32[16,128]{1,0:T(8,128)S(1)}, u32[]{:S(2)}, u32[]{:S(2)}) %collective-permute-start) | collective-permute-done | bytes 8224 | tf_op jit(solution)/shard_map/ppermute | solution.py:283
  8.8 1.3 %collective-permute-done.1.rest_1_ = f32[16,128]{1,0:T(8,128)S(1)} collective-permute-done((f32[16,128]{1,0:T(8,128)S(1)}, f32[16,128]{1,0:T(8,128)S(1)}, u32[]{:S(2)}, u32[]{:S(2)}) %collective-permute-start.1) | collective-permute-done | bytes 8224 | tf_op jit(solution)/shard_map/ppermute | solution.py:283
  10.1 0.0 copy-done.5
  10.1 0.0 copy-done.6
  10.2 2.2 %z_sweep.1 = (f32[4,64,128]{2,1,0:T(8,128)S(1)}, f32[4,8,128]{2,1,0:T(8,128)S(1)}) custom-call(f32[4,64,128]{2,1,0:T(8,128)S(1)} %copy-done.7, s32[4,64,128]{2,1,0:T(8,128)S(1)} %copy-done, f32[4,64,128]{2,1,0:T(8,128)S(1)} %copy-done.8, f32[4,64,128]{2,1,0:T(8,128)S(1)} %copy-done.9, f32[4,64,128]{2,1,0:T(8,128)S(1)} %copy-done.5, ...), custom_call_target="tpu_custom_call" | custom-call | tf_op jit(solution)/shard_map/z_sweep/pallas_call | solution.py:269
  12.3 0.3 %collective-permute-start.2 = (f32[4,8,128]{2,1,0:T(8,128)S(1)}, f32[4,8,128]{2,1,0:T(8,128)S(1)}, u32[]{:S(2)}, u32[]{:S(2)}) collective-permute-start(f32[4,8,128]{2,1,0:T(8,128)S(1)} %get-tuple-element.17), channel_id=1, source_target_pairs={{0,4},{1,5},{2,6},{3,7},{4,0},{5,1},{6,2},{7,3},{8,12},{9,13},{10,... | collective-permute-start | bytes 49160 | tf_op jit(solution)/shard_map/ppermute | solution.py:283
  12.6 2.4 %collective-permute-done.2.rest_0_ = f32[4,8,128]{2,1,0:T(8,128)S(1)} collective-permute-done((f32[4,8,128]{2,1,0:T(8,128)S(1)}, f32[4,8,128]{2,1,0:T(8,128)S(1)}, u32[]{:S(2)}, u32[]{:S(2)}) %collective-permute-start.2) | collective-permute-done | bytes 16416 | tf_op jit(solution)/shard_map/ppermute | solution.py:283
  15.0 0.0 copy-done.2
  15.0 0.0 copy-done.4
  15.0 0.2 %y_sweep.1 = (f32[4,64,128]{2,1,0:T(8,128)S(1)}, f32[2,64,128]{2,1,0:T(8,128)S(1)}, f32[2,64,128]{2,1,0:T(8,128)S(1)}) custom-call(f32[4,64,128]{2,1,0:T(8,128)S(1)} %get-tuple-element.16.g_in, s32[4,64,128]{2,1,0:T(8,128)S(1)} %copy-done, f32[4,64,128]{2,1,0:T(8,128)S(1)} %copy-done.5, f32[4,64,128]{2,1,0:T(8,128)S(1)} %copy-done.6, ...), custom_call_target="tpu_custom_call" | custom-call | tf_op jit(solution)/shard_map/y_sweep/pallas_call | solution.py:269
  15.2 3.1 %collective-permute-start.5 = (f32[2,64,128]{2,1,0:T(8,128)S(1)}, f32[2,64,128]{2,1,0:T(8,128)S(1)}, u32[]{:S(2)}, u32[]{:S(2)}) collective-permute-start(f32[2,64,128]{2,1,0:T(8,128)S(1)} %get-tuple-element.21), channel_id=1, source_target_pairs={{0,8},{1,9},{2,10},{3,11},{4,12},{5,13},{6,14},{7,15},{8,0},{9,1},... | collective-permute-start | bytes 196616 | tf_op jit(solution)/shard_map/ppermute | solution.py:283
  18.3 0.3 %collective-permute-start.6 = (f32[2,64,128]{2,1,0:T(8,128)S(1)}, f32[2,64,128]{2,1,0:T(8,128)S(1)}, u32[]{:S(2)}, u32[]{:S(2)}) collective-permute-start(f32[2,64,128]{2,1,0:T(8,128)S(1)} %get-tuple-element.22), channel_id=1, source_target_pairs={{0,24},{1,25},{2,26},{3,27},{4,28},{5,29},{6,30},{7,31},{8,16},{9,... | collective-permute-start | bytes 196616 | tf_op jit(solution)/shard_map/ppermute | solution.py:283
  18.7 0.6 %collective-permute-done.5.rest_2_ = f32[2,64,128]{2,1,0:T(8,128)S(1)} collective-permute-done((f32[2,64,128]{2,1,0:T(8,128)S(1)}, f32[2,64,128]{2,1,0:T(8,128)S(1)}, u32[]{:S(2)}, u32[]{:S(2)}) %collective-permute-start.5) | collective-permute-done | bytes 65568 | tf_op jit(solution)/shard_map/ppermute | solution.py:283
  19.2 2.9 %collective-permute-done.6.rest_3_ = f32[2,64,128]{2,1,0:T(8,128)S(1)} collective-permute-done((f32[2,64,128]{2,1,0:T(8,128)S(1)}, f32[2,64,128]{2,1,0:T(8,128)S(1)}, u32[]{:S(2)}, u32[]{:S(2)}) %collective-permute-start.6) | collective-permute-done | bytes 65568 | tf_op jit(solution)/shard_map/ppermute | solution.py:283
  22.1 0.0 collective-permute-done.3.rest_0_
  22.1 0.0 collective-permute-done.4.rest_1_
  22.1 0.8 %x_sweep.1 = f32[4,64,128]{2,1,0:T(8,128)} custom-call(f32[4,64,128]{2,1,0:T(8,128)S(1)} %get-tuple-element.18.g_in, s32[4,64,128]{2,1,0:T(8,128)S(1)} %copy-done, f32[4,64,128]{2,1,0:T(8,128)S(1)} %copy-done.2, f32[4,64,128]{2,1,0:T(8,128)S(1)} %copy-done.4, f32[3,64,128]{2,1,0:T(8,128)S(1)} %collective-permute-done.3.rest_0_, ...), custom_call_target="tpu_custom_call" | custom-call | tf_op jit(solution)/shard_map/x_sweep/pallas_call | solution.py:269
  (1 shorter events, 0.0 us)
Async XLA Ops:
  0.0 3.8 %copy-start = (s32[4,64,128]{2,1,0:T(8,128)S(1)}, s32[4,64,128]{2,1,0:T(8,128)}, u32[]{:S(2)}) copy-start(s32[4,64,128]{2,1,0:T(8,128)} %opened.7) | copy-start | bytes 393220
  0.0 0.9 %copy-start.1 = (f32[4,64,128]{2,1,0:T(8,128)S(1)}, f32[4,64,128]{2,1,0:T(8,128)}, u32[]{:S(2)}) copy-start(f32[4,64,128]{2,1,0:T(8,128)} %ax.5) | copy-start | bytes 393220
  0.9 0.9 %copy-start.3 = (f32[4,64,128]{2,1,0:T(8,128)S(1)}, f32[4,64,128]{2,1,0:T(8,128)}, u32[]{:S(2)}) copy-start(f32[4,64,128]{2,1,0:T(8,128)} %cx.5) | copy-start | bytes 393220
  1.8 2.0 %copy-start.7 = (f32[4,64,128]{2,1,0:T(8,128)S(1)}, f32[4,64,128]{2,1,0:T(8,128)}, u32[]{:S(2)}) copy-start(f32[4,64,128]{2,1,0:T(8,128)} %cot.3) | copy-start | bytes 393220
  1.9 20.2 %collective-permute-start.3 = (f32[3,64,128]{2,1,0:T(8,128)S(1)}, f32[3,64,128]{2,1,0:T(8,128)S(1)}, u32[]{:S(2)}, u32[]{:S(2)}) collective-permute-start(f32[3,64,128]{2,1,0:T(8,128)S(1)} %get-tuple-element.19), channel_id=1, source_target_pairs={{0,8},{1,9},{2,10},{3,11},{4,12},{5,13},{6,14},{7,15},{8,0},{9,1},... | collective-permute-start | bytes 294920 | tf_op jit(solution)/shard_map/ppermute | solution.py:283
  2.6 7.5 %copy-start.5 = (f32[4,64,128]{2,1,0:T(8,128)S(1)}, f32[4,64,128]{2,1,0:T(8,128)}, u32[]{:S(2)}) copy-start(f32[4,64,128]{2,1,0:T(8,128)} %ay.3) | copy-start | bytes 393220
  2.6 7.5 %copy-start.6 = (f32[4,64,128]{2,1,0:T(8,128)S(1)}, f32[4,64,128]{2,1,0:T(8,128)}, u32[]{:S(2)}) copy-start(f32[4,64,128]{2,1,0:T(8,128)} %cy.3) | copy-start | bytes 393220
  2.6 19.5 %collective-permute-start.4 = (f32[3,64,128]{2,1,0:T(8,128)S(1)}, f32[3,64,128]{2,1,0:T(8,128)S(1)}, u32[]{:S(2)}, u32[]{:S(2)}) collective-permute-start(f32[3,64,128]{2,1,0:T(8,128)S(1)} %get-tuple-element.20), channel_id=1, source_target_pairs={{0,24},{1,25},{2,26},{3,27},{4,28},{5,29},{6,30},{7,31},{8,16},{9,... | collective-permute-start | bytes 294920 | tf_op jit(solution)/shard_map/ppermute | solution.py:283
  3.8 0.9 %copy-start.8 = (f32[4,64,128]{2,1,0:T(8,128)S(1)}, f32[4,64,128]{2,1,0:T(8,128)}, u32[]{:S(2)}) copy-start(f32[4,64,128]{2,1,0:T(8,128)} %az.1) | copy-start | bytes 393220
  4.7 0.9 %copy-start.9 = (f32[4,64,128]{2,1,0:T(8,128)S(1)}, f32[4,64,128]{2,1,0:T(8,128)}, u32[]{:S(2)}) copy-start(f32[4,64,128]{2,1,0:T(8,128)} %cz.1) | copy-start | bytes 393220
  6.3 2.6 %collective-permute-start = (f32[16,128]{1,0:T(8,128)S(1)}, f32[16,128]{1,0:T(8,128)S(1)}, u32[]{:S(2)}, u32[]{:S(2)}) collective-permute-start(f32[16,128]{1,0:T(8,128)S(1)} %get-tuple-element.14), channel_id=1, source_target_pairs={{0,1},{1,0},{2,3},{3,2},{4,5},{5,4},{6,7},{7,6},{8,9},{9,8},{10,11... | collective-permute-start | bytes 24584 | tf_op jit(solution)/shard_map/ppermute | solution.py:283
  7.6 7.3 %copy-start.2 = (f32[4,64,128]{2,1,0:T(8,128)S(1)}, f32[4,64,128]{2,1,0:T(8,128)}, u32[]{:S(2)}) copy-start(f32[4,64,128]{2,1,0:T(8,128)} %ax.5) | copy-start | bytes 393220
  7.6 7.3 %copy-start.4 = (f32[4,64,128]{2,1,0:T(8,128)S(1)}, f32[4,64,128]{2,1,0:T(8,128)}, u32[]{:S(2)}) copy-start(f32[4,64,128]{2,1,0:T(8,128)} %cx.5) | copy-start | bytes 393220
  7.6 2.5 %collective-permute-start.1 = (f32[16,128]{1,0:T(8,128)S(1)}, f32[16,128]{1,0:T(8,128)S(1)}, u32[]{:S(2)}, u32[]{:S(2)}) collective-permute-start(f32[16,128]{1,0:T(8,128)S(1)} %get-tuple-element.15), channel_id=1, source_target_pairs={{0,8},{1,2},{2,1},{3,11},{4,12},{5,6},{6,5},{7,15},{8,0},{9,10},{1... | collective-permute-start | bytes 24584 | tf_op jit(solution)/shard_map/ppermute | solution.py:283
  12.3 2.7 %collective-permute-start.2 = (f32[4,8,128]{2,1,0:T(8,128)S(1)}, f32[4,8,128]{2,1,0:T(8,128)S(1)}, u32[]{:S(2)}, u32[]{:S(2)}) collective-permute-start(f32[4,8,128]{2,1,0:T(8,128)S(1)} %get-tuple-element.17), channel_id=1, source_target_pairs={{0,4},{1,5},{2,6},{3,7},{4,0},{5,1},{6,2},{7,3},{8,12},{9,13},{10,... | collective-permute-start | bytes 49160 | tf_op jit(solution)/shard_map/ppermute | solution.py:283
  15.2 4.0 %collective-permute-start.5 = (f32[2,64,128]{2,1,0:T(8,128)S(1)}, f32[2,64,128]{2,1,0:T(8,128)S(1)}, u32[]{:S(2)}, u32[]{:S(2)}) collective-permute-start(f32[2,64,128]{2,1,0:T(8,128)S(1)} %get-tuple-element.21), channel_id=1, source_target_pairs={{0,8},{1,9},{2,10},{3,11},{4,12},{5,13},{6,14},{7,15},{8,0},{9,1},... | collective-permute-start | bytes 196616 | tf_op jit(solution)/shard_map/ppermute | solution.py:283
  18.3 3.8 %collective-permute-start.6 = (f32[2,64,128]{2,1,0:T(8,128)S(1)}, f32[2,64,128]{2,1,0:T(8,128)S(1)}, u32[]{:S(2)}, u32[]{:S(2)}) collective-permute-start(f32[2,64,128]{2,1,0:T(8,128)S(1)} %get-tuple-element.22), channel_id=1, source_target_pairs={{0,24},{1,25},{2,26},{3,27},{4,28},{5,29},{6,30},{7,31},{8,16},{9,... | collective-permute-start | bytes 196616 | tf_op jit(solution)/shard_map/ppermute | solution.py:283

commit v2 on v1

--- a/solution.py
+++ b/solution.py
@@ -115,69 +115,114 @@
     return per if per >= 1 and rows % (8 * per) == 0 else 1
 
 
-def z_pack(size, cot, opened, a_ref, c_ref, *out):
-    planes, rows, lanes = a_ref.shape
+def edge_lanes(shape, lanes):
+    at = lax.broadcasted_iota(jnp.int32, shape, 1)
+    return at, lax.rem(at, slot)
+
+
+def z_pack(size, planes, rows, lanes, cot_in, opened_in, a_in, c_in, *out):
+    cot, opened, a_ref, c_ref, w_ref, edge_ref, *out, sems = out
+    copies = [
+        pltpu.make_async_copy(src, dst, sems.at[n])
+        for n, (src, dst) in enumerate(
+            ((cot_in, cot), (opened_in, opened), (a_in, a_ref), (c_in, c_ref))
+        )
+    ]
+    for copy in copies:
+        copy.start()
+    for copy in copies:
+        copy.wait()
     per = fold(planes, rows, lanes)
     step = rows // per
+    at, place = edge_lanes((rows, lanes), lanes)
+    near = (at < 2) | (at >= lanes - 2)
+    totals = [None] * 3
+    for x in range(planes):
+        w = cot[x] * opened[x].astype(jnp.float32)
+        w_ref[x] = w
+        for n, field in enumerate((w, a_ref[x], c_ref[x])):
+            field = jnp.where(near, field, 0.0)
+            for r in range(per):
+                move = slot * (x + planes * r)
+                part = field[r * step : (r + 1) * step]
+                part = pltpu.roll(part, move, 1) if move else part
+                totals[n] = part if totals[n] is None else totals[n] + part
+    for n in range(3):
+        edge_ref[n] = totals[n]
+    _, place = edge_lanes((step, lanes), lanes)
+    ends = [jnp.where(place >= slot - 2, total, 0.0) for total in totals]
+    starts = [jnp.where(place < 2, total, 0.0) for total in totals]
+    up = sum(pltpu.roll(end, 2 + 2 * n, 1) for n, end in enumerate(ends))
+    down = sum(pltpu.roll(start, 2 * n, 1) if n else start for n, start in enumerate(starts))
+    for ref, message in zip(out, to_send("gz", size, up, down)):
+        ref[...] = message
+
+
+def z_inner(g_ref, w_ref, a_ref, c_ref, out):
+    planes, rows, lanes = a_ref.shape
     at = lax.broadcasted_iota(jnp.int32, (rows, lanes), 1)
-    totals = [None] * len(out)
-    for x in range(planes):
-        w = cot[x] * opened[x].astype(jnp.float32)
-        a, c = a_ref[x], c_ref[x]
-        w1 = pltpu.roll(w, 1, 1)
-        back = (w - w1) * jnp.minimum(pltpu.roll(c, 1, 1), 0.0)
-        forth = (pltpu.roll(w, lanes - 1, 1) - w) * jnp.maximum(c, 0.0)
-        up = jnp.where(
-            at < 2,
-            jnp.where(at == 0, w1, pltpu.roll(c, 2, 1)),
-            jnp.where(at < 4, pltpu.roll(a, 4, 1), pltpu.roll(back, 5, 1)),
-        )
-        down = jnp.where(
-            at == 0, w, jnp.where(at < 3, pltpu.roll(a, 1, 1), pltpu.roll(forth, 3, 1))
-        )
-        for n, message in enumerate(to_send("gz", size, up, down)):
-            message = jnp.where(at < 5, message, 0.0)
-            total = totals[n]
-            for r in range(per):
-                part = message[r * step : (r + 1) * step]
-                move = slot * (x + planes * r)
-                part = pltpu.roll(part, move, 1) if move else part
-                total = part if total is None else total + part
-            totals[n] = total
-    for ref, total in zip(out, totals):
-        ref[...] = total
-
-
-def z_unpack(message, x, planes, rows, lanes):
-    per = fold(planes, rows, lanes)
-    parts = []
-    for r in range(per):
-        move = slot * (x + planes * r)
-        parts.append(pltpu.roll(message, lanes - move, 1) if move else message)
-    return jnp.concatenate(parts, axis=0)
-
-
-def z_sweep(sizes, cot, opened, az, cz, ay, cy, *rest):
+    inside = (at > 0) & (at < lanes - 1)
+    prev = lambda value: pltpu.roll(value, 1, 1)
+    after = lambda value: pltpu.roll(value, lanes - 1, 1)
+    for x in range(planes):
+        w, a, c = w_ref[x], a_ref[x], c_ref[x]
+        t, bent = bend(a, after(a) - prev(a))
+        below = prev(c)
+        forth = (after(w) - w) * jnp.maximum(c, 0.0)
+        back = (w - prev(w)) * jnp.minimum(below, 0.0)
+        apart = jnp.where(inside, forth - back, 0.0)
+        own = jnp.where(inside, w * (c - below) + (forth + back), 0.0) + apart * ((0.5 - a) * t)
+        r = apart * bent
+        out[x] = g_ref[x] + own + (prev(r) - after(r))
+
+
+def z_ends(edges, low, high, lanes):
+    shift = lambda value, by: pltpu.roll(value, by % lanes, 1)
+    w, a, c = edges
+    _, place = edge_lanes(w.shape, lanes)
+    w0, w1, a0, a1, c0 = w, shift(w, -1), a, shift(a, -1), c
+    w_far, w_low, a_far, a_low, c_far, c_low = (shift(low, -v) if v else low for v in range(6))
+    r_low = lower_carry(w_low, c_low, a_far, a_low, (w_low - w_far) * jnp.minimum(c_far, 0.0), w0, a0)
+    forth = (w1 - w0) * jnp.maximum(c0, 0.0)
+    back = (w0 - w_low) * jnp.minimum(c_low, 0.0)
+    t, bent = bend(a0, a1 - a_low)
+    first = w0 * (c0 - c_low) + (forth + back) + (forth - back) * ((0.5 - a0) * t) + r_low
+    second = (forth - back) * bent
+    w1, a1, c1 = shift(w, 1), shift(a, 1), shift(c, 1)
+    w0, a0, c0 = shift(w, 2), shift(a, 2), shift(c, 2)
+    w_high, w_far, a_high, a_far, c_high = (shift(high, -v) if v else high for v in range(5))
+    r_high = upper_carry(w_high, a_high, a_far, (w_far - w_high) * jnp.maximum(c_high, 0.0), w1, a1, c1)
+    forth = (w_high - w1) * jnp.maximum(c1, 0.0)
+    back = (w1 - w0) * jnp.minimum(c0, 0.0)
+    t, bent = bend(a1, a_high - a0)
+    last = w1 * (c1 - c0) + (forth + back) + (forth - back) * ((0.5 - a1) * t) - r_high
+    before = (back - forth) * bent
+    ends = jnp.where(place == 0, first, jnp.where(place == 1, shift(second, 1), 0.0))
+    return jnp.where(
+        place == slot - 1, shift(last, -1), jnp.where(place == slot - 2, shift(before, -2), ends)
+    )
+
+
+def z_sweep(sizes, partial, edges, opened, ay, cy, *rest):
     n_in = min(sizes[2] - 1, 2)
     messages, (g_ref, *out) = [m[...] for m in rest[:n_in]], rest[n_in:]
-    planes, rows, lanes = az.shape
-    prev, after = shifts((rows, lanes), 1)
-    low_all, high_all = received("gz", sizes[2], messages, az[0])
+    planes, rows, lanes = ay.shape
+    low, high = received("gz", sizes[2], messages, edges[0])
+    ends = z_ends([edges[n] for n in range(3)], low, high, lanes)
+    at = lax.broadcasted_iota(jnp.int32, (rows, lanes), 1)
+    near = (at < 2) | (at >= lanes - 2)
+    per = fold(planes, rows, lanes)
     tile = lax.broadcasted_iota(jnp.int32, (8, lanes), 0)
     for x in range(planes):
-        mask = opened[x].astype(jnp.float32)
-        g = cot[x]
-        w, a, c = mask * g, az[x], cz[x]
-        low = z_unpack(low_all, x, planes, rows, lanes)
-        high = z_unpack(high_all, x, planes, rows, lanes)
-        lo = [low[:, v : v + 1] for v in range(5)]
-        hi = [high[:, v : v + 1] for v in range(4)]
-        r_low = lower_carry(*lo, w[:, 0:1], a[:, 0:1])
-        r_high = upper_carry(*hi, w[:, lanes - 1 :], a[:, lanes - 1 :], c[:, lanes - 1 :])
-        g = sweep(g, w, a, c, prev, after, lo[3], hi[1], lo[0], hi[0], lo[1], r_low, r_high)
+        parts = []
+        for r in range(per):
+            move = slot * (x + planes * r)
+            parts.append(pltpu.roll(ends, lanes - move, 1) if move else ends)
+        g = partial[x] + jnp.where(near, jnp.concatenate(parts, axis=0), 0.0)
         g_ref[x] = g
         if not out:
             continue
+        mask = opened[x].astype(jnp.float32)
         first, last = (mask * g)[:8], (mask * g)[rows - 8 :]
         a_first, a_last = ay[x, :8], ay[x, rows - 8 :]
         c_first, c_last = cy[x, :8], cy[x, rows - 8 :]
@@ -218,29 +263,25 @@
     if out:
         back = (ws[-1] - ws[-2]) * jnp.minimum(cx[planes - 2], 0.0)
         forth = (ws[1] - ws[0]) * jnp.maximum(cx[0], 0.0)
-        for v, (up, down) in enumerate(((ws[-1], ws[0]), (back, forth))):
+        pairs = (
+            (ws[-1], ws[0]),
+            (back, forth),
+            (ax[planes - 2], ax[0]),
+            (ax[planes - 1], ax[1]),
+            (cx[planes - 1], cx[0]),
+        )
+        for v, (up, down) in enumerate(pairs):
             for ref, message in zip(out, to_send("gx", sizes[0], up, down)):
                 ref[v] = message
 
 
-def x_fields(sizes, ax, cx, *out):
-    planes = ax.shape[0]
-    pairs = ((ax[planes - 2], ax[0]), (ax[planes - 1], ax[1]), (cx[planes - 1], cx[0]))
-    for v, (up, down) in enumerate(pairs):
-        for ref, message in zip(out, to_send("gx", sizes[0], up, down)):
-            ref[v] = message
-
-
 def x_sweep(sizes, g_in, opened, ax, cx, *rest):
     n_in = min(sizes[0] - 1, 2)
-    fields, late, (out,) = rest[:n_in], rest[n_in : 2 * n_in], rest[2 * n_in :]
+    messages, (out,) = rest[:n_in], rest[n_in:]
     planes = ax.shape[0]
     like = ax[0]
-    (f0, h0), (f1, h1), (c_low, _) = (
-        received("gx", sizes[0], [m[v] for m in fields], like) for v in range(3)
-    )
-    (w_low, w_high), (back, forth) = (
-        received("gx", sizes[0], [m[v] for m in late], like) for v in range(2)
+    (w_low, w_high), (back, forth), (f0, h0), (f1, h1), (c_low, _) = (
+        received("gx", sizes[0], [m[v] for m in messages], like) for v in range(5)
     )
     g = [g_in[x] for x in range(planes)]
     w = [opened[x].astype(jnp.float32) * g[x] for x in range(planes)]
@@ -264,14 +305,15 @@
         out[x] = own[x] + (r[x] - r[x + 2])
 
 
-def call(body, out, *args, name):
-    shapes = [jax.ShapeDtypeStruct(shape, jnp.float32) for shape in out]
+def call(body, out, *args, name, source=pltpu.VMEM, scratch=(), limit=8):
+    shapes = [jax.ShapeDtypeStruct(o, jnp.float32) if isinstance(o, tuple) else o for o in out]
     return pl.pallas_call(
         body,
         out_shape=shapes,
-        in_specs=[pl.BlockSpec(memory_space=pltpu.VMEM)] * len(args),
+        in_specs=[pl.BlockSpec(memory_space=source)] * len(args),
         out_specs=[pl.BlockSpec(memory_space=pltpu.VMEM)] * len(shapes),
-        compiler_params=pltpu.CompilerParams(vmem_limit_bytes=8 * 2**20),
+        scratch_shapes=scratch,
+        compiler_params=pltpu.CompilerParams(vmem_limit_bytes=limit * 2**20),
         name=name,
     )(*args)
 
@@ -282,33 +324,31 @@
     planes, rows, lanes = block
     swap = lambda value, perm: lax.ppermute(value, AXES, perm)
     packed = (rows // fold(planes, rows, lanes), lanes)
-    z_out = call(
-        functools.partial(z_pack, sizes[2]),
-        [packed] * len(z_rounds),
-        cot, opened, az, cz,
-        name="z_pack",
+    cot, opened, az, cz, w, edges, *z_out = call(
+        functools.partial(z_pack, sizes[2], planes, rows, lanes),
+        [block, jax.ShapeDtypeStruct(block, jnp.int32), block, block, block, (3, *packed)]
+        + [packed] * len(z_rounds),
+        *(pltpu.with_memory_space_constraint(v, pltpu.HBM) for v in (cot, opened, az, cz)),
+        name="z_pack", source=pltpu.HBM, limit=8, scratch=[pltpu.SemaphoreType.DMA((4,))],
     )
     z_in = [swap(m, p) for m, p in zip(z_out, z_rounds)]
-    fields = call(
-        functools.partial(x_fields, sizes), [(3, rows, lanes)] * len(x_rounds), ax, cx, name="x_fields"
-    )
-    fields = [swap(m, p) for m, p in zip(fields, x_rounds)]
+    (partial,) = call(z_inner, [block], cot, w, az, cz, name="z_inner")
     g, *y_out = call(
         functools.partial(z_sweep, sizes),
         [block] + [(planes, 8, lanes)] * len(y_rounds),
-        cot, opened, az, cz, ay, cy, *z_in,
+        partial, edges, opened, ay, cy, *z_in,
         name="z_sweep",
     )
     y_in = [swap(m, p) for m, p in zip(y_out, y_rounds)]
     g, *x_out = call(
         functools.partial(y_sweep, sizes),
-        [block] + [(2, rows, lanes)] * len(x_rounds),
+        [block] + [(5, rows, lanes)] * len(x_rounds),
         g, opened, ay, cy, ax, cx, *y_in,
         name="y_sweep",
     )
     x_in = [swap(m, p) for m, p in zip(x_out, x_rounds)]
     (g,) = call(
-        functools.partial(x_sweep, sizes), [block], g, opened, ax, cx, *fields, *x_in, name="x_sweep"
+        functools.partial(x_sweep, sizes), [block], g, opened, ax, cx, *x_in, name="x_sweep"
     )
     return g
 

time: 23.1 us -> 18.6 us (0.81)
  local copies, waits for them, and re-layouts: 3.67 us -> 0.01 us
  starting transfers between devices: 7 us -> 6.02 us
  waiting for transfers between devices: 8.3 us -> 9.23 us
  Pallas kernels: 3.93 us -> 3.2 us
    unnamed x20 -> x8, local copies, waits for them, and re-layouts: 3.67 us -> 0.01 us
    ppermute x7 -> x5, starting transfers between devices: 7 us -> 6.02 us  [per_device(): swap = lambda value, perm: lax.ppermute(value, AXES, perm)]
    ppermute x7 -> x5, waiting for transfers between devices: 8.3 us -> 9.23 us  [per_device(): swap = lambda value, perm: lax.ppermute(value, AXES, perm)]
    pallas_call x5, Pallas kernels: 3.93 us -> 3.2 us  [call(): pl.pallas_call(body, out_shape=shapes, in_specs=[pl.BlockSpec(memory_spac...]
  transfers between devices with their start and end apart: 7 -> 5, of which waited for: 5 -> 4; matrix products, arithmetic and copies ran while one was open for 0% -> 0% of each run, Pallas kernels for 13% -> 2%
where the time goes in v2:
time: 18.6 us; the launch traced here: 18.5 us
  waiting for transfers between devices  9.23 us (50%)
  starting transfers between devices  6.02 us (32%)
  Pallas kernels  3.2 us (17%)
    ppermute x5, waiting for transfers between devices, per_device(): swap = lambda value, perm: lax.ppermute(value, AXES, perm)  9.23 us
    ppermute x5, starting transfers between devices, per_device(): swap = lambda value, perm: lax.ppermute(value, AXES, perm)  6.02 us
    pallas_call x5, Pallas kernels, call(): pl.pallas_call(body, out_shape=shapes, in_specs=[pl.BlockSpec(memory_spac...  3.2 us
  transfers between devices with their start and end apart: 5, of which 4 were waited for; matrix products, arithmetic and copies ran while one was open for 0% of the time, Pallas kernels for 2%

profile of v2, /device:TPU:21, one launch (start us, length us, event | category | flops | bytes accessed | tf_op | source)
XLA Modules:
  0.0 18.5 jit_solution(351186031673790751)
XLA Ops:
  0.0 1.4 %z_pack.1 = (f32[4,64,128]{2,1,0:T(8,128)S(1)}, s32[4,64,128]{2,1,0:T(8,128)S(1)}, f32[4,64,128]{2,1,0:T(8,128)S(1)}, f32[4,64,128]{2,1,0:T(8,128)S(1)}, f32[4,6...) custom-call(f32[4,64,128]{2,1,0:T(8,128)} %cot_in.1, ...), custom_call_target="tpu_custom_call" | custom-call | tf_op jit(solution)/shard_map/z_pack/pallas_call | solution.py:310
  1.4 1.4 %collective-permute-start = (f32[16,128]{1,0:T(8,128)S(1)}, f32[16,128]{1,0:T(8,128)S(1)}, u32[]{:S(2)}, u32[]{:S(2)}) collective-permute-start(f32[16,128]{1,0:T(8,128)S(1)} %get-tuple-element.24), channel_id=1, source_target_pairs={{0,1},{1,0},{2,3},{3,2},{4,5},{5,4},{6,7},{7,6},{8,9},{9,8},{10,11... | collective-permute-start | bytes 24584 | tf_op jit(solution)/shard_map/ppermute | solution.py:325
  2.7 0.0 collective-permute-start.1
  2.7 0.0 copy-start
  2.7 0.0 copy-start.1
  2.7 0.5 %z_inner.1.partial = f32[4,64,128]{2,1,0:T(8,128)S(1)} custom-call(f32[4,64,128]{2,1,0:T(8,128)S(1)} %get-tuple-element.18.g_ref, f32[4,64,128]{2,1,0:T(8,128)S(1)} %get-tuple-element.19.w_ref, f32[4,64,128]{2,1,0:T(8,128)S(1)} %get-tuple-element.20.a_ref, f32[4,64,128]{2,1,0:T(8,128)S(1)} %get-tuple-element.21.c_ref), custom_call_target="tpu_custom_call" | custom-call | tf_op jit(solution)/shard_map/z_inner/pallas_call | solution.py:310
  3.2 0.7 %collective-permute-done.rest_0_ = f32[16,128]{1,0:T(8,128)S(1)} collective-permute-done((f32[16,128]{1,0:T(8,128)S(1)}, f32[16,128]{1,0:T(8,128)S(1)}, u32[]{:S(2)}, u32[]{:S(2)}) %collective-permute-start) | collective-permute-done | bytes 8224 | tf_op jit(solution)/shard_map/ppermute | solution.py:325
  3.9 1.4 %collective-permute-done.1.rest_1_ = f32[16,128]{1,0:T(8,128)S(1)} collective-permute-done((f32[16,128]{1,0:T(8,128)S(1)}, f32[16,128]{1,0:T(8,128)S(1)}, u32[]{:S(2)}, u32[]{:S(2)}) %collective-permute-start.1) | collective-permute-done | bytes 8224 | tf_op jit(solution)/shard_map/ppermute | solution.py:325
  5.4 0.0 copy-done
  5.4 0.0 copy-done.1
  5.4 0.0 copy-start.2
  5.4 0.0 copy-start.3
  5.4 0.3 %z_sweep.1 = (f32[4,64,128]{2,1,0:T(8,128)S(1)}, f32[4,8,128]{2,1,0:T(8,128)S(1)}) custom-call(f32[4,64,128]{2,1,0:T(8,128)S(1)} %z_inner.1.partial, f32[3,16,128]{2,1,0:T(8,128)S(1)} %get-tuple-element.22.edges, s32[4,64,128]{2,1,0:T(8,128)S(1)} %get-tuple-element.23.opened, f32[4,64,128]{2,1,0:T(8,128)S(1)} %copy-done, f32[4,64,128]{2,1,0:T(8,128)S(1)} %copy-done.1, ...), custom_call_target="tpu_custom_call" | custom-call | tf_op jit(solution)/shard_map/z_sweep/pallas_call | solution.py:310
  5.7 0.3 %collective-permute-start.2 = (f32[4,8,128]{2,1,0:T(8,128)S(1)}, f32[4,8,128]{2,1,0:T(8,128)S(1)}, u32[]{:S(2)}, u32[]{:S(2)}) collective-permute-start(f32[4,8,128]{2,1,0:T(8,128)S(1)} %get-tuple-element.27), channel_id=1, source_target_pairs={{0,4},{1,5},{2,6},{3,7},{4,0},{5,1},{6,2},{7,3},{8,12},{9,13},{10,... | collective-permute-start | bytes 49160 | tf_op jit(solution)/shard_map/ppermute | solution.py:325
  6.0 2.4 %collective-permute-done.2.rest_0_ = f32[4,8,128]{2,1,0:T(8,128)S(1)} collective-permute-done((f32[4,8,128]{2,1,0:T(8,128)S(1)}, f32[4,8,128]{2,1,0:T(8,128)S(1)}, u32[]{:S(2)}, u32[]{:S(2)}) %collective-permute-start.2) | collective-permute-done | bytes 16416 | tf_op jit(solution)/shard_map/ppermute | solution.py:325
  8.3 0.0 copy-done.2
  8.3 0.0 copy-done.3
  8.3 0.3 %y_sweep.1 = (f32[4,64,128]{2,1,0:T(8,128)S(1)}, f32[5,64,128]{2,1,0:T(8,128)S(1)}, f32[5,64,128]{2,1,0:T(8,128)S(1)}) custom-call(f32[4,64,128]{2,1,0:T(8,128)S(1)} %get-tuple-element.26.g_in, s32[4,64,128]{2,1,0:T(8,128)S(1)} %get-tuple-element.23.opened, f32[4,64,128]{2,1,0:T(8,128)S(1)} %copy-done, f32[4,64,128]{2,1,0:T(8,128)S(1)} %copy-done.1, ...), custom_call_target="tpu_custom_call" | custom-call | tf_op jit(solution)/shard_map/y_sweep/pallas_call | solution.py:310
  8.6 3.2 %collective-permute-start.3 = (f32[5,64,128]{2,1,0:T(8,128)S(1)}, f32[5,64,128]{2,1,0:T(8,128)S(1)}, u32[]{:S(2)}, u32[]{:S(2)}) collective-permute-start(f32[5,64,128]{2,1,0:T(8,128)S(1)} %get-tuple-element.29), channel_id=1, source_target_pairs={{0,8},{1,9},{2,10},{3,11},{4,12},{5,13},{6,14},{7,15},{8,0},{9,1},... | collective-permute-start | bytes 491528 | tf_op jit(solution)/shard_map/ppermute | solution.py:325
  11.8 1.2 %collective-permute-start.4 = (f32[5,64,128]{2,1,0:T(8,128)S(1)}, f32[5,64,128]{2,1,0:T(8,128)S(1)}, u32[]{:S(2)}, u32[]{:S(2)}) collective-permute-start(f32[5,64,128]{2,1,0:T(8,128)S(1)} %get-tuple-element.30), channel_id=1, source_target_pairs={{0,24},{1,25},{2,26},{3,27},{4,28},{5,29},{6,30},{7,31},{8,16},{9,... | collective-permute-start | bytes 491528 | tf_op jit(solution)/shard_map/ppermute | solution.py:325
  12.9 0.0 collective-permute-done.3.rest_0_
  13.0 4.7 %collective-permute-done.4.rest_1_ = f32[5,64,128]{2,1,0:T(8,128)S(1)} collective-permute-done((f32[5,64,128]{2,1,0:T(8,128)S(1)}, f32[5,64,128]{2,1,0:T(8,128)S(1)}, u32[]{:S(2)}, u32[]{:S(2)}) %collective-permute-start.4) | collective-permute-done | bytes 163872 | tf_op jit(solution)/shard_map/ppermute | solution.py:325
  17.7 0.8 %x_sweep.1 = f32[4,64,128]{2,1,0:T(8,128)} custom-call(f32[4,64,128]{2,1,0:T(8,128)S(1)} %get-tuple-element.28.g_in, s32[4,64,128]{2,1,0:T(8,128)S(1)} %get-tuple-element.23.opened, f32[4,64,128]{2,1,0:T(8,128)S(1)} %copy-done.2, f32[4,64,128]{2,1,0:T(8,128)S(1)} %copy-done.3, f32[5,64,128]{2,1,0:T(8,128)S(1)} %collective-permute-done.3.rest_0_, ...), custom_call_target="tpu_custom_call" | custom-call | tf_op jit(solution)/shard_map/x_sweep/pallas_call | solution.py:310
Async XLA Ops:
  1.4 2.6 %collective-permute-start = (f32[16,128]{1,0:T(8,128)S(1)}, f32[16,128]{1,0:T(8,128)S(1)}, u32[]{:S(2)}, u32[]{:S(2)}) collective-permute-start(f32[16,128]{1,0:T(8,128)S(1)} %get-tuple-element.24), channel_id=1, source_target_pairs={{0,1},{1,0},{2,3},{3,2},{4,5},{5,4},{6,7},{7,6},{8,9},{9,8},{10,11... | collective-permute-start | bytes 24584 | tf_op jit(solution)/shard_map/ppermute | solution.py:325
  2.7 2.6 %collective-permute-start.1 = (f32[16,128]{1,0:T(8,128)S(1)}, f32[16,128]{1,0:T(8,128)S(1)}, u32[]{:S(2)}, u32[]{:S(2)}) collective-permute-start(f32[16,128]{1,0:T(8,128)S(1)} %get-tuple-element.25), channel_id=1, source_target_pairs={{0,8},{1,2},{2,1},{3,11},{4,12},{5,6},{6,5},{7,15},{8,0},{9,10},{1... | collective-permute-start | bytes 24584 | tf_op jit(solution)/shard_map/ppermute | solution.py:325
  2.7 2.6 %copy-start = (f32[4,64,128]{2,1,0:T(8,128)S(1)}, f32[4,64,128]{2,1,0:T(8,128)}, u32[]{:S(2)}) copy-start(f32[4,64,128]{2,1,0:T(8,128)} %ay.3) | copy-start | bytes 393220
  2.7 2.6 %copy-start.1 = (f32[4,64,128]{2,1,0:T(8,128)S(1)}, f32[4,64,128]{2,1,0:T(8,128)}, u32[]{:S(2)}) copy-start(f32[4,64,128]{2,1,0:T(8,128)} %cy.3) | copy-start | bytes 393220
  5.4 2.9 %copy-start.2 = (f32[4,64,128]{2,1,0:T(8,128)S(1)}, f32[4,64,128]{2,1,0:T(8,128)}, u32[]{:S(2)}) copy-start(f32[4,64,128]{2,1,0:T(8,128)} %ax.3) | copy-start | bytes 393220
  5.4 2.9 %copy-start.3 = (f32[4,64,128]{2,1,0:T(8,128)S(1)}, f32[4,64,128]{2,1,0:T(8,128)}, u32[]{:S(2)}) copy-start(f32[4,64,128]{2,1,0:T(8,128)} %cx.3) | copy-start | bytes 393220
  5.7 2.7 %collective-permute-start.2 = (f32[4,8,128]{2,1,0:T(8,128)S(1)}, f32[4,8,128]{2,1,0:T(8,128)S(1)}, u32[]{:S(2)}, u32[]{:S(2)}) collective-permute-start(f32[4,8,128]{2,1,0:T(8,128)S(1)} %get-tuple-element.27), channel_id=1, source_target_pairs={{0,4},{1,5},{2,6},{3,7},{4,0},{5,1},{6,2},{7,3},{8,12},{9,13},{10,... | collective-permute-start | bytes 49160 | tf_op jit(solution)/shard_map/ppermute | solution.py:325
  8.6 4.4 %collective-permute-start.3 = (f32[5,64,128]{2,1,0:T(8,128)S(1)}, f32[5,64,128]{2,1,0:T(8,128)S(1)}, u32[]{:S(2)}, u32[]{:S(2)}) collective-permute-start(f32[5,64,128]{2,1,0:T(8,128)S(1)} %get-tuple-element.29), channel_id=1, source_target_pairs={{0,8},{1,9},{2,10},{3,11},{4,12},{5,13},{6,14},{7,15},{8,0},{9,1},... | collective-permute-start | bytes 491528 | tf_op jit(solution)/shard_map/ppermute | solution.py:325
  11.8 5.9 %collective-permute-start.4 = (f32[5,64,128]{2,1,0:T(8,128)S(1)}, f32[5,64,128]{2,1,0:T(8,128)S(1)}, u32[]{:S(2)}, u32[]{:S(2)}) collective-permute-start(f32[5,64,128]{2,1,0:T(8,128)S(1)} %get-tuple-element.30), channel_id=1, source_target_pairs={{0,24},{1,25},{2,26},{3,27},{4,28},{5,29},{6,30},{7,31},{8,16},{9,... | collective-permute-start | bytes 491528 | tf_op jit(solution)/shard_map/ppermute | solution.py:325

commit v3 on v2

v3 whole, which is shorter than its diff:
```python
import functools

import jax
import jax.numpy as jnp
from jax import lax
from jax.experimental import pallas as pl
from jax.experimental.pallas import tpu as pltpu
from jax.sharding import PartitionSpec as P

sharpness = 3.5
slot = 8
AXES = ("gx", "gy", "gz")


def pair_rounds(sizes, along):
    size = sizes[along]
    if size == 1:
        return []
    assert size % 2 == 0

    def perm(partner):
        pairs = []
        for i in range(sizes[0]):
            for j in range(sizes[1]):
                for k in range(sizes[2]):
                    a, b, c = partner(i, j, k)
                    pairs.append(
                        ((i * sizes[1] + j) * sizes[2] + k, (a * sizes[1] + b) * sizes[2] + c)
                    )
        return pairs

    def even(*at):
        at = list(at)
        at[along] ^= 1
        return at

    def odd(*at):
        at = list(at)
        if 0 < at[along] < size - 1:
            at[along] = (at[along] - 1) ^ 1
            at[along] += 1
        elif along != 0 and sizes[0] % 2 == 0:
            at[0] ^= 1
        elif along == 0 and sizes[1] % 2 == 0:
            at[1] ^= 1
        else:
            at[along] = size - 1 - at[along]
        return at

    return [perm(even)] if size == 2 else [perm(even), perm(odd)]


def roles(axis, size):
    at = lax.axis_index(axis)
    return lax.rem(at, 2) == 0, at > 0, at < size - 1


def to_send(axis, size, up, down):
    if size == 1:
        return []
    even, _, _ = roles(axis, size)
    first = jnp.where(even, up, down)
    return [first] if size == 2 else [first, jnp.where(even, down, up)]


def received(axis, size, messages, like):
    if size == 1:
        return jnp.zeros_like(like), jnp.zeros_like(like)
    even, has_low, has_high = roles(axis, size)
    first, second = messages[0], messages[-1]
    low = jnp.where(even, second, first)
    high = jnp.where(even, first, second)
    return jnp.where(has_low, low, 0.0), jnp.where(has_high, high, 0.0)


def bend(a, difference):
    t = jnp.tanh(sharpness * difference)
    return t, 0.5 * sharpness * a * (1.0 - a) * (1.0 - t * t)


def low_end(low, w0, w1, a0, a1, c0):
    w_far, w_low, a_far, a_low, c_far, c_low = low
    _, bent = bend(a_low, a0 - a_far)
    across = w0 - w_low
    r_low = (across * jnp.maximum(c_low, 0.0) - (w_low - w_far) * jnp.minimum(c_far, 0.0)) * bent
    forth = (w1 - w0) * jnp.maximum(c0, 0.0)
    back = across * jnp.minimum(c_low, 0.0)
    t, bent = bend(a0, a1 - a_low)
    first = w0 * (c0 - c_low) + (forth + back) + (forth - back) * ((0.5 - a0) * t) + r_low
    return first, (forth - back) * bent


def high_end(high, w0, w1, a0, a1, c0, c1):
    w_high, w_far, a_high, a_far, c_high = high
    _, bent = bend(a_high, a_far - a1)
    across = w_high - w1
    r_high = ((w_far - w_high) * jnp.maximum(c_high, 0.0) - across * jnp.minimum(c1, 0.0)) * bent
    forth = across * jnp.maximum(c1, 0.0)
    back = (w1 - w0) * jnp.minimum(c0, 0.0)
    t, bent = bend(a1, a_high - a0)
    last = w1 * (c1 - c0) + (forth + back) + (forth - back) * ((0.5 - a1) * t) - r_high
    return last, (back - forth) * bent


def interior(g, w, a, c, dim):
    length = a.shape[dim]
    at = lax.broadcasted_iota(jnp.int32, a.shape, dim)
    inside = (at > 0) & (at < length - 1)
    prev = lambda value: pltpu.roll(value, 1, dim)
    after = lambda value: pltpu.roll(value, length - 1, dim)
    t, bent = bend(a, after(a) - prev(a))
    below = prev(c)
    forth = (after(w) - w) * jnp.maximum(c, 0.0)
    back = (w - prev(w)) * jnp.minimum(below, 0.0)
    apart = jnp.where(inside, forth - back, 0.0)
    own = jnp.where(inside, w * (c - below) + (forth + back), 0.0) + apart * ((0.5 - a) * t)
    r = apart * bent
    return g + own + (prev(r) - after(r))


def fold(planes, rows, lanes):
    per = lanes // (slot * planes)
    return per if per >= 1 and rows % (8 * per) == 0 else 1


def edge_lanes(shape, lanes):
    at = lax.broadcasted_iota(jnp.int32, shape, 1)
    return at, lax.rem(at, slot)


def z_pack(size, planes, rows, lanes, cot_in, opened_in, a_in, c_in, *out):
    cot, opened, a_ref, c_ref, w_ref, edge_ref, *out, sems = out
    copies = [
        pltpu.make_async_copy(src, dst, sems.at[n])
        for n, (src, dst) in enumerate(
            ((cot_in, cot), (opened_in, opened), (a_in, a_ref), (c_in, c_ref))
        )
    ]
    for copy in copies:
        copy.start()
    for copy in copies:
        copy.wait()
    per = fold(planes, rows, lanes)
    step = rows // per
    at, place = edge_lanes((rows, lanes), lanes)
    near = (at < 2) | (at >= lanes - 2)
    totals = [None] * 3
    for x in range(planes):
        w = cot[x] * opened[x].astype(jnp.float32)
        w_ref[x] = w
        for n, field in enumerate((w, a_ref[x], c_ref[x])):
            field = jnp.where(near, field, 0.0)
            for r in range(per):
                move = slot * (x + planes * r)
                part = field[r * step : (r + 1) * step]
                part = pltpu.roll(part, move, 1) if move else part
                totals[n] = part if totals[n] is None else totals[n] + part
    for n in range(3):
        edge_ref[n] = totals[n]
    _, place = edge_lanes((step, lanes), lanes)
    ends = [jnp.where(place >= slot - 2, total, 0.0) for total in totals]
    starts = [jnp.where(place < 2, total, 0.0) for total in totals]
    up = sum(pltpu.roll(end, 2 + 2 * n, 1) for n, end in enumerate(ends))
    down = sum(pltpu.roll(start, 2 * n, 1) if n else start for n, start in enumerate(starts))
    for ref, message in zip(out, to_send("gz", size, up, down)):
        ref[...] = message


def z_inner(g_ref, w_ref, a_ref, c_ref, *rest):
    *sources, out = rest[: len(rest) // 2]
    *targets, sems = rest[len(rest) // 2 :]
    copies = [
        pltpu.make_async_copy(src, dst, sems.at[n]) for n, (src, dst) in enumerate(zip(sources, targets))
    ]
    for copy in copies:
        copy.start()
    for x in range(a_ref.shape[0]):
        out[x] = interior(g_ref[x], w_ref[x], a_ref[x], c_ref[x], 1)
    for copy in copies:
        copy.wait()


def z_ends(edges, low, high, lanes):
    shift = lambda value, by: pltpu.roll(value, by % lanes, 1)
    w, a, c = edges
    _, place = edge_lanes(w.shape, lanes)
    low = [shift(low, -v) if v else low for v in range(6)]
    first, second = low_end(low, w, shift(w, -1), a, shift(a, -1), c)
    high = [shift(high, -v) if v else high for v in range(5)]
    last, before = high_end(
        high, shift(w, 2), shift(w, 1), shift(a, 2), shift(a, 1), shift(c, 2), shift(c, 1)
    )
    ends = jnp.where(place == 0, first, jnp.where(place == 1, shift(second, 1), 0.0))
    return jnp.where(
        place == slot - 1, shift(last, -1), jnp.where(place == slot - 2, shift(before, -2), ends)
    )


def z_sweep(sizes, partial, edges, opened, ay, cy, *rest):
    n_in = min(sizes[2] - 1, 2)
    messages, (g_ref, *out) = [m[...] for m in rest[:n_in]], rest[n_in:]
    planes, rows, lanes = ay.shape
    low, high = received("gz", sizes[2], messages, edges[0])
    ends = z_ends([edges[n] for n in range(3)], low, high, lanes)
    at = lax.broadcasted_iota(jnp.int32, (rows, lanes), 1)
    near = (at < 2) | (at >= lanes - 2)
    per = fold(planes, rows, lanes)
    tile = lax.broadcasted_iota(jnp.int32, (8, lanes), 0)
    for x in range(planes):
        parts = []
        for r in range(per):
            move = slot * (x + planes * r)
            parts.append(pltpu.roll(ends, lanes - move, 1) if move else ends)
        g = partial[x] + jnp.where(near, jnp.concatenate(parts, axis=0), 0.0)
        g_ref[x] = g
        if not out:
            continue
        mask = opened[x].astype(jnp.float32)
        w = mask * g
        pick = lambda *tiles: jnp.where(tile < 2, tiles[0], jnp.where(tile < 4, tiles[1], tiles[2]))
        up = pick(
            *(
                pltpu.roll(field[rows - 8 :], by, 0)
                for field, by in ((w, 2), (ay[x], 4), (cy[x], 6))
            )
        )
        down = pick(w[:8], pltpu.roll(ay[x, :8], 2, 0), pltpu.roll(cy[x, :8], 4, 0))
        for ref, message in zip(out, to_send("gy", sizes[1], up, down)):
            ref[x] = message


def x_messages(w, ax, cx):
    planes = len(w)
    back = (w[-1] - w[-2]) * jnp.minimum(cx[planes - 2], 0.0)
    forth = (w[1] - w[0]) * jnp.maximum(cx[0], 0.0)
    return (w[-1], w[0]), (back, forth)


def y_inner(sizes, g_in, opened, ay, cy, ax, cx, partial, *out):
    planes = ay.shape[0]
    w = []
    for x in range(planes):
        mask = opened[x].astype(jnp.float32)
        g = interior(g_in[x], mask * g_in[x], ay[x], cy[x], 0)
        partial[x] = g
        w.append(mask * g)
    pairs = (
        *x_messages(w, ax, cx),
        (ax[planes - 2], ax[0]),
        (ax[planes - 1], ax[1]),
        (cx[planes - 1], cx[0]),
    )
    for v, (up, down) in enumerate(pairs):
        for ref, message in zip(out, to_send("gx", sizes[0], up, down)):
            ref[v] = message


def y_sweep(sizes, partial, g_in, opened, ay, cy, cx, *rest):
    n_in = min(sizes[1] - 1, 2)
    messages, (g_ref, *out) = rest[:n_in], rest[n_in:]
    planes, rows, lanes = ay.shape
    tile = lax.broadcasted_iota(jnp.int32, (8, lanes), 0)
    ws = []
    for x in range(planes):
        low, high = received("gy", sizes[1], [m[x] for m in messages], ay[x, :8])
        row = lambda ref, n: ref[x, n : n + 1]
        w = [opened[x, n : n + 1].astype(jnp.float32) * row(g_in, n) for n in (0, 1, rows - 2, rows - 1)]
        first, second = low_end(
            [low[v : v + 1] for v in range(6)], w[0], w[1], row(ay, 0), row(ay, 1), row(cy, 0)
        )
        last, before = high_end(
            [high[v : v + 1] for v in range(5)],
            w[2],
            w[3],
            *(row(ref, n) for ref in (ay, cy) for n in (rows - 2, rows - 1)),
        )
        top = partial[x, :8] + jnp.where(tile == 0, first, jnp.where(tile == 1, second, 0.0))
        bottom = partial[x, rows - 8 :] + jnp.where(
            tile == 7, last, jnp.where(tile == 6, before, 0.0)
        )
        g_ref[x, :8] = top
        g_ref[x, 8 : rows - 8] = partial[x, 8 : rows - 8]
        g_ref[x, rows - 8 :] = bottom
        mask = jnp.where(tile < 4, opened[x, :8], opened[x, rows - 8 :]).astype(jnp.float32)
        ws.append(mask * jnp.where(tile < 4, top, bottom))
    if out:
        c = [jnp.where(tile < 4, cx[x, :8], cx[x, rows - 8 :]) for x in range(planes)]
        for v, (up, down) in enumerate(x_messages(ws, None, c)):
            for ref, message in zip(out, to_send("gx", sizes[0], up, down)):
                ref[v] = message


def x_sweep(sizes, g_in, opened, ax, cx, *rest):
    n_in = min(sizes[0] - 1, 2)
    early, late, (out,) = rest[:n_in], rest[n_in : 2 * n_in], rest[2 * n_in :]
    planes, rows, lanes = ax.shape
    like = ax[0]
    tile = lax.broadcasted_iota(jnp.int32, (8, lanes), 0)

    def whole(n, v):
        if v > 1:
            return early[n][v]
        ends = late[n][v]
        top = jnp.where(tile < 2, ends, early[n][v, :8])
        bottom = jnp.where(tile >= 6, ends, early[n][v, rows - 8 :])
        return jnp.concatenate([top, early[n][v, 8 : rows - 8], bottom], axis=0)

    (w_low, w_high), (b_low, f_high), (f0, h0), (f1, h1), (c_low, _) = (
        received("gx", sizes[0], [whole(n, v) for n in range(n_in)], like) for v in range(5)
    )
    g = [g_in[x] for x in range(planes)]
    w = [opened[x].astype(jnp.float32) * g[x] for x in range(planes)]
    a = [f1] + [ax[x] for x in range(planes)] + [h0]
    c = [c_low] + [cx[x] for x in range(planes)]
    last = planes - 1
    _, bent = bend(f1, a[1] - f0)
    r = [((w[0] - w_low) * jnp.maximum(c_low, 0.0) - b_low) * bent]
    own = []
    for x in range(planes):
        t, bent = bend(a[x + 1], a[x + 2] - a[x])
        forth = ((w[x + 1] if x < last else w_high) - w[x]) * jnp.maximum(c[x + 1], 0.0)
        back = (w[x] - (w[x - 1] if x else w_low)) * jnp.minimum(c[x], 0.0)
        apart = forth - back
        r.append(apart * bent)
        own.append(
            g[x] + w[x] * (c[x + 1] - c[x]) + (forth + back) + apart * ((0.5 - a[x + 1]) * t)
        )
    _, bent = bend(h0, h1 - a[planes])
    r.append((f_high - (w_high - w[last]) * jnp.minimum(c[planes], 0.0)) * bent)
    for x in range(planes):
        out[x] = own[x] + (r[x] - r[x + 2])


def call(body, out, *args, name, loads=(), scratch=(), us=0.3, flops=0):
    shapes = [jax.ShapeDtypeStruct(o, jnp.float32) if isinstance(o, tuple) else o for o in out]
    loads = [pltpu.with_memory_space_constraint(v, pltpu.HBM) for v in loads]
    return pl.pallas_call(
        body,
        out_shape=shapes,
        in_specs=[pl.BlockSpec(memory_space=pltpu.VMEM)] * len(args)
        + [pl.BlockSpec(memory_space=pltpu.HBM)] * len(loads),
        out_specs=[pl.BlockSpec(memory_space=pltpu.VMEM)] * len(shapes),
        scratch_shapes=scratch,
        compiler_params=pltpu.CompilerParams(vmem_limit_bytes=8 * 2**20),
        cost_estimate=pl.CostEstimate(
            flops=flops, bytes_accessed=int(us * 3_690_000), transcendentals=0
        ),
        name=name,
    )(*args, *loads)


def per_device(sizes, cot, ax, ay, az, cx, cy, cz, opened):
    x_rounds, y_rounds, z_rounds = (pair_rounds(sizes, d) for d in range(3))
    block = az.shape
    planes, rows, lanes = block
    swap = lambda value, perm: lax.ppermute(value, AXES, perm)
    packed = (rows // fold(planes, rows, lanes), lanes)
    cot, opened, az, cz, w, edges, *z_out = call(
        functools.partial(z_pack, sizes[2], planes, rows, lanes),
        [block, jax.ShapeDtypeStruct(block, jnp.int32), block, block, block, (3, *packed)]
        + [packed] * len(z_rounds),
        loads=(cot, opened, az, cz),
        name="z_pack", scratch=[pltpu.SemaphoreType.DMA((4,))],
    )
    z_in = [swap(m, p) for m, p in zip(z_out, z_rounds)]
    partial, ax, ay, cx, cy = call(
        z_inner,
        [block] * 5,
        cot, w, az, cz,
        loads=(ax, ay, cx, cy),
        name="z_inner", scratch=[pltpu.SemaphoreType.DMA((4,))],
    )
    g, *y_out = call(
        functools.partial(z_sweep, sizes),
        [block] + [(planes, 8, lanes)] * len(y_rounds),
        partial, edges, opened, ay, cy, *z_in,
        name="z_sweep",
    )
    y_in = [swap(m, p) for m, p in zip(y_out, y_rounds)]
    partial, *x_out = call(
        functools.partial(y_inner, sizes),
        [block] + [(5, rows, lanes)] * len(x_rounds),
        g, opened, ay, cy, ax, cx,
        name="y_inner",
    )
    x_early = [swap(m, p) for m, p in zip(x_out, x_rounds)]
    g, *x_out = call(
        functools.partial(y_sweep, sizes),
        [block] + [(2, 8, lanes)] * len(x_rounds),
        partial, g, opened, ay, cy, cx, *y_in,
        name="y_sweep", flops=10000000000,
    )
    x_late = [swap(m, p) for m, p in zip(x_out, x_rounds)]
    (g,) = call(
        functools.partial(x_sweep, sizes), [block], g, opened, ax, cx, *x_early, *x_late, name="x_sweep"
    )
    return g


def solution(mesh):
    sizes = tuple(mesh.shape[axis] for axis in AXES)
    placed = P(*AXES)
    return jax.shard_map(
        functools.partial(per_device, sizes),
        mesh=mesh,
        in_specs=(placed,) * 8,
        out_specs=placed,
        check_vma=False,
    )
```

time: 18.6 us -> 15.9 us (0.85)
  waiting for transfers between devices: 9.23 us -> 3.66 us
  starting transfers between devices: 6.02 us -> 8.14 us
  Pallas kernels: 3.2 us -> 3.93 us
    ppermute x5 -> x7, waiting for transfers between devices: 9.23 us -> 3.66 us  [per_device(): swap = lambda value, perm: lax.ppermute(value, AXES, perm)]
    ppermute x5 -> x7, starting transfers between devices: 6.02 us -> 8.14 us  [per_device(): swap = lambda value, perm: lax.ppermute(value, AXES, perm)]
    pallas_call x5 -> x6, Pallas kernels: 3.2 us -> 3.93 us  [call(): pl.pallas_call(body, out_shape=shapes, in_specs=[pl.BlockSpec(memory_spac...]
  transfers between devices with their start and end apart: 5 -> 7, of which waited for: 4 -> 3; matrix products, arithmetic and copies ran while one was open for 0% -> 0% of each run, Pallas kernels for 2% -> 9%
where the time goes in v3:
time: 15.9 us; the launch traced here: 15.8 us
  starting transfers between devices  8.14 us (51%)
  Pallas kernels  3.93 us (25%)
  waiting for transfers between devices  3.66 us (23%)
    ppermute x7, starting transfers between devices, per_device(): swap = lambda value, perm: lax.ppermute(value, AXES, perm)  8.14 us
    pallas_call x6, Pallas kernels, call(): pl.pallas_call(body, out_shape=shapes, in_specs=[pl.BlockSpec(memory_spac...  3.93 us
    ppermute x7, waiting for transfers between devices, per_device(): swap = lambda value, perm: lax.ppermute(value, AXES, perm)  3.66 us
  transfers between devices with their start and end apart: 7, of which 3 were waited for; matrix products, arithmetic and copies ran while one was open for 0% of the time, Pallas kernels for 9%

profile of v3, /device:TPU:21, one launch (start us, length us, event | category | flops | bytes accessed | tf_op | source)
XLA Modules:
  0.0 15.8 jit_solution(17453415339065936422)
XLA Ops:
  0.0 1.4 %z_pack.1 = (f32[4,64,128]{2,1,0:T(8,128)S(1)}, s32[4,64,128]{2,1,0:T(8,128)S(1)}, f32[4,64,128]{2,1,0:T(8,128)S(1)}, f32[4,64,128]{2,1,0:T(8,128)S(1)}, f32[4,6...) custom-call(f32[4,64,128]{2,1,0:T(8,128)} %cot_in.1, ...), custom_call_target="tpu_custom_call" | custom-call | bytes 1107000 | tf_op jit(solution)/shard_map/z_pack/pallas_call | solution.py:337
  1.4 1.4 %collective-permute-start = (f32[16,128]{1,0:T(8,128)S(1)}, f32[16,128]{1,0:T(8,128)S(1)}, u32[]{:S(2)}, u32[]{:S(2)}) collective-permute-start(f32[16,128]{1,0:T(8,128)S(1)} %get-tuple-element.35), channel_id=1, source_target_pairs={{0,1},{1,0},{2,3},{3,2},{4,5},{5,4},{6,7},{7,6},{8,9},{9,8},{10,11... | collective-permute-start | bytes 24584 | tf_op jit(solution)/shard_map/ppermute | solution.py:356
  2.7 0.0 collective-permute-start.1
  2.7 1.1 %z_inner.1 = (f32[4,64,128]{2,1,0:T(8,128)S(1)}, f32[4,64,128]{2,1,0:T(8,128)S(1)}, f32[4,64,128]{2,1,0:T(8,128)S(1)}, f32[4,64,128]{2,1,0:T(8,128)S(1)}, f32[4,64,128]{2,1,0:T(8,128)S(1)}) custom-call(f32[4,64,128]{2,1,0:T(8,128)S(1)} %get-tuple-element.26.g_ref, f32[4,64,128]{2,1,0:T(8,128)S(1)} %get-tuple-element.27.w_ref, ...), custom_call_target="tpu_custom_call" | custom-call | bytes 1107000 | tf_op jit(solution)/shard_map/z_inner/pallas_call | solution.py:337
  3.9 0.1 collective-permute-done.rest_0_
  3.9 1.4 %collective-permute-done.1.rest_1_ = f32[16,128]{1,0:T(8,128)S(1)} collective-permute-done((f32[16,128]{1,0:T(8,128)S(1)}, f32[16,128]{1,0:T(8,128)S(1)}, u32[]{:S(2)}, u32[]{:S(2)}) %collective-permute-start.1) | collective-permute-done | bytes 8224 | tf_op jit(solution)/shard_map/ppermute | solution.py:356
  5.4 0.3 %z_sweep.1 = (f32[4,64,128]{2,1,0:T(8,128)S(1)}, f32[4,8,128]{2,1,0:T(8,128)S(1)}) custom-call(f32[4,64,128]{2,1,0:T(8,128)S(1)} %get-tuple-element.30.partial, f32[3,16,128]{2,1,0:T(8,128)S(1)} %get-tuple-element.31.edges, s32[4,64,128]{2,1,0:T(8,128)S(1)} %get-tuple-element.32.opened, f32[4,64,128]{2,1,0:T(8,128)S(1)} %get-tuple-element.33.ay, ...), custom_call_target="tpu_custom_call" | custom-call | bytes 1107000 | tf_op jit(solution)/shard_map/z_sweep/pallas_call | solution.py:337
  5.6 0.3 %collective-permute-start.2 = (f32[4,8,128]{2,1,0:T(8,128)S(1)}, f32[4,8,128]{2,1,0:T(8,128)S(1)}, u32[]{:S(2)}, u32[]{:S(2)}) collective-permute-start(f32[4,8,128]{2,1,0:T(8,128)S(1)} %get-tuple-element.41), channel_id=1, source_target_pairs={{0,4},{1,5},{2,6},{3,7},{4,0},{5,1},{6,2},{7,3},{8,12},{9,13},{10,... | collective-permute-start | bytes 49160 | tf_op jit(solution)/shard_map/ppermute | solution.py:356
  5.9 0.2 %y_inner.1 = (f32[4,64,128]{2,1,0:T(8,128)S(1)}, f32[5,64,128]{2,1,0:T(8,128)S(1)}, f32[5,64,128]{2,1,0:T(8,128)S(1)}) custom-call(f32[4,64,128]{2,1,0:T(8,128)S(1)} %get-tuple-element.37.g_in, s32[4,64,128]{2,1,0:T(8,128)S(1)} %get-tuple-element.32.opened, f32[4,64,128]{2,1,0:T(8,128)S(1)} %get-tuple-element.33.ay, f32[4,64,128]{2,1,0:T(8,128)S(1)} %get-tuple-element.34.cy, ...), custom_call_target="tpu_custom_call" | custom-call | bytes 1107000 | tf_op jit(solution)/shard_map/y_inner/pallas_call | solution.py:337
  6.2 2.3 %collective-permute-start.3 = (f32[5,64,128]{2,1,0:T(8,128)S(1)}, f32[5,64,128]{2,1,0:T(8,128)S(1)}, u32[]{:S(2)}, u32[]{:S(2)}) collective-permute-start(f32[5,64,128]{2,1,0:T(8,128)S(1)} %get-tuple-element.43), channel_id=1, source_target_pairs={{0,8},{1,9},{2,10},{3,11},{4,12},{5,13},{6,14},{7,15},{8,0},{9,1},... | collective-permute-start | bytes 491528 | tf_op jit(solution)/shard_map/ppermute | solution.py:356
  8.5 1.2 %collective-permute-start.4 = (f32[5,64,128]{2,1,0:T(8,128)S(1)}, f32[5,64,128]{2,1,0:T(8,128)S(1)}, u32[]{:S(2)}, u32[]{:S(2)}) collective-permute-start(f32[5,64,128]{2,1,0:T(8,128)S(1)} %get-tuple-element.44), channel_id=1, source_target_pairs={{0,4},{1,5},{2,6},{3,7},{4,0},{5,1},{6,2},{7,3},{8,16},{9,17},{10,... | collective-permute-start | bytes 491528 | tf_op jit(solution)/shard_map/ppermute | solution.py:356
  9.7 0.0 collective-permute-done.2.rest_0_
  9.7 0.1 y_sweep.1
  9.8 1.8 %collective-permute-start.5 = (f32[2,8,128]{2,1,0:T(8,128)S(1)}, f32[2,8,128]{2,1,0:T(8,128)S(1)}, u32[]{:S(2)}, u32[]{:S(2)}) collective-permute-start(f32[2,8,128]{2,1,0:T(8,128)S(1)} %get-tuple-element.45), channel_id=1, source_target_pairs={{0,8},{1,9},{2,10},{3,11},{4,12},{5,13},{6,14},{7,15},{8,0},{9,1},... | collective-permute-start | bytes 24584 | tf_op jit(solution)/shard_map/ppermute | solution.py:356
  11.6 1.2 %collective-permute-start.6 = (f32[2,8,128]{2,1,0:T(8,128)S(1)}, f32[2,8,128]{2,1,0:T(8,128)S(1)}, u32[]{:S(2)}, u32[]{:S(2)}) collective-permute-start(f32[2,8,128]{2,1,0:T(8,128)S(1)} %get-tuple-element.46), channel_id=1, source_target_pairs={{0,4},{1,5},{2,6},{3,7},{4,0},{5,1},{6,2},{7,3},{8,16},{9,17},{10,... | collective-permute-start | bytes 24584 | tf_op jit(solution)/shard_map/ppermute | solution.py:356
  12.8 0.0 collective-permute-done.5.rest_2_
  12.8 2.2 %collective-permute-done.6.rest_3_ = f32[2,8,128]{2,1,0:T(8,128)S(1)} collective-permute-done((f32[2,8,128]{2,1,0:T(8,128)S(1)}, f32[2,8,128]{2,1,0:T(8,128)S(1)}, u32[]{:S(2)}, u32[]{:S(2)}) %collective-permute-start.6) | collective-permute-done | bytes 8224 | tf_op jit(solution)/shard_map/ppermute | solution.py:356
  14.9 0.0 collective-permute-done.3.rest_0_
  14.9 0.0 collective-permute-done.4.rest_1_
  14.9 0.8 %x_sweep.1 = f32[4,64,128]{2,1,0:T(8,128)} custom-call(f32[4,64,128]{2,1,0:T(8,128)S(1)} %get-tuple-element.42.g_in, s32[4,64,128]{2,1,0:T(8,128)S(1)} %get-tuple-element.32.opened, f32[4,64,128]{2,1,0:T(8,128)S(1)} %get-tuple-element.38.ax, f32[4,64,128]{2,1,0:T(8,128)S(1)} %get-tuple-element.39.cx, f32[5,64,128]{2,1,0:T(8,128)S(1)} %collective-permute-done.3.rest_0_, ...), custom_call_target="tpu_custom_call" | custom-call | bytes 1107000 | tf_op jit(solution)/shard_map/x_sweep/pallas_call | solution.py:337
Async XLA Ops:
  1.4 2.6 %collective-permute-start = (f32[16,128]{1,0:T(8,128)S(1)}, f32[16,128]{1,0:T(8,128)S(1)}, u32[]{:S(2)}, u32[]{:S(2)}) collective-permute-start(f32[16,128]{1,0:T(8,128)S(1)} %get-tuple-element.35), channel_id=1, source_target_pairs={{0,1},{1,0},{2,3},{3,2},{4,5},{5,4},{6,7},{7,6},{8,9},{9,8},{10,11... | collective-permute-start | bytes 24584 | tf_op jit(solution)/shard_map/ppermute | solution.py:356
  2.7 2.6 %collective-permute-start.1 = (f32[16,128]{1,0:T(8,128)S(1)}, f32[16,128]{1,0:T(8,128)S(1)}, u32[]{:S(2)}, u32[]{:S(2)}) collective-permute-start(f32[16,128]{1,0:T(8,128)S(1)} %get-tuple-element.36), channel_id=1, source_target_pairs={{0,8},{1,2},{2,1},{3,11},{4,12},{5,6},{6,5},{7,15},{8,0},{9,10},{1... | collective-permute-start | bytes 24584 | tf_op jit(solution)/shard_map/ppermute | solution.py:356
  5.6 4.0 %collective-permute-start.2 = (f32[4,8,128]{2,1,0:T(8,128)S(1)}, f32[4,8,128]{2,1,0:T(8,128)S(1)}, u32[]{:S(2)}, u32[]{:S(2)}) collective-permute-start(f32[4,8,128]{2,1,0:T(8,128)S(1)} %get-tuple-element.41), channel_id=1, source_target_pairs={{0,4},{1,5},{2,6},{3,7},{4,0},{5,1},{6,2},{7,3},{8,12},{9,13},{10,... | collective-permute-start | bytes 49160 | tf_op jit(solution)/shard_map/ppermute | solution.py:356
  6.2 8.7 %collective-permute-start.3 = (f32[5,64,128]{2,1,0:T(8,128)S(1)}, f32[5,64,128]{2,1,0:T(8,128)S(1)}, u32[]{:S(2)}, u32[]{:S(2)}) collective-permute-start(f32[5,64,128]{2,1,0:T(8,128)S(1)} %get-tuple-element.43), channel_id=1, source_target_pairs={{0,8},{1,9},{2,10},{3,11},{4,12},{5,13},{6,14},{7,15},{8,0},{9,1},... | collective-permute-start | bytes 491528 | tf_op jit(solution)/shard_map/ppermute | solution.py:356
  8.5 6.4 %collective-permute-start.4 = (f32[5,64,128]{2,1,0:T(8,128)S(1)}, f32[5,64,128]{2,1,0:T(8,128)S(1)}, u32[]{:S(2)}, u32[]{:S(2)}) collective-permute-start(f32[5,64,128]{2,1,0:T(8,128)S(1)} %get-tuple-element.44), channel_id=1, source_target_pairs={{0,4},{1,5},{2,6},{3,7},{4,0},{5,1},{6,2},{7,3},{8,16},{9,17},{10,... | collective-permute-start | bytes 491528 | tf_op jit(solution)/shard_map/ppermute | solution.py:356
  9.8 3.0 %collective-permute-start.5 = (f32[2,8,128]{2,1,0:T(8,128)S(1)}, f32[2,8,128]{2,1,0:T(8,128)S(1)}, u32[]{:S(2)}, u32[]{:S(2)}) collective-permute-start(f32[2,8,128]{2,1,0:T(8,128)S(1)} %get-tuple-element.45), channel_id=1, source_target_pairs={{0,8},{1,9},{2,10},{3,11},{4,12},{5,13},{6,14},{7,15},{8,0},{9,1},... | collective-permute-start | bytes 24584 | tf_op jit(solution)/shard_map/ppermute | solution.py:356
  11.6 3.3 %collective-permute-start.6 = (f32[2,8,128]{2,1,0:T(8,128)S(1)}, f32[2,8,128]{2,1,0:T(8,128)S(1)}, u32[]{:S(2)}, u32[]{:S(2)}) collective-permute-start(f32[2,8,128]{2,1,0:T(8,128)S(1)} %get-tuple-element.46), channel_id=1, source_target_pairs={{0,4},{1,5},{2,6},{3,7},{4,0},{5,1},{6,2},{7,3},{8,16},{9,17},{10,... | collective-permute-start | bytes 24584 | tf_op jit(solution)/shard_map/ppermute | solution.py:356

commit v4 on v3

v4 whole, which is shorter than its diff:
```python
import functools
import itertools

import jax
import jax.numpy as jnp
from jax import lax
from jax.experimental import pallas as pl
from jax.experimental.pallas import tpu as pltpu
from jax.sharding import PartitionSpec as P

sharpness = 3.5
slot = 8
AXES = ("gx", "gy", "gz")


def colours(sizes, along):
    return min(sizes[along] - 1, 3 if along == 2 else 2)


def turn_of(face, along, n):
    return (face + (1 if along == 0 else 0)) % n


def pair_rounds(sizes, along, aside=0):
    n = colours(sizes, along)

    def partner(at, turn):
        at = list(at)
        i = at[along]
        if turn_of(i, along, n) == turn and i + 1 < sizes[along]:
            at[along] += 1
        elif i > 0 and turn_of(i - 1, along, n) == turn:
            at[along] -= 1
        elif aside == along:
            at[along] = sizes[along] - 1 - i
        elif sizes[aside] % 2 == 0:
            at[aside] ^= 1
        return at

    places = list(itertools.product(*(range(size) for size in sizes)))
    flat = lambda at: (at[0] * sizes[1] + at[1]) * sizes[2] + at[2]
    return [[(flat(at), flat(partner(at, turn))) for at in places] for turn in range(n)]


def to_send(sizes, along, up, down):
    n, at = colours(sizes, along), lax.axis_index(AXES[along])
    if n <= 1:
        return [jnp.where(at == 0, up, down)] * n
    mine = turn_of(at, along, n)
    return [jnp.where((mine == turn) & (at < sizes[along] - 1), up, down) for turn in range(n)]


def received(sizes, along, messages, like):
    n, at = colours(sizes, along), lax.axis_index(AXES[along])
    if n == 0:
        return jnp.zeros_like(like), jnp.zeros_like(like)
    low = high = messages[0]
    for turn in range(1, n):
        low = jnp.where(turn_of(at + n - 1, along, n) == turn, messages[turn], low)
        high = jnp.where(turn_of(at, along, n) == turn, messages[turn], high)
    return jnp.where(at > 0, low, 0.0), jnp.where(at < sizes[along] - 1, high, 0.0)


def bend(a, difference):
    t = jnp.tanh(sharpness * difference)
    return t, 0.5 * sharpness * a * (1.0 - a) * (1.0 - t * t)


def low_end(low, w0, w1, a0, a1, c0):
    w_far, w_low, a_far, a_low, c_far, c_low = low
    _, bent = bend(a_low, a0 - a_far)
    across = w0 - w_low
    r_low = (across * jnp.maximum(c_low, 0.0) - (w_low - w_far) * jnp.minimum(c_far, 0.0)) * bent
    forth = (w1 - w0) * jnp.maximum(c0, 0.0)
    back = across * jnp.minimum(c_low, 0.0)
    t, bent = bend(a0, a1 - a_low)
    first = w0 * (c0 - c_low) + (forth + back) + (forth - back) * ((0.5 - a0) * t) + r_low
    return first, (forth - back) * bent


def high_end(high, w0, w1, a0, a1, c0, c1):
    w_high, w_far, a_high, a_far, c_high = high
    _, bent = bend(a_high, a_far - a1)
    across = w_high - w1
    r_high = ((w_far - w_high) * jnp.maximum(c_high, 0.0) - across * jnp.minimum(c1, 0.0)) * bent
    forth = across * jnp.maximum(c1, 0.0)
    back = (w1 - w0) * jnp.minimum(c0, 0.0)
    t, bent = bend(a1, a_high - a0)
    last = w1 * (c1 - c0) + (forth + back) + (forth - back) * ((0.5 - a1) * t) - r_high
    return last, (back - forth) * bent


def interior(g, w, a, c, dim):
    length = a.shape[dim]
    at = lax.broadcasted_iota(jnp.int32, a.shape, dim)
    inside = (at > 0) & (at < length - 1)
    prev = lambda value: pltpu.roll(value, 1, dim)
    after = lambda value: pltpu.roll(value, length - 1, dim)
    t, bent = bend(a, after(a) - prev(a))
    below = prev(c)
    forth = (after(w) - w) * jnp.maximum(c, 0.0)
    back = (w - prev(w)) * jnp.minimum(below, 0.0)
    apart = jnp.where(inside, forth - back, 0.0)
    own = jnp.where(inside, w * (c - below) + (forth + back), 0.0) + apart * ((0.5 - a) * t)
    r = apart * bent
    return g + own + (prev(r) - after(r))


def fold(planes, rows, lanes):
    per = lanes // (slot * planes)
    return per if per >= 1 and rows % (8 * per) == 0 else 1


def edge_lanes(shape, lanes):
    at = lax.broadcasted_iota(jnp.int32, shape, 1)
    return at, lax.rem(at, slot)


def z_pack(sizes, planes, rows, lanes, *refs):
    sources, targets, (w_ref, edge_ref, *out, sems) = refs[:4], refs[4:8], refs[8:]
    copies = [
        [
            pltpu.make_async_copy(src.at[x], dst.at[x], sems.at[n, x])
            for n, (src, dst) in enumerate(zip(sources, targets))
        ]
        for x in range(planes)
    ]
    for copy in itertools.chain(*copies):
        copy.start()
    cot, opened, a_ref, c_ref = targets
    per = fold(planes, rows, lanes)
    step = rows // per
    at, place = edge_lanes((rows, lanes), lanes)
    near = (at < 2) | (at >= lanes - 2)
    totals = [None] * 3
    for x in range(planes):
        for copy in copies[x]:
            copy.wait()
        w = cot[x] * opened[x].astype(jnp.float32)
        w_ref[x] = w
        for n, field in enumerate((w, a_ref[x], c_ref[x])):
            field = jnp.where(near, field, 0.0)
            for r in range(per):
                move = slot * (x + planes * r)
                part = field[r * step : (r + 1) * step]
                part = pltpu.roll(part, move, 1) if move else part
                totals[n] = part if totals[n] is None else totals[n] + part
    for n in range(3):
        edge_ref[n] = totals[n]
    _, place = edge_lanes((step, lanes), lanes)
    ends = [jnp.where(place >= slot - 2, total, 0.0) for total in totals]
    starts = [jnp.where(place < 2, total, 0.0) for total in totals]
    up = sum(pltpu.roll(end, 2 + 2 * n, 1) for n, end in enumerate(ends))
    down = sum(pltpu.roll(start, 2 * n, 1) if n else start for n, start in enumerate(starts))
    for ref, message in zip(out, to_send(sizes, 2, up, down)):
        ref[...] = message


def z_inner(g_ref, w_ref, a_ref, c_ref, out):
    for x in range(a_ref.shape[0]):
        out[x] = interior(g_ref[x], w_ref[x], a_ref[x], c_ref[x], 1)


def z_ends(edges, low, high, lanes):
    shift = lambda value, by: pltpu.roll(value, by % lanes, 1)
    w, a, c = edges
    _, place = edge_lanes(w.shape, lanes)
    low = [shift(low, -v) if v else low for v in range(6)]
    first, second = low_end(low, w, shift(w, -1), a, shift(a, -1), c)
    high = [shift(high, -v) if v else high for v in range(5)]
    last, before = high_end(
        high, shift(w, 2), shift(w, 1), shift(a, 2), shift(a, 1), shift(c, 2), shift(c, 1)
    )
    ends = jnp.where(place == 0, first, jnp.where(place == 1, shift(second, 1), 0.0))
    return jnp.where(
        place == slot - 1, shift(last, -1), jnp.where(place == slot - 2, shift(before, -2), ends)
    )


def spread(ends, x, r, planes, lanes):
    move = slot * (x + planes * r)
    return pltpu.roll(ends, lanes - move, 1) if move else ends


def z_sweep(sizes, partial, edges, opened, ay, cy, ax, cx, *rest):
    n_in = colours(sizes, 2)
    messages, (ends_ref, *out) = [m[...] for m in rest[:n_in]], rest[n_in:]
    planes, rows, lanes = ay.shape
    per = fold(planes, rows, lanes)
    step = rows // per
    low, high = received(sizes, 2, messages, edges[0])
    ends = z_ends([edges[n] for n in range(3)], low, high, lanes)
    ends_ref[...] = ends
    if not out:
        return
    at = lax.broadcasted_iota(jnp.int32, (8, lanes), 1)
    near = (at < 2) | (at >= lanes - 2)
    tile = lax.broadcasted_iota(jnp.int32, (8, lanes), 0)
    pick = lambda *tiles: jnp.where(tile < 2, tiles[0], jnp.where(tile < 4, tiles[1], tiles[2]))
    for x in range(planes):
        ws = []
        for rim, group, r in ((slice(0, 8), ends[:8], 0), (slice(rows - 8, rows), ends[step - 8 :], per - 1)):
            g = partial[x, rim] + jnp.where(near, spread(group, x, r, planes, lanes), 0.0)
            ws.append(opened[x, rim].astype(jnp.float32) * g)
        up = pick(
            *(
                pltpu.roll(field, by, 0)
                for field, by in ((ws[1], 2), (ay[x, rows - 8 :], 4), (cy[x, rows - 8 :], 6))
            )
        )
        down = pick(ws[0], pltpu.roll(ay[x, :8], 2, 0), pltpu.roll(cy[x, :8], 4, 0))
        for ref, message in zip(out, to_send(sizes, 1, up, down)):
            ref[x] = message


def x_products(w, cx):
    planes = len(w)
    back = (w[-1] - w[-2]) * jnp.minimum(cx[planes - 2], 0.0)
    forth = (w[1] - w[0]) * jnp.maximum(cx[0], 0.0)
    return (w[-1], w[0]), (back, forth)


def y_inner(sizes, partial_z, ends_ref, opened, ay, cy, ax, cx, partial, w_rims, *out):
    planes, rows, lanes = ay.shape
    ends = ends_ref[...]
    at = lax.broadcasted_iota(jnp.int32, (rows, lanes), 1)
    near = (at < 2) | (at >= lanes - 2)
    tile = lax.broadcasted_iota(jnp.int32, (8, lanes), 0)
    per = fold(planes, rows, lanes)
    ws = []
    for x in range(planes):
        mask = opened[x].astype(jnp.float32)
        parts = jnp.concatenate([spread(ends, x, r, planes, lanes) for r in range(per)], axis=0)
        g = partial_z[x] + jnp.where(near, parts, 0.0)
        w = mask * g
        w_rims[x] = jnp.where(tile < 4, w[:8], w[rows - 8 :])
        g = interior(g, w, ay[x], cy[x], 0)
        partial[x] = g
        ws.append(mask * g)
    pairs = (
        *x_products(ws, cx),
        (ax[planes - 2], ax[0]),
        (ax[planes - 1], ax[1]),
        (cx[planes - 1], cx[0]),
    )
    for v, (up, down) in enumerate(pairs):
        for ref, message in zip(out, to_send(sizes, 0, up, down)):
            ref[v] = message


def y_sweep(sizes, partial, w_rims, opened, ay, cy, cx, *rest):
    n_in = colours(sizes, 1)
    messages, (g_ref, *out) = rest[:n_in], rest[n_in:]
    planes, rows, lanes = ay.shape
    tile = lax.broadcasted_iota(jnp.int32, (8, lanes), 0)
    ws = []
    for x in range(planes):
        low, high = received(sizes, 1, [m[x] for m in messages], ay[x, :8])
        row = lambda ref, n: ref[x, n : n + 1]
        first, second = low_end(
            [low[v : v + 1] for v in range(6)],
            *(row(ref, n) for ref, n in ((w_rims, 0), (w_rims, 1), (ay, 0), (ay, 1), (cy, 0))),
        )
        last, before = high_end(
            [high[v : v + 1] for v in range(5)],
            row(w_rims, 6),
            row(w_rims, 7),
            *(row(ref, n) for ref in (ay, cy) for n in (rows - 2, rows - 1)),
        )
        top = partial[x, :8] + jnp.where(tile == 0, first, jnp.where(tile == 1, second, 0.0))
        bottom = partial[x, rows - 8 :] + jnp.where(
            tile == 7, last, jnp.where(tile == 6, before, 0.0)
        )
        g_ref[x, :8] = top
        g_ref[x, 8 : rows - 8] = partial[x, 8 : rows - 8]
        g_ref[x, rows - 8 :] = bottom
        mask = jnp.where(tile < 4, opened[x, :8], opened[x, rows - 8 :]).astype(jnp.float32)
        ws.append(mask * jnp.where(tile < 4, top, bottom))
    if out:
        c = [jnp.where(tile < 4, cx[x, :8], cx[x, rows - 8 :]) for x in range(planes)]
        for v, (up, down) in enumerate(x_products(ws, c)):
            for ref, message in zip(out, to_send(sizes, 0, up, down)):
                ref[v] = message


def x_sweep(sizes, g, opened, ax, cx, *rest):
    n_in = colours(sizes, 0)
    early, late, (out, stage, sems) = rest[:n_in], rest[n_in : 2 * n_in], rest[2 * n_in :]
    planes, rows, lanes = ax.shape
    tile = lax.broadcasted_iota(jnp.int32, (8, lanes), 0)

    def whole(n, v):
        if v > 1:
            return early[n][v]
        top = jnp.where(tile < 2, late[n][v], early[n][v, :8])
        bottom = jnp.where(tile >= 6, late[n][v], early[n][v, rows - 8 :])
        return jnp.concatenate([top, early[n][v, 8 : rows - 8], bottom], axis=0)

    (w_low, w_high), (b_low, f_high), (f0, h0), (f1, h1), (c_low, _) = (
        received(sizes, 0, [whole(n, v) for n in range(n_in)], ax[0]) for v in range(5)
    )
    last = planes - 1
    w = [opened[x].astype(jnp.float32) * g[x] for x in range(planes)]
    a = [f1, *(ax[x] for x in range(planes)), h0]
    c = [c_low, *(cx[x] for x in range(planes))]
    _, bent = bend(f1, a[1] - f0)
    r = [((w[0] - w_low) * jnp.maximum(c_low, 0.0) - b_low) * bent]
    own, copies = [], []

    def leave(x):
        stage[x] = own[x] + (r[x] - r[x + 2])
        copies.append(pltpu.make_async_copy(stage.at[x], out.at[x], sems.at[x]))
        copies[-1].start()

    for x in range(planes):
        t, bent = bend(a[x + 1], a[x + 2] - a[x])
        forth = ((w[x + 1] if x < last else w_high) - w[x]) * jnp.maximum(c[x + 1], 0.0)
        back = (w[x] - (w[x - 1] if x else w_low)) * jnp.minimum(c[x], 0.0)
        apart = forth - back
        r.append(apart * bent)
        own.append(
            g[x] + w[x] * (c[x + 1] - c[x]) + (forth + back) + apart * ((0.5 - a[x + 1]) * t)
        )
        if x:
            leave(x - 1)
    _, bent = bend(h0, h1 - a[planes])
    r.append((f_high - (w_high - w[last]) * jnp.minimum(c[planes], 0.0)) * bent)
    leave(last)
    for copy in copies:
        copy.wait()


def call(body, out, *args, name, loads=(), scratch=(), flops=0, target=pltpu.VMEM):
    shapes = [jax.ShapeDtypeStruct(o, jnp.float32) if isinstance(o, tuple) else o for o in out]
    loads = [pltpu.with_memory_space_constraint(v, pltpu.HBM) for v in loads]
    return pl.pallas_call(
        body,
        out_shape=shapes,
        in_specs=[pl.BlockSpec(memory_space=pltpu.VMEM)] * len(args)
        + [pl.BlockSpec(memory_space=pltpu.HBM)] * len(loads),
        out_specs=[pl.BlockSpec(memory_space=target)] * len(shapes),
        scratch_shapes=scratch,
        compiler_params=pltpu.CompilerParams(vmem_limit_bytes=8 * 2**20),
        cost_estimate=pl.CostEstimate(flops=flops, bytes_accessed=2**20, transcendentals=0),
        name=name,
    )(*args, *loads)


def per_device(sizes, cot, ax, ay, az, cx, cy, cz, opened):
    x_rounds, y_rounds, z_rounds = (pair_rounds(sizes, d) for d in range(3))
    early_rounds = pair_rounds(sizes, 0, 1)
    x_rounds = pair_rounds(sizes, 0, 0)
    block = az.shape
    planes, rows, lanes = block
    swap = lambda value, perm: lax.ppermute(value, AXES, perm)
    packed = (rows // fold(planes, rows, lanes), lanes)
    dma = pltpu.SemaphoreType.DMA
    cot, opened, az, cz, w, edges, *z_out = call(
        functools.partial(z_pack, sizes, planes, rows, lanes),
        [block, jax.ShapeDtypeStruct(block, jnp.int32), block, block, block, (3, *packed)]
        + [packed] * len(z_rounds),
        loads=(cot, opened, az, cz),
        name="z_pack", scratch=[dma((4, planes))],
    )
    z_in = [swap(m, p) for m, p in zip(z_out, z_rounds)]
    (partial,) = call(z_inner, [block], cot, w, az, cz, name="z_inner")
    ends, *y_out = call(
        functools.partial(z_sweep, sizes),
        [packed] + [(planes, 8, lanes)] * len(y_rounds),
        partial, edges, opened, ay, cy, ax, cx, *z_in,
        name="z_sweep",
    )
    y_in = [swap(m, p) for m, p in zip(y_out, y_rounds)]
    partial, w_rims, *x_out = call(
        functools.partial(y_inner, sizes),
        [block, (planes, 8, lanes)] + [(5, rows, lanes)] * len(x_rounds),
        partial, ends, opened, ay, cy, ax, cx,
        name="y_inner",
    )
    x_early = [swap(m, p) for m, p in zip(x_out, early_rounds)]
    g, *x_out = call(
        functools.partial(y_sweep, sizes),
        [block] + [(2, 8, lanes)] * len(x_rounds),
        partial, w_rims, opened, ay, cy, cx, *y_in,
        name="y_sweep", flops=10**10,
    )
    x_late = [swap(m, p) for m, p in zip(x_out, x_rounds)]
    (out,) = call(
        functools.partial(x_sweep, sizes), [block], g, opened, ax, cx, *x_early, *x_late,
        target=pltpu.HBM, name="x_sweep",
        scratch=[pltpu.VMEM(block, jnp.float32), dma((planes,))],
    )
    return out


def solution(mesh):
    sizes = tuple(mesh.shape[axis] for axis in AXES)
    placed = P(*AXES)
    return jax.shard_map(
        functools.partial(per_device, sizes),
        mesh=mesh,
        in_specs=(placed,) * 8,
        out_specs=placed,
        check_vma=False,
    )
```

time: 15.9 us -> 15.2 us (0.956)
  the two profiles are of different devices: /device:TPU:21 before, /device:TPU:0 now
where the time goes in v4:
time: 15.2 us; the launch traced here: 15 us
  starting transfers between devices  9.23 us (61%)
  Pallas kernels  3.35 us (22%)
  waiting for transfers between devices  2.33 us (15%)
    ppermute x8, starting transfers between devices, per_device(): swap = lambda value, perm: lax.ppermute(value, AXES, perm)  9.23 us
    pallas_call x6, Pallas kernels, call(): pl.pallas_call(body, out_shape=shapes, in_specs=[pl.BlockSpec(memory_spac...  3.35 us
    ppermute x8, waiting for transfers between devices, per_device(): swap = lambda value, perm: lax.ppermute(value, AXES, perm)  2.33 us
  transfers between devices with their start and end apart: 8, of which 3 were waited for; matrix products, arithmetic and copies ran while one was open for 0% of the time, Pallas kernels for 5%

profile of v4, /device:TPU:0, one launch (start us, length us, event | category | flops | bytes accessed | tf_op | source)
XLA Modules:
  0.0 15.0 jit_solution(8275097582419536586)
XLA Ops:
  0.0 1.4 %z_pack.1 = (f32[4,64,128]{2,1,0:T(8,128)S(1)}, s32[4,64,128]{2,1,0:T(8,128)S(1)}, f32[4,64,128]{2,1,0:T(8,128)S(1)}, f32[4,64,128]{2,1,0:T(8,128)S(1)}, f32[4,6...) custom-call(f32[4,64,128]{2,1,0:T(8,128)} %refs_0_.1, ...), custom_call_target="tpu_custom_call" | custom-call | bytes 1048576 | tf_op jit(solution)/shard_map/z_pack/pallas_call | solution.py:336
  1.4 3.1 %collective-permute-start = (f32[16,128]{1,0:T(8,128)S(1)}, f32[16,128]{1,0:T(8,128)S(1)}, u32[]{:S(2)}, u32[]{:S(2)}) collective-permute-start(f32[16,128]{1,0:T(8,128)S(1)} %get-tuple-element.29), channel_id=1, source_target_pairs={{0,1},{1,0},{2,10},{3,11},{4,5},{5,4},{6,14},{7,15},{8,9},{9,8},{1... | collective-permute-start | bytes 24584 | tf_op jit(solution)/shard_map/ppermute | solution.py:355
  4.5 0.0 collective-permute-start.1
  4.5 0.5 %collective-permute-start.2 = (f32[16,128]{1,0:T(8,128)S(1)}, f32[16,128]{1,0:T(8,128)S(1)}, u32[]{:S(2)}, u32[]{:S(2)}) collective-permute-start(f32[16,128]{1,0:T(8,128)S(1)} %get-tuple-element.31), channel_id=1, source_target_pairs={{0,8},{1,9},{2,3},{3,2},{4,12},{5,13},{6,7},{7,6},{8,0},{9,1},{10,... | collective-permute-start | bytes 24584 | tf_op jit(solution)/shard_map/ppermute | solution.py:355
  5.0 0.0 copy-start
  5.0 0.0 copy-start.1
  5.0 0.0 copy-start.2
  5.0 0.0 copy-start.3
  5.0 0.5 %z_inner.1.partial.partial_z = f32[4,64,128]{2,1,0:T(8,128)S(1)} custom-call(f32[4,64,128]{2,1,0:T(8,128)S(1)} %get-tuple-element.23.g_ref, f32[4,64,128]{2,1,0:T(8,128)S(1)} %get-tuple-element.24.w_ref, f32[4,64,128]{2,1,0:T(8,128)S(1)} %get-tuple-element.25.a_ref, f32[4,64,128]{2,1,0:T(8,128)S(1)} %get-tuple-element.26.c_ref), custom_call_target="tpu_custom_call" | custom-call | bytes 1048576 | tf_op jit(solution)/shard_map/z_inner/pallas_call | solution.py:336
  5.5 0.6 %collective-permute-done.rest_0_ = f32[16,128]{1,0:T(8,128)S(1)} collective-permute-done((f32[16,128]{1,0:T(8,128)S(1)}, f32[16,128]{1,0:T(8,128)S(1)}, u32[]{:S(2)}, u32[]{:S(2)}) %collective-permute-start) | collective-permute-done | bytes 8224 | tf_op jit(solution)/shard_map/ppermute | solution.py:355
  6.1 0.0 collective-permute-done.1.rest_1_
  6.1 0.0 collective-permute-done.2.rest_2_
  6.1 0.0 copy-done
  6.2 0.0 copy-done.1
  6.2 0.0 copy-done.2
  6.2 0.0 copy-done.3
  6.2 0.3 %z_sweep.1 = (f32[16,128]{1,0:T(8,128)S(1)}, f32[4,8,128]{2,1,0:T(8,128)S(1)}) custom-call(f32[4,64,128]{2,1,0:T(8,128)S(1)} %z_inner.1.partial.partial_z, f32[3,16,128]{2,1,0:T(8,128)S(1)} %get-tuple-element.27.edges, s32[4,64,128]{2,1,0:T(8,128)S(1)} %get-tuple-element.28.opened, f32[4,64,128]{2,1,0:T(8,128)S(1)} %copy-done.2, ...), custom_call_target="tpu_custom_call" | custom-call | bytes 1048576 | tf_op jit(solution)/shard_map/z_sweep/pallas_call | solution.py:336
  6.5 2.0 %collective-permute-start.3 = (f32[4,8,128]{2,1,0:T(8,128)S(1)}, f32[4,8,128]{2,1,0:T(8,128)S(1)}, u32[]{:S(2)}, u32[]{:S(2)}) collective-permute-start(f32[4,8,128]{2,1,0:T(8,128)S(1)} %get-tuple-element.35), channel_id=1, source_target_pairs={{0,4},{1,5},{2,6},{3,7},{4,0},{5,1},{6,2},{7,3},{8,12},{9,13},{10,... | collective-permute-start | bytes 49160 | tf_op jit(solution)/shard_map/ppermute | solution.py:355
  8.5 0.3 %y_inner.1 = (f32[4,64,128]{2,1,0:T(8,128)S(1)}, f32[4,8,128]{2,1,0:T(8,128)S(1)}, f32[5,64,128]{2,1,0:T(8,128)S(1)}, f32[5,64,128]{2,1,0:T(8,128)S(1)}) custom-call(f32[4,64,128]{2,1,0:T(8,128)S(1)} %z_inner.1.partial.partial_z, f32[16,128]{1,0:T(8,128)S(1)} %get-tuple-element.32.ends_ref, s32[4,64,128]{2,1,0:T(8,128)S(1)} %get-tuple-element.28.opened, ...), custom_call_target="tpu_custom_call" | custom-call | bytes 1048576 | tf_op jit(solution)/shard_map/y_inner/pallas_call | solution.py:336
  8.8 0.1 collective-permute-start.4
  8.9 1.5 %collective-permute-start.5 = (f32[5,64,128]{2,1,0:T(8,128)S(1)}, f32[5,64,128]{2,1,0:T(8,128)S(1)}, u32[]{:S(2)}, u32[]{:S(2)}) collective-permute-start(f32[5,64,128]{2,1,0:T(8,128)S(1)} %get-tuple-element.38), channel_id=1, source_target_pairs={{0,8},{1,9},{2,10},{3,11},{4,12},{5,13},{6,14},{7,15},{8,0},{9,1},... | collective-permute-start | bytes 491528 | tf_op jit(solution)/shard_map/ppermute | solution.py:355
  10.4 0.0 collective-permute-done.3.rest_0_
  10.4 0.1 y_sweep.1
  10.5 0.1 collective-permute-start.6
  10.7 1.8 %collective-permute-start.7 = (f32[2,8,128]{2,1,0:T(8,128)S(1)}, f32[2,8,128]{2,1,0:T(8,128)S(1)}, u32[]{:S(2)}, u32[]{:S(2)}) collective-permute-start(f32[2,8,128]{2,1,0:T(8,128)S(1)} %get-tuple-element.40), channel_id=1, source_target_pairs={{0,8},{1,9},{2,10},{3,11},{4,12},{5,13},{6,14},{7,15},{8,0},{9,1},... | collective-permute-start | bytes 24584 | tf_op jit(solution)/shard_map/ppermute | solution.py:355
  12.5 1.2 %collective-permute-done.6.rest_2_ = f32[2,8,128]{2,1,0:T(8,128)S(1)} collective-permute-done((f32[2,8,128]{2,1,0:T(8,128)S(1)}, f32[2,8,128]{2,1,0:T(8,128)S(1)}, u32[]{:S(2)}, u32[]{:S(2)}) %collective-permute-start.6) | collective-permute-done | bytes 8224 | tf_op jit(solution)/shard_map/ppermute | solution.py:355
  13.7 0.0 collective-permute-done.7.rest_3_
  13.7 0.4 %collective-permute-done.4.rest_0_ = f32[5,64,128]{2,1,0:T(8,128)S(1)} collective-permute-done((f32[5,64,128]{2,1,0:T(8,128)S(1)}, f32[5,64,128]{2,1,0:T(8,128)S(1)}, u32[]{:S(2)}, u32[]{:S(2)}) %collective-permute-start.4) | collective-permute-done | bytes 163872 | tf_op jit(solution)/shard_map/ppermute | solution.py:355
  14.1 0.0 collective-permute-done.5.rest_1_
  14.1 0.9 %x_sweep.1 = f32[4,64,128]{2,1,0:T(8,128)} custom-call(f32[4,64,128]{2,1,0:T(8,128)S(1)} %get-tuple-element.36.g, s32[4,64,128]{2,1,0:T(8,128)S(1)} %get-tuple-element.28.opened, f32[4,64,128]{2,1,0:T(8,128)S(1)} %copy-done, f32[4,64,128]{2,1,0:T(8,128)S(1)} %copy-done.1, f32[5,64,128]{2,1,0:T(8,128)S(1)} %collective-permute-done.4.rest_0_, ...), custom_call_target="tpu_custom_call" | custom-call | bytes 1048576 | tf_op jit(solution)/shard_map/x_sweep/pallas_call | solution.py:336
Async XLA Ops:
  1.4 4.7 %collective-permute-start = (f32[16,128]{1,0:T(8,128)S(1)}, f32[16,128]{1,0:T(8,128)S(1)}, u32[]{:S(2)}, u32[]{:S(2)}) collective-permute-start(f32[16,128]{1,0:T(8,128)S(1)} %get-tuple-element.29), channel_id=1, source_target_pairs={{0,1},{1,0},{2,10},{3,11},{4,5},{5,4},{6,14},{7,15},{8,9},{9,8},{1... | collective-permute-start | bytes 24584 | tf_op jit(solution)/shard_map/ppermute | solution.py:355
  4.5 1.6 %collective-permute-start.1 = (f32[16,128]{1,0:T(8,128)S(1)}, f32[16,128]{1,0:T(8,128)S(1)}, u32[]{:S(2)}, u32[]{:S(2)}) collective-permute-start(f32[16,128]{1,0:T(8,128)S(1)} %get-tuple-element.30), channel_id=1, source_target_pairs={{0,8},{1,2},{2,1},{3,11},{4,12},{5,6},{6,5},{7,15},{8,0},{9,10},{1... | collective-permute-start | bytes 24584 | tf_op jit(solution)/shard_map/ppermute | solution.py:355
  4.5 1.6 %collective-permute-start.2 = (f32[16,128]{1,0:T(8,128)S(1)}, f32[16,128]{1,0:T(8,128)S(1)}, u32[]{:S(2)}, u32[]{:S(2)}) collective-permute-start(f32[16,128]{1,0:T(8,128)S(1)} %get-tuple-element.31), channel_id=1, source_target_pairs={{0,8},{1,9},{2,3},{3,2},{4,12},{5,13},{6,7},{7,6},{8,0},{9,1},{10,... | collective-permute-start | bytes 24584 | tf_op jit(solution)/shard_map/ppermute | solution.py:355
  5.0 1.1 %copy-start = (f32[4,64,128]{2,1,0:T(8,128)S(1)}, f32[4,64,128]{2,1,0:T(8,128)}, u32[]{:S(2)}) copy-start(f32[4,64,128]{2,1,0:T(8,128)} %ax.5) | copy-start | bytes 393220
  5.0 1.1 %copy-start.1 = (f32[4,64,128]{2,1,0:T(8,128)S(1)}, f32[4,64,128]{2,1,0:T(8,128)}, u32[]{:S(2)}) copy-start(f32[4,64,128]{2,1,0:T(8,128)} %cx.7) | copy-start | bytes 393220
  5.0 1.1 %copy-start.2 = (f32[4,64,128]{2,1,0:T(8,128)S(1)}, f32[4,64,128]{2,1,0:T(8,128)}, u32[]{:S(2)}) copy-start(f32[4,64,128]{2,1,0:T(8,128)} %ay.5) | copy-start | bytes 393220
  5.0 1.1 %copy-start.3 = (f32[4,64,128]{2,1,0:T(8,128)S(1)}, f32[4,64,128]{2,1,0:T(8,128)}, u32[]{:S(2)}) copy-start(f32[4,64,128]{2,1,0:T(8,128)} %cy.5) | copy-start | bytes 393220
  6.5 4.0 %collective-permute-start.3 = (f32[4,8,128]{2,1,0:T(8,128)S(1)}, f32[4,8,128]{2,1,0:T(8,128)S(1)}, u32[]{:S(2)}, u32[]{:S(2)}) collective-permute-start(f32[4,8,128]{2,1,0:T(8,128)S(1)} %get-tuple-element.35), channel_id=1, source_target_pairs={{0,4},{1,5},{2,6},{3,7},{4,0},{5,1},{6,2},{7,3},{8,12},{9,13},{10,... | collective-permute-start | bytes 49160 | tf_op jit(solution)/shard_map/ppermute | solution.py:355
  8.8 5.4 %collective-permute-start.4 = (f32[5,64,128]{2,1,0:T(8,128)S(1)}, f32[5,64,128]{2,1,0:T(8,128)S(1)}, u32[]{:S(2)}, u32[]{:S(2)}) collective-permute-start(f32[5,64,128]{2,1,0:T(8,128)S(1)} %get-tuple-element.37), channel_id=1, source_target_pairs={{0,4},{1,5},{2,6},{3,7},{4,0},{5,1},{6,2},{7,3},{8,16},{9,17},{10,... | collective-permute-start | bytes 491528 | tf_op jit(solution)/shard_map/ppermute | solution.py:355
  8.9 5.3 %collective-permute-start.5 = (f32[5,64,128]{2,1,0:T(8,128)S(1)}, f32[5,64,128]{2,1,0:T(8,128)S(1)}, u32[]{:S(2)}, u32[]{:S(2)}) collective-permute-start(f32[5,64,128]{2,1,0:T(8,128)S(1)} %get-tuple-element.38), channel_id=1, source_target_pairs={{0,8},{1,9},{2,10},{3,11},{4,12},{5,13},{6,14},{7,15},{8,0},{9,1},... | collective-permute-start | bytes 491528 | tf_op jit(solution)/shard_map/ppermute | solution.py:355
  10.5 3.2 %collective-permute-start.6 = (f32[2,8,128]{2,1,0:T(8,128)S(1)}, f32[2,8,128]{2,1,0:T(8,128)S(1)}, u32[]{:S(2)}, u32[]{:S(2)}) collective-permute-start(f32[2,8,128]{2,1,0:T(8,128)S(1)} %get-tuple-element.39), channel_id=1, source_target_pairs={{0,24},{1,25},{2,26},{3,27},{4,28},{5,29},{6,30},{7,31},{8,16},{9,... | collective-permute-start | bytes 24584 | tf_op jit(solution)/shard_map/ppermute | solution.py:355
  10.7 3.0 %collective-permute-start.7 = (f32[2,8,128]{2,1,0:T(8,128)S(1)}, f32[2,8,128]{2,1,0:T(8,128)S(1)}, u32[]{:S(2)}, u32[]{:S(2)}) collective-permute-start(f32[2,8,128]{2,1,0:T(8,128)S(1)} %get-tuple-element.40), channel_id=1, source_target_pairs={{0,8},{1,9},{2,10},{3,11},{4,12},{5,13},{6,14},{7,15},{8,0},{9,1},... | collective-permute-start | bytes 24584 | tf_op jit(solution)/shard_map/ppermute | solution.py:355

commit v5 on v4

--- a/solution.py
+++ b/solution.py
@@ -90,20 +90,31 @@
     return last, (back - forth) * bent
 
 
-def interior(g, w, a, c, dim):
+def factors(a, c, dim):
     length = a.shape[dim]
     at = lax.broadcasted_iota(jnp.int32, a.shape, dim)
     inside = (at > 0) & (at < length - 1)
+    below = pltpu.roll(c, 1, dim)
+    t, bent = bend(a, pltpu.roll(a, length - 1, dim) - pltpu.roll(a, 1, dim))
+    return (
+        jnp.where(inside, c - below, 0.0),
+        jnp.where(inside, jnp.maximum(c, 0.0), 0.0),
+        jnp.where(inside, jnp.minimum(below, 0.0), 0.0),
+        (0.5 - a) * t,
+        bent,
+    )
+
+
+def interior(g, w, parts, dim):
+    rise, ahead, behind, lean, bent = parts
+    length = w.shape[dim]
     prev = lambda value: pltpu.roll(value, 1, dim)
     after = lambda value: pltpu.roll(value, length - 1, dim)
-    t, bent = bend(a, after(a) - prev(a))
-    below = prev(c)
-    forth = (after(w) - w) * jnp.maximum(c, 0.0)
-    back = (w - prev(w)) * jnp.minimum(below, 0.0)
-    apart = jnp.where(inside, forth - back, 0.0)
-    own = jnp.where(inside, w * (c - below) + (forth + back), 0.0) + apart * ((0.5 - a) * t)
+    forth = (after(w) - w) * ahead
+    back = (w - prev(w)) * behind
+    apart = forth - back
     r = apart * bent
-    return g + own + (prev(r) - after(r))
+    return g + (w * rise + (forth + back) + apart * lean) + (prev(r) - after(r))
 
 
 def fold(planes, rows, lanes):
@@ -134,7 +145,7 @@
     near = (at < 2) | (at >= lanes - 2)
     totals = [None] * 3
     for x in range(planes):
-        for copy in copies[x]:
+        for copy in itertools.chain(*({0: copies[:2], 2: copies[2:]}.get(x, []))):
             copy.wait()
         w = cot[x] * opened[x].astype(jnp.float32)
         w_ref[x] = w
@@ -158,7 +169,13 @@
 
 def z_inner(g_ref, w_ref, a_ref, c_ref, out):
     for x in range(a_ref.shape[0]):
-        out[x] = interior(g_ref[x], w_ref[x], a_ref[x], c_ref[x], 1)
+        out[x] = interior(g_ref[x], w_ref[x], factors(a_ref[x], c_ref[x], 1), 1)
+
+
+def y_factors(ay, cy, *out):
+    for x in range(ay.shape[0]):
+        for ref, part in zip(out, factors(ay[x], cy[x], 0)):
+            ref[x] = part
 
 
 def z_ends(edges, low, high, lanes):
@@ -182,7 +199,7 @@
     return pltpu.roll(ends, lanes - move, 1) if move else ends
 
 
-def z_sweep(sizes, partial, edges, opened, ay, cy, ax, cx, *rest):
+def z_sweep(sizes, partial, edges, opened, ay, cy, ax, cx, _, *rest):
     n_in = colours(sizes, 2)
     messages, (ends_ref, *out) = [m[...] for m in rest[:n_in]], rest[n_in:]
     planes, rows, lanes = ay.shape
@@ -220,8 +237,9 @@
     return (w[-1], w[0]), (back, forth)
 
 
-def y_inner(sizes, partial_z, ends_ref, opened, ay, cy, ax, cx, partial, w_rims, *out):
-    planes, rows, lanes = ay.shape
+def y_inner(sizes, partial_z, ends_ref, opened, ax, cx, *rest):
+    parts_y, (partial, w_rims, *out) = rest[:5], rest[5:]
+    planes, rows, lanes = ax.shape
     ends = ends_ref[...]
     at = lax.broadcasted_iota(jnp.int32, (rows, lanes), 1)
     near = (at < 2) | (at >= lanes - 2)
@@ -234,18 +252,20 @@
         g = partial_z[x] + jnp.where(near, parts, 0.0)
         w = mask * g
         w_rims[x] = jnp.where(tile < 4, w[:8], w[rows - 8 :])
-        g = interior(g, w, ay[x], cy[x], 0)
+        g = interior(g, w, [part[x] for part in parts_y], 0)
         partial[x] = g
         ws.append(mask * g)
     pairs = (
         *x_products(ws, cx),
         (ax[planes - 2], ax[0]),
         (ax[planes - 1], ax[1]),
-        (cx[planes - 1], cx[0]),
     )
     for v, (up, down) in enumerate(pairs):
         for ref, message in zip(out, to_send(sizes, 0, up, down)):
-            ref[v] = message
+            ref[v * rows : (v + 1) * rows] = message
+    half = slice(0, rows // 2)
+    for ref, message in zip(out, to_send(sizes, 0, cx[planes - 1, half], cx[0, half])):
+        ref[4 * rows :] = message
 
 
 def y_sweep(sizes, partial, w_rims, opened, ay, cy, cx, *rest):
@@ -280,52 +300,81 @@
         c = [jnp.where(tile < 4, cx[x, :8], cx[x, rows - 8 :]) for x in range(planes)]
         for v, (up, down) in enumerate(x_products(ws, c)):
             for ref, message in zip(out, to_send(sizes, 0, up, down)):
-                ref[v] = message
-
-
-def x_sweep(sizes, g, opened, ax, cx, *rest):
+                ref[8 * v : 8 * v + 8] = message
+        half = slice(rows // 2, rows)
+        for ref, message in zip(out, to_send(sizes, 0, cx[planes - 1, half], cx[0, half])):
+            ref[16:] = message
+
+
+def x_inner(g_ref, opened, ax, cx, ready, own_ref, r_ref):
+    planes = ax.shape[0]
+    last = planes - 1
+    w = [opened[x].astype(jnp.float32) * g_ref[x] for x in range(planes)]
+    ready[0], ready[1] = w[0], w[last]
+    ready[2] = (w[1] - w[0]) * jnp.maximum(cx[0], 0.0)
+    ready[3] = (w[last] - w[last - 1]) * jnp.minimum(cx[last - 1], 0.0)
+    for x in range(1, last):
+        t, bent = bend(ax[x], ax[x + 1] - ax[x - 1])
+        forth = (w[x + 1] - w[x]) * jnp.maximum(cx[x], 0.0)
+        back = (w[x] - w[x - 1]) * jnp.minimum(cx[x - 1], 0.0)
+        apart = forth - back
+        r_ref[x - 1] = apart * bent
+        own_ref[x - 1] = (
+            g_ref[x] + w[x] * (cx[x] - cx[x - 1]) + (forth + back) + apart * ((0.5 - ax[x]) * t)
+        )
+
+
+def x_sweep(sizes, g_ref, ax, cx, ready, own_ref, r_ref, *rest):
     n_in = colours(sizes, 0)
     early, late, (out, stage, sems) = rest[:n_in], rest[n_in : 2 * n_in], rest[2 * n_in :]
     planes, rows, lanes = ax.shape
+    last = planes - 1
     tile = lax.broadcasted_iota(jnp.int32, (8, lanes), 0)
 
     def whole(n, v):
+        if v == 4:
+            return jnp.concatenate([early[n][4 * rows :], late[n][16:]], axis=0)
+        value = early[n][v * rows : (v + 1) * rows]
         if v > 1:
-            return early[n][v]
-        top = jnp.where(tile < 2, late[n][v], early[n][v, :8])
-        bottom = jnp.where(tile >= 6, late[n][v], early[n][v, rows - 8 :])
-        return jnp.concatenate([top, early[n][v, 8 : rows - 8], bottom], axis=0)
+            return value
+        ends = late[n][8 * v : 8 * v + 8]
+        top = jnp.where(tile < 2, ends, value[:8])
+        bottom = jnp.where(tile >= 6, ends, value[rows - 8 :])
+        return jnp.concatenate([top, value[8 : rows - 8], bottom], axis=0)
 
     (w_low, w_high), (b_low, f_high), (f0, h0), (f1, h1), (c_low, _) = (
         received(sizes, 0, [whole(n, v) for n in range(n_in)], ax[0]) for v in range(5)
     )
-    last = planes - 1
-    w = [opened[x].astype(jnp.float32) * g[x] for x in range(planes)]
-    a = [f1, *(ax[x] for x in range(planes)), h0]
-    c = [c_low, *(cx[x] for x in range(planes))]
-    _, bent = bend(f1, a[1] - f0)
-    r = [((w[0] - w_low) * jnp.maximum(c_low, 0.0) - b_low) * bent]
-    own, copies = [], []
-
-    def leave(x):
-        stage[x] = own[x] + (r[x] - r[x + 2])
+    copies = []
+
+    def leave(x, value):
+        stage[x] = value
         copies.append(pltpu.make_async_copy(stage.at[x], out.at[x], sems.at[x]))
         copies[-1].start()
 
+    def outer(x, w, a_next, forth, back, c_low):
+        t, bent = bend(ax[x], a_next)
+        apart = forth - back
+        own = g_ref[x] + w * (cx[x] - c_low) + (forth + back) + apart * ((0.5 - ax[x]) * t)
+        return own, apart * bent
+
+    w_first, w_last = ready[0], ready[1]
+    across = w_first - w_low
+    own_first, r_first = outer(
+        0, w_first, ax[1] - f1, ready[2], across * jnp.minimum(c_low, 0.0), c_low
+    )
+    _, bent = bend(f1, ax[0] - f0)
+    r_low = (across * jnp.maximum(c_low, 0.0) - b_low) * bent
+    across = w_high - w_last
+    own_last, r_last = outer(
+        last, w_last, h0 - ax[last - 1], across * jnp.maximum(cx[last], 0.0), ready[3], cx[last - 1]
+    )
+    _, bent = bend(h0, h1 - ax[last])
+    r_high = (f_high - across * jnp.minimum(cx[last], 0.0)) * bent
+    r = [r_low, r_first, *(r_ref[x] for x in range(last - 1)), r_last, r_high]
     for x in range(planes):
-        t, bent = bend(a[x + 1], a[x + 2] - a[x])
-        forth = ((w[x + 1] if x < last else w_high) - w[x]) * jnp.maximum(c[x + 1], 0.0)
-        back = (w[x] - (w[x - 1] if x else w_low)) * jnp.minimum(c[x], 0.0)
-        apart = forth - back
-        r.append(apart * bent)
-        own.append(
-            g[x] + w[x] * (c[x + 1] - c[x]) + (forth + back) + apart * ((0.5 - a[x + 1]) * t)
-        )
-        if x:
-            leave(x - 1)
-    _, bent = bend(h0, h1 - a[planes])
-    r.append((f_high - (w_high - w[last]) * jnp.minimum(c[planes], 0.0)) * bent)
-    leave(last)
+        own = own_first if x == 0 else own_last if x == last else own_ref[x - 1]
+        leave(x, own + (r[x] - r[x + 2]))
     for copy in copies:
         copy.wait()
 
@@ -364,29 +413,33 @@
     )
     z_in = [swap(m, p) for m, p in zip(z_out, z_rounds)]
     (partial,) = call(z_inner, [block], cot, w, az, cz, name="z_inner")
+    parts_y = call(y_factors, [block] * 5, ay, cy, name="y_factors")
     ends, *y_out = call(
         functools.partial(z_sweep, sizes),
         [packed] + [(planes, 8, lanes)] * len(y_rounds),
-        partial, edges, opened, ay, cy, ax, cx, *z_in,
+        partial, edges, opened, ay, cy, ax, cx, parts_y[0], *z_in,
         name="z_sweep",
     )
     y_in = [swap(m, p) for m, p in zip(y_out, y_rounds)]
     partial, w_rims, *x_out = call(
         functools.partial(y_inner, sizes),
-        [block, (planes, 8, lanes)] + [(5, rows, lanes)] * len(x_rounds),
-        partial, ends, opened, ay, cy, ax, cx,
+        [block, (planes, 8, lanes)] + [(4 * rows + rows // 2, lanes)] * len(x_rounds),
+        partial, ends, opened, ax, cx, *parts_y,
         name="y_inner",
     )
     x_early = [swap(m, p) for m, p in zip(x_out, early_rounds)]
     g, *x_out = call(
         functools.partial(y_sweep, sizes),
-        [block] + [(2, 8, lanes)] * len(x_rounds),
+        [block] + [(16 + rows // 2, lanes)] * len(x_rounds),
         partial, w_rims, opened, ay, cy, cx, *y_in,
         name="y_sweep", flops=10**10,
     )
     x_late = [swap(m, p) for m, p in zip(x_out, x_rounds)]
+    ready = call(
+        x_inner, [(4, rows, lanes)] + [(planes - 2, rows, lanes)] * 2, g, opened, ax, cx, name="x_inner"
+    )
     (out,) = call(
-        functools.partial(x_sweep, sizes), [block], g, opened, ax, cx, *x_early, *x_late,
+        functools.partial(x_sweep, sizes), [block], g, ax, cx, *ready, *x_early, *x_late,
         target=pltpu.HBM, name="x_sweep",
         scratch=[pltpu.VMEM(block, jnp.float32), dma((planes,))],
     )

time: 15.2 us -> 14.9 us (0.980)
  the two profiles are of different devices: /device:TPU:0 before, /device:TPU:21 now
where the time goes in v5:
time: 14.9 us; the launch traced here: 14.8 us
  starting transfers between devices  8.88 us (60%)
  Pallas kernels  3.35 us (22%)
  waiting for transfers between devices  2.44 us (16%)
    ppermute x8, starting transfers between devices, per_device(): swap = lambda value, perm: lax.ppermute(value, AXES, perm)  8.88 us
    pallas_call x8, Pallas kernels, call(): pl.pallas_call(body, out_shape=shapes, in_specs=[pl.BlockSpec(memory_spac...  3.35 us
    ppermute x8, waiting for transfers between devices, per_device(): swap = lambda value, perm: lax.ppermute(value, AXES, perm)  2.44 us
  transfers between devices with their start and end apart: 8, of which 2 were waited for; matrix products, arithmetic and copies ran while one was open for 0% of the time, Pallas kernels for 6%

profile of v5, /device:TPU:21, one launch (start us, length us, event | category | flops | bytes accessed | tf_op | source)
XLA Modules:
  0.0 14.8 jit_solution(167255896603248004)
XLA Ops:
  0.0 0.0 copy-start.2
  0.0 0.0 copy-start.3
  0.0 1.4 %z_pack.1 = (f32[4,64,128]{2,1,0:T(8,128)S(1)}, s32[4,64,128]{2,1,0:T(8,128)S(1)}, f32[4,64,128]{2,1,0:T(8,128)S(1)}, f32[4,64,128]{2,1,0:T(8,128)S(1)}, f32[4,6...) custom-call(f32[4,64,128]{2,1,0:T(8,128)} %refs_0_.1, ...), custom_call_target="tpu_custom_call" | custom-call | bytes 1048576 | tf_op jit(solution)/shard_map/z_pack/pallas_call | solution.py:385
  1.4 0.7 %collective-permute-start = (f32[16,128]{1,0:T(8,128)S(1)}, f32[16,128]{1,0:T(8,128)S(1)}, u32[]{:S(2)}, u32[]{:S(2)}) collective-permute-start(f32[16,128]{1,0:T(8,128)S(1)} %get-tuple-element.38), channel_id=1, source_target_pairs={{0,1},{1,0},{2,10},{3,11},{4,5},{5,4},{6,14},{7,15},{8,9},{9,8},{1... | collective-permute-start | bytes 24584 | tf_op jit(solution)/shard_map/ppermute | solution.py:404
  2.1 0.0 collective-permute-start.1
  2.1 1.4 %collective-permute-start.2 = (f32[16,128]{1,0:T(8,128)S(1)}, f32[16,128]{1,0:T(8,128)S(1)}, u32[]{:S(2)}, u32[]{:S(2)}) collective-permute-start(f32[16,128]{1,0:T(8,128)S(1)} %get-tuple-element.40), channel_id=1, source_target_pairs={{0,8},{1,9},{2,3},{3,2},{4,12},{5,13},{6,7},{7,6},{8,0},{9,1},{10,... | collective-permute-start | bytes 24584 | tf_op jit(solution)/shard_map/ppermute | solution.py:404
  3.5 0.0 copy-done.2
  3.5 0.0 copy-done.3
  3.5 0.1 y_factors.1
  3.6 0.0 copy-start
  3.6 0.0 copy-start.1
  3.6 0.5 %z_inner.1.partial.partial_z = f32[4,64,128]{2,1,0:T(8,128)S(1)} custom-call(f32[4,64,128]{2,1,0:T(8,128)S(1)} %get-tuple-element.31.g_ref, f32[4,64,128]{2,1,0:T(8,128)S(1)} %get-tuple-element.32.w_ref, f32[4,64,128]{2,1,0:T(8,128)S(1)} %get-tuple-element.33.a_ref, f32[4,64,128]{2,1,0:T(8,128)S(1)} %get-tuple-element.34.c_ref), custom_call_target="tpu_custom_call" | custom-call | bytes 1048576 | tf_op jit(solution)/shard_map/z_inner/pallas_call | solution.py:385
  4.1 0.0 collective-permute-done.rest_0_
  4.1 0.5 %collective-permute-done.1.rest_1_ = f32[16,128]{1,0:T(8,128)S(1)} collective-permute-done((f32[16,128]{1,0:T(8,128)S(1)}, f32[16,128]{1,0:T(8,128)S(1)}, u32[]{:S(2)}, u32[]{:S(2)}) %collective-permute-start.1) | collective-permute-done | bytes 8224 | tf_op jit(solution)/shard_map/ppermute | solution.py:404
  4.6 0.0 collective-permute-done.2.rest_2_
  4.6 0.0 copy-done
  4.6 0.0 copy-done.1
  4.7 0.3 %z_sweep.1 = (f32[16,128]{1,0:T(8,128)S(1)}, f32[4,8,128]{2,1,0:T(8,128)S(1)}) custom-call(f32[4,64,128]{2,1,0:T(8,128)S(1)} %z_inner.1.partial.partial_z, f32[3,16,128]{2,1,0:T(8,128)S(1)} %get-tuple-element.35.edges, s32[4,64,128]{2,1,0:T(8,128)S(1)} %get-tuple-element.36.opened, f32[4,64,128]{2,1,0:T(8,128)S(1)} %copy-done.2, ...), custom_call_target="tpu_custom_call" | custom-call | bytes 1048576 | tf_op jit(solution)/shard_map/z_sweep/pallas_call | solution.py:385
  4.9 0.3 %collective-permute-start.3 = (f32[4,8,128]{2,1,0:T(8,128)S(1)}, f32[4,8,128]{2,1,0:T(8,128)S(1)}, u32[]{:S(2)}, u32[]{:S(2)}) collective-permute-start(f32[4,8,128]{2,1,0:T(8,128)S(1)} %get-tuple-element.48), channel_id=1, source_target_pairs={{0,4},{1,5},{2,6},{3,7},{4,0},{5,1},{6,2},{7,3},{8,12},{9,13},{10,... | collective-permute-start | bytes 49160 | tf_op jit(solution)/shard_map/ppermute | solution.py:404
  5.2 0.2 %y_inner.1 = (f32[4,64,128]{2,1,0:T(8,128)S(1)}, f32[4,8,128]{2,1,0:T(8,128)S(1)}, f32[288,128]{1,0:T(8,128)S(1)}, f32[288,128]{1,0:T(8,128)S(1)}) custom-call(f32[4,64,128]{2,1,0:T(8,128)S(1)} %z_inner.1.partial.partial_z, f32[16,128]{1,0:T(8,128)S(1)} %get-tuple-element.41.ends_ref, s32[4,64,128]{2,1,0:T(8,128)S(1)} %get-tuple-element.36.opened, ...), custom_call_target="tpu_custom_call" | custom-call | bytes 1048576 | tf_op jit(solution)/shard_map/y_inner/pallas_call | solution.py:385
  5.4 3.5 %collective-permute-start.4 = (f32[288,128]{1,0:T(8,128)S(1)}, f32[288,128]{1,0:T(8,128)S(1)}, u32[]{:S(2)}, u32[]{:S(2)}) collective-permute-start(f32[288,128]{1,0:T(8,128)S(1)} %get-tuple-element.53), channel_id=1, source_target_pairs={{0,4},{1,5},{2,6},{3,7},{4,0},{5,1},{6,2},{7,3},{8,16},{9,17},{10,... | collective-permute-start | bytes 442376 | tf_op jit(solution)/shard_map/ppermute | solution.py:404
  8.9 0.4 %collective-permute-start.5 = (f32[288,128]{1,0:T(8,128)S(1)}, f32[288,128]{1,0:T(8,128)S(1)}, u32[]{:S(2)}, u32[]{:S(2)}) collective-permute-start(f32[288,128]{1,0:T(8,128)S(1)} %get-tuple-element.54), channel_id=1, source_target_pairs={{0,8},{1,9},{2,10},{3,11},{4,12},{5,13},{6,14},{7,15},{8,0},{9,1},... | collective-permute-start | bytes 442376 | tf_op jit(solution)/shard_map/ppermute | solution.py:404
  9.3 0.0 collective-permute-done.3.rest_0_
  9.3 0.1 y_sweep.1
  9.4 2.6 %collective-permute-start.6 = (f32[48,128]{1,0:T(8,128)S(1)}, f32[48,128]{1,0:T(8,128)S(1)}, u32[]{:S(2)}, u32[]{:S(2)}) collective-permute-start(f32[48,128]{1,0:T(8,128)S(1)} %get-tuple-element.55), channel_id=1, source_target_pairs={{0,24},{1,25},{2,26},{3,27},{4,28},{5,29},{6,30},{7,31},{8,16},{9,... | collective-permute-start | bytes 73736 | tf_op jit(solution)/shard_map/ppermute | solution.py:404
  12.0 0.0 collective-permute-start.7
  12.0 0.1 x_inner.1
  12.1 1.9 %collective-permute-done.6.rest_2_ = f32[48,128]{1,0:T(8,128)S(1)} collective-permute-done((f32[48,128]{1,0:T(8,128)S(1)}, f32[48,128]{1,0:T(8,128)S(1)}, u32[]{:S(2)}, u32[]{:S(2)}) %collective-permute-start.6) | collective-permute-done | bytes 24608 | tf_op jit(solution)/shard_map/ppermute | solution.py:404
  14.0 0.0 collective-permute-done.7.rest_3_
  14.0 0.0 collective-permute-done.4.rest_0_
  14.0 0.0 collective-permute-done.5.rest_1_
  14.0 0.8 %x_sweep.1 = f32[4,64,128]{2,1,0:T(8,128)} custom-call(f32[4,64,128]{2,1,0:T(8,128)S(1)} %get-tuple-element.49.g_ref, f32[4,64,128]{2,1,0:T(8,128)S(1)} %copy-done, f32[4,64,128]{2,1,0:T(8,128)S(1)} %copy-done.1, f32[4,64,128]{2,1,0:T(8,128)S(1)} %get-tuple-element.50.ready, f32[2,64,128]{2,1,0:T(8,128)S(1)} %get-tuple-element.51.own_ref, ...), custom_call_target="tpu_custom_call" | custom-call | bytes 1048576 | tf_op jit(solution)/shard_map/x_sweep/pallas_call | solution.py:385
Async XLA Ops:
  0.0 3.5 %copy-start.2 = (f32[4,64,128]{2,1,0:T(8,128)S(1)}, f32[4,64,128]{2,1,0:T(8,128)}, u32[]{:S(2)}) copy-start(f32[4,64,128]{2,1,0:T(8,128)} %ay.5) | copy-start | bytes 393220
  0.0 3.5 %copy-start.3 = (f32[4,64,128]{2,1,0:T(8,128)S(1)}, f32[4,64,128]{2,1,0:T(8,128)}, u32[]{:S(2)}) copy-start(f32[4,64,128]{2,1,0:T(8,128)} %cy.5) | copy-start | bytes 393220
  1.4 2.7 %collective-permute-start = (f32[16,128]{1,0:T(8,128)S(1)}, f32[16,128]{1,0:T(8,128)S(1)}, u32[]{:S(2)}, u32[]{:S(2)}) collective-permute-start(f32[16,128]{1,0:T(8,128)S(1)} %get-tuple-element.38), channel_id=1, source_target_pairs={{0,1},{1,0},{2,10},{3,11},{4,5},{5,4},{6,14},{7,15},{8,9},{9,8},{1... | collective-permute-start | bytes 24584 | tf_op jit(solution)/shard_map/ppermute | solution.py:404
  2.1 2.5 %collective-permute-start.1 = (f32[16,128]{1,0:T(8,128)S(1)}, f32[16,128]{1,0:T(8,128)S(1)}, u32[]{:S(2)}, u32[]{:S(2)}) collective-permute-start(f32[16,128]{1,0:T(8,128)S(1)} %get-tuple-element.39), channel_id=1, source_target_pairs={{0,8},{1,2},{2,1},{3,11},{4,12},{5,6},{6,5},{7,15},{8,0},{9,10},{1... | collective-permute-start | bytes 24584 | tf_op jit(solution)/shard_map/ppermute | solution.py:404
  2.1 2.5 %collective-permute-start.2 = (f32[16,128]{1,0:T(8,128)S(1)}, f32[16,128]{1,0:T(8,128)S(1)}, u32[]{:S(2)}, u32[]{:S(2)}) collective-permute-start(f32[16,128]{1,0:T(8,128)S(1)} %get-tuple-element.40), channel_id=1, source_target_pairs={{0,8},{1,9},{2,3},{3,2},{4,12},{5,13},{6,7},{7,6},{8,0},{9,1},{10,... | collective-permute-start | bytes 24584 | tf_op jit(solution)/shard_map/ppermute | solution.py:404
  3.6 1.0 %copy-start = (f32[4,64,128]{2,1,0:T(8,128)S(1)}, f32[4,64,128]{2,1,0:T(8,128)}, u32[]{:S(2)}) copy-start(f32[4,64,128]{2,1,0:T(8,128)} %ax.7) | copy-start | bytes 393220
  3.6 1.0 %copy-start.1 = (f32[4,64,128]{2,1,0:T(8,128)S(1)}, f32[4,64,128]{2,1,0:T(8,128)}, u32[]{:S(2)}) copy-start(f32[4,64,128]{2,1,0:T(8,128)} %cx.9) | copy-start | bytes 393220
  4.9 4.4 %collective-permute-start.3 = (f32[4,8,128]{2,1,0:T(8,128)S(1)}, f32[4,8,128]{2,1,0:T(8,128)S(1)}, u32[]{:S(2)}, u32[]{:S(2)}) collective-permute-start(f32[4,8,128]{2,1,0:T(8,128)S(1)} %get-tuple-element.48), channel_id=1, source_target_pairs={{0,4},{1,5},{2,6},{3,7},{4,0},{5,1},{6,2},{7,3},{8,12},{9,13},{10,... | collective-permute-start | bytes 49160 | tf_op jit(solution)/shard_map/ppermute | solution.py:404
  5.4 8.5 %collective-permute-start.4 = (f32[288,128]{1,0:T(8,128)S(1)}, f32[288,128]{1,0:T(8,128)S(1)}, u32[]{:S(2)}, u32[]{:S(2)}) collective-permute-start(f32[288,128]{1,0:T(8,128)S(1)} %get-tuple-element.53), channel_id=1, source_target_pairs={{0,4},{1,5},{2,6},{3,7},{4,0},{5,1},{6,2},{7,3},{8,16},{9,17},{10,... | collective-permute-start | bytes 442376 | tf_op jit(solution)/shard_map/ppermute | solution.py:404
  8.9 5.1 %collective-permute-start.5 = (f32[288,128]{1,0:T(8,128)S(1)}, f32[288,128]{1,0:T(8,128)S(1)}, u32[]{:S(2)}, u32[]{:S(2)}) collective-permute-start(f32[288,128]{1,0:T(8,128)S(1)} %get-tuple-element.54), channel_id=1, source_target_pairs={{0,8},{1,9},{2,10},{3,11},{4,12},{5,13},{6,14},{7,15},{8,0},{9,1},... | collective-permute-start | bytes 442376 | tf_op jit(solution)/shard_map/ppermute | solution.py:404
  9.4 4.6 %collective-permute-start.6 = (f32[48,128]{1,0:T(8,128)S(1)}, f32[48,128]{1,0:T(8,128)S(1)}, u32[]{:S(2)}, u32[]{:S(2)}) collective-permute-start(f32[48,128]{1,0:T(8,128)S(1)} %get-tuple-element.55), channel_id=1, source_target_pairs={{0,24},{1,25},{2,26},{3,27},{4,28},{5,29},{6,30},{7,31},{8,16},{9,... | collective-permute-start | bytes 73736 | tf_op jit(solution)/shard_map/ppermute | solution.py:404
  12.0 2.0 %collective-permute-start.7 = (f32[48,128]{1,0:T(8,128)S(1)}, f32[48,128]{1,0:T(8,128)S(1)}, u32[]{:S(2)}, u32[]{:S(2)}) collective-permute-start(f32[48,128]{1,0:T(8,128)S(1)} %get-tuple-element.56), channel_id=1, source_target_pairs={{0,8},{1,9},{2,10},{3,11},{4,12},{5,13},{6,14},{7,15},{8,0},{9,1},... | collective-permute-start | bytes 73736 | tf_op jit(solution)/shard_map/ppermute | solution.py:404

commit v6 on v5

--- a/solution.py
+++ b/solution.py
@@ -143,26 +143,23 @@
     step = rows // per
     at, place = edge_lanes((rows, lanes), lanes)
     near = (at < 2) | (at >= lanes - 2)
-    totals = [None] * 3
+    totals = [None] * 2
     for x in range(planes):
         for copy in itertools.chain(*({0: copies[:2], 2: copies[2:]}.get(x, []))):
             copy.wait()
         w = cot[x] * opened[x].astype(jnp.float32)
         w_ref[x] = w
-        for n, field in enumerate((w, a_ref[x], c_ref[x])):
+        for n, field, lane in ((0, w, 2), (0, a_ref[x], 6), (1, c_ref[x], 4)):
             field = jnp.where(near, field, 0.0)
             for r in range(per):
-                move = slot * (x + planes * r)
                 part = field[r * step : (r + 1) * step]
-                part = pltpu.roll(part, move, 1) if move else part
+                part = pltpu.roll(part, (slot * (x + planes * r) + lane) % lanes, 1)
                 totals[n] = part if totals[n] is None else totals[n] + part
-    for n in range(3):
+    for n in range(2):
         edge_ref[n] = totals[n]
     _, place = edge_lanes((step, lanes), lanes)
-    ends = [jnp.where(place >= slot - 2, total, 0.0) for total in totals]
-    starts = [jnp.where(place < 2, total, 0.0) for total in totals]
-    up = sum(pltpu.roll(end, 2 + 2 * n, 1) for n, end in enumerate(ends))
-    down = sum(pltpu.roll(start, 2 * n, 1) if n else start for n, start in enumerate(starts))
+    up = jnp.where(lax.rem(place, 4) < 2, totals[0], jnp.where(place < 4, totals[1], 0.0))
+    down = jnp.where(lax.rem(place, 4) >= 2, totals[0], jnp.where(place >= 4, totals[1], 0.0))
     for ref, message in zip(out, to_send(sizes, 2, up, down)):
         ref[...] = message
 
@@ -179,24 +176,36 @@
 
 
 def z_ends(edges, low, high, lanes):
-    shift = lambda value, by: pltpu.roll(value, by % lanes, 1)
-    w, a, c = edges
-    _, place = edge_lanes(w.shape, lanes)
-    low = [shift(low, -v) if v else low for v in range(6)]
-    first, second = low_end(low, w, shift(w, -1), a, shift(a, -1), c)
-    high = [shift(high, -v) if v else high for v in range(5)]
+    lane = lambda value, at: pltpu.roll(value, lanes - at, 1) if at else value
+    wa, c = edges
+    w_far, w_low, c_far, c_low, a_far, a_low = (lane(low, at) for at in range(6))
+    first, second = low_end(
+        (w_far, w_low, a_far, a_low, c_far, c_low),
+        *(lane(wa, at) for at in (2, 3, 6, 7)),
+        lane(c, 4),
+    )
+    w_high, w_far, c_high, a_high, a_far = (lane(high, at) for at in (2, 3, 4, 6, 7))
     last, before = high_end(
-        high, shift(w, 2), shift(w, 1), shift(a, 2), shift(a, 1), shift(c, 2), shift(c, 1)
-    )
-    ends = jnp.where(place == 0, first, jnp.where(place == 1, shift(second, 1), 0.0))
-    return jnp.where(
-        place == slot - 1, shift(last, -1), jnp.where(place == slot - 2, shift(before, -2), ends)
-    )
-
-
-def spread(ends, x, r, planes, lanes):
-    move = slot * (x + planes * r)
-    return pltpu.roll(ends, lanes - move, 1) if move else ends
+        (w_high, w_far, a_high, a_far, c_high),
+        *(lane(wa, at) for at in (0, 1, 4, 5)),
+        *(lane(c, at) for at in (2, 3)),
+    )
+    return first, second, last, before
+
+
+columns = (0, 1, -1, -2)
+
+
+def spread(ends, x, r, planes, lanes, column=0):
+    move = (column - slot * (x + planes * r)) % lanes
+    return pltpu.roll(ends, move, 1) if move else ends
+
+
+def on_columns(at, lanes, values):
+    total = 0.0
+    for column, value in zip(columns, values):
+        total = jnp.where(at == column % lanes, value, total)
+    return total
 
 
 def z_sweep(sizes, partial, edges, opened, ay, cy, ax, cx, _, *rest):
@@ -206,26 +215,27 @@
     per = fold(planes, rows, lanes)
     step = rows // per
     low, high = received(sizes, 2, messages, edges[0])
-    ends = z_ends([edges[n] for n in range(3)], low, high, lanes)
-    ends_ref[...] = ends
+    ends = z_ends([edges[0], edges[1]], low, high, lanes)
+    _, place = edge_lanes((step, lanes), lanes)
+    ends_ref[...] = on_columns(
+        place, slot, [spread(end, 0, 0, planes, lanes, column) for end, column in zip(ends, columns)]
+    )
     if not out:
         return
     at = lax.broadcasted_iota(jnp.int32, (8, lanes), 1)
-    near = (at < 2) | (at >= lanes - 2)
     tile = lax.broadcasted_iota(jnp.int32, (8, lanes), 0)
-    pick = lambda *tiles: jnp.where(tile < 2, tiles[0], jnp.where(tile < 4, tiles[1], tiles[2]))
     for x in range(planes):
         ws = []
-        for rim, group, r in ((slice(0, 8), ends[:8], 0), (slice(rows - 8, rows), ends[step - 8 :], per - 1)):
-            g = partial[x, rim] + jnp.where(near, spread(group, x, r, planes, lanes), 0.0)
+        for rim, group, r in ((slice(0, 8), slice(0, 8), 0), (slice(rows - 8, rows), slice(step - 8, step), per - 1)):
+            added = [
+                spread(end[group], x, r, planes, lanes, column) for end, column in zip(ends, columns)
+            ]
+            g = partial[x, rim] + on_columns(at, lanes, added)
             ws.append(opened[x, rim].astype(jnp.float32) * g)
-        up = pick(
-            *(
-                pltpu.roll(field, by, 0)
-                for field, by in ((ws[1], 2), (ay[x, rows - 8 :], 4), (cy[x, rows - 8 :], 6))
-            )
-        )
-        down = pick(ws[0], pltpu.roll(ay[x, :8], 2, 0), pltpu.roll(cy[x, :8], 4, 0))
+        a, c = (pltpu.roll(ref[x, rows - 8 :], by, 0) for ref, by in ((ay, 6), (cy, 4)))
+        up = jnp.where(tile >= 6, ws[1], jnp.where(tile >= 4, a, c))
+        a, c = (pltpu.roll(ref[x, :8], by, 0) for ref, by in ((ay, 2), (cy, 4)))
+        down = jnp.where(tile < 2, ws[0], jnp.where(tile < 4, a, c))
         for ref, message in zip(out, to_send(sizes, 1, up, down)):
             ref[x] = message
 
@@ -278,7 +288,7 @@
         low, high = received(sizes, 1, [m[x] for m in messages], ay[x, :8])
         row = lambda ref, n: ref[x, n : n + 1]
         first, second = low_end(
-            [low[v : v + 1] for v in range(6)],
+            [low[v : v + 1] for v in (6, 7, 4, 5, 2, 3)],
             *(row(ref, n) for ref, n in ((w_rims, 0), (w_rims, 1), (ay, 0), (ay, 1), (cy, 0))),
         )
         last, before = high_end(
@@ -406,7 +416,7 @@
     dma = pltpu.SemaphoreType.DMA
     cot, opened, az, cz, w, edges, *z_out = call(
         functools.partial(z_pack, sizes, planes, rows, lanes),
-        [block, jax.ShapeDtypeStruct(block, jnp.int32), block, block, block, (3, *packed)]
+        [block, jax.ShapeDtypeStruct(block, jnp.int32), block, block, block, (2, *packed)]
         + [packed] * len(z_rounds),
         loads=(cot, opened, az, cz),
         name="z_pack", scratch=[dma((4, planes))],

time: 14.9 us -> 14.8 us (level)
  no operation moved by 1% of the time
where the time goes in v6:
time: 14.8 us; the launch traced here: 14.7 us
  starting transfers between devices  8.88 us (60%)
  Pallas kernels  3.26 us (22%)
  waiting for transfers between devices  2.44 us (16%)
    ppermute x8, starting transfers between devices, per_device(): swap = lambda value, perm: lax.ppermute(value, AXES, perm)  8.88 us
    pallas_call x8, Pallas kernels, call(): pl.pallas_call(body, out_shape=shapes, in_specs=[pl.BlockSpec(memory_spac...  3.26 us
    ppermute x8, waiting for transfers between devices, per_device(): swap = lambda value, perm: lax.ppermute(value, AXES, perm)  2.44 us
  transfers between devices with their start and end apart: 8, of which 2 were waited for; matrix products, arithmetic and copies ran while one was open for 0% of the time, Pallas kernels for 6%

profile of v6, /device:TPU:21, one launch (start us, length us, event | category | flops | bytes accessed | tf_op | source)
XLA Modules:
  0.0 14.7 jit_solution(12191166009393023002)
XLA Ops:
  0.0 0.0 copy-start.2
  0.0 0.0 copy-start.3
  0.0 1.3 %z_pack.1 = (f32[4,64,128]{2,1,0:T(8,128)S(1)}, s32[4,64,128]{2,1,0:T(8,128)S(1)}, f32[4,64,128]{2,1,0:T(8,128)S(1)}, f32[4,64,128]{2,1,0:T(8,128)S(1)}, f32[4,6...) custom-call(f32[4,64,128]{2,1,0:T(8,128)} %refs_0_.1, ...), custom_call_target="tpu_custom_call" | custom-call | bytes 1048576 | tf_op jit(solution)/shard_map/z_pack/pallas_call | solution.py:395
  1.3 0.7 %collective-permute-start = (f32[16,128]{1,0:T(8,128)S(1)}, f32[16,128]{1,0:T(8,128)S(1)}, u32[]{:S(2)}, u32[]{:S(2)}) collective-permute-start(f32[16,128]{1,0:T(8,128)S(1)} %get-tuple-element.38), channel_id=1, source_target_pairs={{0,1},{1,0},{2,10},{3,11},{4,5},{5,4},{6,14},{7,15},{8,9},{9,8},{1... | collective-permute-start | bytes 24584 | tf_op jit(solution)/shard_map/ppermute | solution.py:414
  2.1 0.0 collective-permute-start.1
  2.1 1.4 %collective-permute-start.2 = (f32[16,128]{1,0:T(8,128)S(1)}, f32[16,128]{1,0:T(8,128)S(1)}, u32[]{:S(2)}, u32[]{:S(2)}) collective-permute-start(f32[16,128]{1,0:T(8,128)S(1)} %get-tuple-element.40), channel_id=1, source_target_pairs={{0,8},{1,9},{2,3},{3,2},{4,12},{5,13},{6,7},{7,6},{8,0},{9,1},{10,... | collective-permute-start | bytes 24584 | tf_op jit(solution)/shard_map/ppermute | solution.py:414
  3.4 0.0 copy-done.2
  3.4 0.0 copy-done.3
  3.4 0.1 y_factors.1
  3.5 0.0 copy-start
  3.6 0.0 copy-start.1
  3.6 0.5 %z_inner.1.partial.partial_z = f32[4,64,128]{2,1,0:T(8,128)S(1)} custom-call(f32[4,64,128]{2,1,0:T(8,128)S(1)} %get-tuple-element.31.g_ref, f32[4,64,128]{2,1,0:T(8,128)S(1)} %get-tuple-element.32.w_ref, f32[4,64,128]{2,1,0:T(8,128)S(1)} %get-tuple-element.33.a_ref, f32[4,64,128]{2,1,0:T(8,128)S(1)} %get-tuple-element.34.c_ref), custom_call_target="tpu_custom_call" | custom-call | bytes 1048576 | tf_op jit(solution)/shard_map/z_inner/pallas_call | solution.py:395
  4.0 0.0 collective-permute-done.rest_0_
  4.0 0.5 %collective-permute-done.1.rest_1_ = f32[16,128]{1,0:T(8,128)S(1)} collective-permute-done((f32[16,128]{1,0:T(8,128)S(1)}, f32[16,128]{1,0:T(8,128)S(1)}, u32[]{:S(2)}, u32[]{:S(2)}) %collective-permute-start.1) | collective-permute-done | bytes 8224 | tf_op jit(solution)/shard_map/ppermute | solution.py:414
  4.6 0.0 collective-permute-done.2.rest_2_
  4.6 0.0 copy-done
  4.6 0.0 copy-done.1
  4.6 0.2 %z_sweep.1 = (f32[16,128]{1,0:T(8,128)S(1)}, f32[4,8,128]{2,1,0:T(8,128)S(1)}) custom-call(f32[4,64,128]{2,1,0:T(8,128)S(1)} %z_inner.1.partial.partial_z, f32[2,16,128]{2,1,0:T(8,128)S(1)} %get-tuple-element.35.edges, s32[4,64,128]{2,1,0:T(8,128)S(1)} %get-tuple-element.36.opened, f32[4,64,128]{2,1,0:T(8,128)S(1)} %copy-done.2, ...), custom_call_target="tpu_custom_call" | custom-call | bytes 1048576 | tf_op jit(solution)/shard_map/z_sweep/pallas_call | solution.py:395
  4.8 0.3 %collective-permute-start.3 = (f32[4,8,128]{2,1,0:T(8,128)S(1)}, f32[4,8,128]{2,1,0:T(8,128)S(1)}, u32[]{:S(2)}, u32[]{:S(2)}) collective-permute-start(f32[4,8,128]{2,1,0:T(8,128)S(1)} %get-tuple-element.48), channel_id=1, source_target_pairs={{0,4},{1,5},{2,6},{3,7},{4,0},{5,1},{6,2},{7,3},{8,12},{9,13},{10,... | collective-permute-start | bytes 49160 | tf_op jit(solution)/shard_map/ppermute | solution.py:414
  5.1 0.2 %y_inner.1 = (f32[4,64,128]{2,1,0:T(8,128)S(1)}, f32[4,8,128]{2,1,0:T(8,128)S(1)}, f32[288,128]{1,0:T(8,128)S(1)}, f32[288,128]{1,0:T(8,128)S(1)}) custom-call(f32[4,64,128]{2,1,0:T(8,128)S(1)} %z_inner.1.partial.partial_z, f32[16,128]{1,0:T(8,128)S(1)} %get-tuple-element.41.ends_ref, s32[4,64,128]{2,1,0:T(8,128)S(1)} %get-tuple-element.36.opened, ...), custom_call_target="tpu_custom_call" | custom-call | bytes 1048576 | tf_op jit(solution)/shard_map/y_inner/pallas_call | solution.py:395
  5.3 3.5 %collective-permute-start.4 = (f32[288,128]{1,0:T(8,128)S(1)}, f32[288,128]{1,0:T(8,128)S(1)}, u32[]{:S(2)}, u32[]{:S(2)}) collective-permute-start(f32[288,128]{1,0:T(8,128)S(1)} %get-tuple-element.53), channel_id=1, source_target_pairs={{0,4},{1,5},{2,6},{3,7},{4,0},{5,1},{6,2},{7,3},{8,16},{9,17},{10,... | collective-permute-start | bytes 442376 | tf_op jit(solution)/shard_map/ppermute | solution.py:414
  8.8 0.4 %collective-permute-start.5 = (f32[288,128]{1,0:T(8,128)S(1)}, f32[288,128]{1,0:T(8,128)S(1)}, u32[]{:S(2)}, u32[]{:S(2)}) collective-permute-start(f32[288,128]{1,0:T(8,128)S(1)} %get-tuple-element.54), channel_id=1, source_target_pairs={{0,8},{1,9},{2,10},{3,11},{4,12},{5,13},{6,14},{7,15},{8,0},{9,1},... | collective-permute-start | bytes 442376 | tf_op jit(solution)/shard_map/ppermute | solution.py:414
  9.2 0.0 collective-permute-done.3.rest_0_
  9.2 0.1 y_sweep.1
  9.3 2.6 %collective-permute-start.6 = (f32[48,128]{1,0:T(8,128)S(1)}, f32[48,128]{1,0:T(8,128)S(1)}, u32[]{:S(2)}, u32[]{:S(2)}) collective-permute-start(f32[48,128]{1,0:T(8,128)S(1)} %get-tuple-element.55), channel_id=1, source_target_pairs={{0,24},{1,25},{2,26},{3,27},{4,28},{5,29},{6,30},{7,31},{8,16},{9,... | collective-permute-start | bytes 73736 | tf_op jit(solution)/shard_map/ppermute | solution.py:414
  11.9 0.0 collective-permute-start.7
  11.9 0.1 x_inner.1
  12.0 1.9 %collective-permute-done.6.rest_2_ = f32[48,128]{1,0:T(8,128)S(1)} collective-permute-done((f32[48,128]{1,0:T(8,128)S(1)}, f32[48,128]{1,0:T(8,128)S(1)}, u32[]{:S(2)}, u32[]{:S(2)}) %collective-permute-start.6) | collective-permute-done | bytes 24608 | tf_op jit(solution)/shard_map/ppermute | solution.py:414
  13.9 0.0 collective-permute-done.7.rest_3_
  13.9 0.0 collective-permute-done.4.rest_0_
  13.9 0.0 collective-permute-done.5.rest_1_
  13.9 0.8 %x_sweep.1 = f32[4,64,128]{2,1,0:T(8,128)} custom-call(f32[4,64,128]{2,1,0:T(8,128)S(1)} %get-tuple-element.49.g_ref, f32[4,64,128]{2,1,0:T(8,128)S(1)} %copy-done, f32[4,64,128]{2,1,0:T(8,128)S(1)} %copy-done.1, f32[4,64,128]{2,1,0:T(8,128)S(1)} %get-tuple-element.50.ready, f32[2,64,128]{2,1,0:T(8,128)S(1)} %get-tuple-element.51.own_ref, ...), custom_call_target="tpu_custom_call" | custom-call | bytes 1048576 | tf_op jit(solution)/shard_map/x_sweep/pallas_call | solution.py:395
Async XLA Ops:
  0.0 3.4 %copy-start.2 = (f32[4,64,128]{2,1,0:T(8,128)S(1)}, f32[4,64,128]{2,1,0:T(8,128)}, u32[]{:S(2)}) copy-start(f32[4,64,128]{2,1,0:T(8,128)} %ay.5) | copy-start | bytes 393220
  0.0 3.4 %copy-start.3 = (f32[4,64,128]{2,1,0:T(8,128)S(1)}, f32[4,64,128]{2,1,0:T(8,128)}, u32[]{:S(2)}) copy-start(f32[4,64,128]{2,1,0:T(8,128)} %cy.5) | copy-start | bytes 393220
  1.3 2.7 %collective-permute-start = (f32[16,128]{1,0:T(8,128)S(1)}, f32[16,128]{1,0:T(8,128)S(1)}, u32[]{:S(2)}, u32[]{:S(2)}) collective-permute-start(f32[16,128]{1,0:T(8,128)S(1)} %get-tuple-element.38), channel_id=1, source_target_pairs={{0,1},{1,0},{2,10},{3,11},{4,5},{5,4},{6,14},{7,15},{8,9},{9,8},{1... | collective-permute-start | bytes 24584 | tf_op jit(solution)/shard_map/ppermute | solution.py:414
  2.1 2.5 %collective-permute-start.1 = (f32[16,128]{1,0:T(8,128)S(1)}, f32[16,128]{1,0:T(8,128)S(1)}, u32[]{:S(2)}, u32[]{:S(2)}) collective-permute-start(f32[16,128]{1,0:T(8,128)S(1)} %get-tuple-element.39), channel_id=1, source_target_pairs={{0,8},{1,2},{2,1},{3,11},{4,12},{5,6},{6,5},{7,15},{8,0},{9,10},{1... | collective-permute-start | bytes 24584 | tf_op jit(solution)/shard_map/ppermute | solution.py:414
  2.1 2.5 %collective-permute-start.2 = (f32[16,128]{1,0:T(8,128)S(1)}, f32[16,128]{1,0:T(8,128)S(1)}, u32[]{:S(2)}, u32[]{:S(2)}) collective-permute-start(f32[16,128]{1,0:T(8,128)S(1)} %get-tuple-element.40), channel_id=1, source_target_pairs={{0,8},{1,9},{2,3},{3,2},{4,12},{5,13},{6,7},{7,6},{8,0},{9,1},{10,... | collective-permute-start | bytes 24584 | tf_op jit(solution)/shard_map/ppermute | solution.py:414
  3.5 1.0 %copy-start = (f32[4,64,128]{2,1,0:T(8,128)S(1)}, f32[4,64,128]{2,1,0:T(8,128)}, u32[]{:S(2)}) copy-start(f32[4,64,128]{2,1,0:T(8,128)} %ax.7) | copy-start | bytes 393220
  3.6 1.0 %copy-start.1 = (f32[4,64,128]{2,1,0:T(8,128)S(1)}, f32[4,64,128]{2,1,0:T(8,128)}, u32[]{:S(2)}) copy-start(f32[4,64,128]{2,1,0:T(8,128)} %cx.9) | copy-start | bytes 393220
  4.8 4.4 %collective-permute-start.3 = (f32[4,8,128]{2,1,0:T(8,128)S(1)}, f32[4,8,128]{2,1,0:T(8,128)S(1)}, u32[]{:S(2)}, u32[]{:S(2)}) collective-permute-start(f32[4,8,128]{2,1,0:T(8,128)S(1)} %get-tuple-element.48), channel_id=1, source_target_pairs={{0,4},{1,5},{2,6},{3,7},{4,0},{5,1},{6,2},{7,3},{8,12},{9,13},{10,... | collective-permute-start | bytes 49160 | tf_op jit(solution)/shard_map/ppermute | solution.py:414
  5.3 8.5 %collective-permute-start.4 = (f32[288,128]{1,0:T(8,128)S(1)}, f32[288,128]{1,0:T(8,128)S(1)}, u32[]{:S(2)}, u32[]{:S(2)}) collective-permute-start(f32[288,128]{1,0:T(8,128)S(1)} %get-tuple-element.53), channel_id=1, source_target_pairs={{0,4},{1,5},{2,6},{3,7},{4,0},{5,1},{6,2},{7,3},{8,16},{9,17},{10,... | collective-permute-start | bytes 442376 | tf_op jit(solution)/shard_map/ppermute | solution.py:414
  8.8 5.1 %collective-permute-start.5 = (f32[288,128]{1,0:T(8,128)S(1)}, f32[288,128]{1,0:T(8,128)S(1)}, u32[]{:S(2)}, u32[]{:S(2)}) collective-permute-start(f32[288,128]{1,0:T(8,128)S(1)} %get-tuple-element.54), channel_id=1, source_target_pairs={{0,8},{1,9},{2,10},{3,11},{4,12},{5,13},{6,14},{7,15},{8,0},{9,1},... | collective-permute-start | bytes 442376 | tf_op jit(solution)/shard_map/ppermute | solution.py:414
  9.3 4.6 %collective-permute-start.6 = (f32[48,128]{1,0:T(8,128)S(1)}, f32[48,128]{1,0:T(8,128)S(1)}, u32[]{:S(2)}, u32[]{:S(2)}) collective-permute-start(f32[48,128]{1,0:T(8,128)S(1)} %get-tuple-element.55), channel_id=1, source_target_pairs={{0,24},{1,25},{2,26},{3,27},{4,28},{5,29},{6,30},{7,31},{8,16},{9,... | collective-permute-start | bytes 73736 | tf_op jit(solution)/shard_map/ppermute | solution.py:414
  11.9 2.0 %collective-permute-start.7 = (f32[48,128]{1,0:T(8,128)S(1)}, f32[48,128]{1,0:T(8,128)S(1)}, u32[]{:S(2)}, u32[]{:S(2)}) collective-permute-start(f32[48,128]{1,0:T(8,128)S(1)} %get-tuple-element.56), channel_id=1, source_target_pairs={{0,8},{1,9},{2,10},{3,11},{4,12},{5,13},{6,14},{7,15},{8,0},{9,1},... | collective-permute-start | bytes 73736 | tf_op jit(solution)/shard_map/ppermute | solution.py:414

commit v7 on v6

--- a/solution.py
+++ b/solution.py
@@ -247,6 +247,10 @@
     return (w[-1], w[0]), (back, forth)
 
 
+def early_rows(rows):
+    return rows * 5 // 64 * 8
+
+
 def y_inner(sizes, partial_z, ends_ref, opened, ax, cx, *rest):
     parts_y, (partial, w_rims, *out) = rest[:5], rest[5:]
     planes, rows, lanes = ax.shape
@@ -273,7 +277,7 @@
     for v, (up, down) in enumerate(pairs):
         for ref, message in zip(out, to_send(sizes, 0, up, down)):
             ref[v * rows : (v + 1) * rows] = message
-    half = slice(0, rows // 2)
+    half = slice(0, early_rows(rows))
     for ref, message in zip(out, to_send(sizes, 0, cx[planes - 1, half], cx[0, half])):
         ref[4 * rows :] = message
 
@@ -311,7 +315,7 @@
         for v, (up, down) in enumerate(x_products(ws, c)):
             for ref, message in zip(out, to_send(sizes, 0, up, down)):
                 ref[8 * v : 8 * v + 8] = message
-        half = slice(rows // 2, rows)
+        half = slice(early_rows(rows), rows)
         for ref, message in zip(out, to_send(sizes, 0, cx[planes - 1, half], cx[0, half])):
             ref[16:] = message
 
@@ -433,14 +437,14 @@
     y_in = [swap(m, p) for m, p in zip(y_out, y_rounds)]
     partial, w_rims, *x_out = call(
         functools.partial(y_inner, sizes),
-        [block, (planes, 8, lanes)] + [(4 * rows + rows // 2, lanes)] * len(x_rounds),
+        [block, (planes, 8, lanes)] + [(4 * rows + early_rows(rows), lanes)] * len(x_rounds),
         partial, ends, opened, ax, cx, *parts_y,
         name="y_inner",
     )
     x_early = [swap(m, p) for m, p in zip(x_out, early_rounds)]
     g, *x_out = call(
         functools.partial(y_sweep, sizes),
-        [block] + [(16 + rows // 2, lanes)] * len(x_rounds),
+        [block] + [(16 + rows - early_rows(rows), lanes)] * len(x_rounds),
         partial, w_rims, opened, ay, cy, cx, *y_in,
         name="y_sweep", flops=10**10,
     )

time: 14.8 us -> 14.7 us (level)
  no operation moved by 1% of the time
where the time goes in v7:
time: 14.7 us; the launch traced here: 14.6 us
  starting transfers between devices  8.88 us (60%)
  Pallas kernels  3.25 us (22%)
  waiting for transfers between devices  2.36 us (16%)
    ppermute x8, starting transfers between devices, per_device(): swap = lambda value, perm: lax.ppermute(value, AXES, perm)  8.88 us
    pallas_call x8, Pallas kernels, call(): pl.pallas_call(body, out_shape=shapes, in_specs=[pl.BlockSpec(memory_spac...  3.25 us
    ppermute x8, waiting for transfers between devices, per_device(): swap = lambda value, perm: lax.ppermute(value, AXES, perm)  2.36 us
  transfers between devices with their start and end apart: 8, of which 2 were waited for; matrix products, arithmetic and copies ran while one was open for 0% of the time, Pallas kernels for 6%

profile of v7, /device:TPU:21, one launch (start us, length us, event | category | flops | bytes accessed | tf_op | source)
XLA Modules:
  0.0 14.6 jit_solution(9272648706192535843)
XLA Ops:
  0.0 0.0 copy-start.2
  0.0 0.0 copy-start.3
  0.0 1.3 %z_pack.1 = (f32[4,64,128]{2,1,0:T(8,128)S(1)}, s32[4,64,128]{2,1,0:T(8,128)S(1)}, f32[4,64,128]{2,1,0:T(8,128)S(1)}, f32[4,64,128]{2,1,0:T(8,128)S(1)}, f32[4,6...) custom-call(f32[4,64,128]{2,1,0:T(8,128)} %refs_0_.1, ...), custom_call_target="tpu_custom_call" | custom-call | bytes 1048576 | tf_op jit(solution)/shard_map/z_pack/pallas_call | solution.py:399
  1.3 0.7 %collective-permute-start = (f32[16,128]{1,0:T(8,128)S(1)}, f32[16,128]{1,0:T(8,128)S(1)}, u32[]{:S(2)}, u32[]{:S(2)}) collective-permute-start(f32[16,128]{1,0:T(8,128)S(1)} %get-tuple-element.38), channel_id=1, source_target_pairs={{0,1},{1,0},{2,10},{3,11},{4,5},{5,4},{6,14},{7,15},{8,9},{9,8},{1... | collective-permute-start | bytes 24584 | tf_op jit(solution)/shard_map/ppermute | solution.py:418
  2.1 0.0 collective-permute-start.1
  2.1 1.4 %collective-permute-start.2 = (f32[16,128]{1,0:T(8,128)S(1)}, f32[16,128]{1,0:T(8,128)S(1)}, u32[]{:S(2)}, u32[]{:S(2)}) collective-permute-start(f32[16,128]{1,0:T(8,128)S(1)} %get-tuple-element.40), channel_id=1, source_target_pairs={{0,8},{1,9},{2,3},{3,2},{4,12},{5,13},{6,7},{7,6},{8,0},{9,1},{10,... | collective-permute-start | bytes 24584 | tf_op jit(solution)/shard_map/ppermute | solution.py:418
  3.4 0.0 copy-done.2
  3.4 0.0 copy-done.3
  3.4 0.1 y_factors.1
  3.5 0.0 copy-start
  3.6 0.0 copy-start.1
  3.6 0.5 %z_inner.1.partial.partial_z = f32[4,64,128]{2,1,0:T(8,128)S(1)} custom-call(f32[4,64,128]{2,1,0:T(8,128)S(1)} %get-tuple-element.31.g_ref, f32[4,64,128]{2,1,0:T(8,128)S(1)} %get-tuple-element.32.w_ref, f32[4,64,128]{2,1,0:T(8,128)S(1)} %get-tuple-element.33.a_ref, f32[4,64,128]{2,1,0:T(8,128)S(1)} %get-tuple-element.34.c_ref), custom_call_target="tpu_custom_call" | custom-call | bytes 1048576 | tf_op jit(solution)/shard_map/z_inner/pallas_call | solution.py:399
  4.0 0.0 collective-permute-done.rest_0_
  4.0 0.5 %collective-permute-done.1.rest_1_ = f32[16,128]{1,0:T(8,128)S(1)} collective-permute-done((f32[16,128]{1,0:T(8,128)S(1)}, f32[16,128]{1,0:T(8,128)S(1)}, u32[]{:S(2)}, u32[]{:S(2)}) %collective-permute-start.1) | collective-permute-done | bytes 8224 | tf_op jit(solution)/shard_map/ppermute | solution.py:418
  4.6 0.0 collective-permute-done.2.rest_2_
  4.6 0.0 copy-done
  4.6 0.0 copy-done.1
  4.6 0.2 %z_sweep.1 = (f32[16,128]{1,0:T(8,128)S(1)}, f32[4,8,128]{2,1,0:T(8,128)S(1)}) custom-call(f32[4,64,128]{2,1,0:T(8,128)S(1)} %z_inner.1.partial.partial_z, f32[2,16,128]{2,1,0:T(8,128)S(1)} %get-tuple-element.35.edges, s32[4,64,128]{2,1,0:T(8,128)S(1)} %get-tuple-element.36.opened, f32[4,64,128]{2,1,0:T(8,128)S(1)} %copy-done.2, ...), custom_call_target="tpu_custom_call" | custom-call | bytes 1048576 | tf_op jit(solution)/shard_map/z_sweep/pallas_call | solution.py:399
  4.8 0.3 %collective-permute-start.3 = (f32[4,8,128]{2,1,0:T(8,128)S(1)}, f32[4,8,128]{2,1,0:T(8,128)S(1)}, u32[]{:S(2)}, u32[]{:S(2)}) collective-permute-start(f32[4,8,128]{2,1,0:T(8,128)S(1)} %get-tuple-element.48), channel_id=1, source_target_pairs={{0,4},{1,5},{2,6},{3,7},{4,0},{5,1},{6,2},{7,3},{8,12},{9,13},{10,... | collective-permute-start | bytes 49160 | tf_op jit(solution)/shard_map/ppermute | solution.py:418
  5.1 0.2 %y_inner.1 = (f32[4,64,128]{2,1,0:T(8,128)S(1)}, f32[4,8,128]{2,1,0:T(8,128)S(1)}, f32[296,128]{1,0:T(8,128)S(1)}, f32[296,128]{1,0:T(8,128)S(1)}) custom-call(f32[4,64,128]{2,1,0:T(8,128)S(1)} %z_inner.1.partial.partial_z, f32[16,128]{1,0:T(8,128)S(1)} %get-tuple-element.41.ends_ref, s32[4,64,128]{2,1,0:T(8,128)S(1)} %get-tuple-element.36.opened, ...), custom_call_target="tpu_custom_call" | custom-call | bytes 1048576 | tf_op jit(solution)/shard_map/y_inner/pallas_call | solution.py:399
  5.3 3.5 %collective-permute-start.4 = (f32[296,128]{1,0:T(8,128)S(1)}, f32[296,128]{1,0:T(8,128)S(1)}, u32[]{:S(2)}, u32[]{:S(2)}) collective-permute-start(f32[296,128]{1,0:T(8,128)S(1)} %get-tuple-element.53), channel_id=1, source_target_pairs={{0,4},{1,5},{2,6},{3,7},{4,0},{5,1},{6,2},{7,3},{8,16},{9,17},{10,... | collective-permute-start | bytes 454664 | tf_op jit(solution)/shard_map/ppermute | solution.py:418
  8.8 0.4 %collective-permute-start.5 = (f32[296,128]{1,0:T(8,128)S(1)}, f32[296,128]{1,0:T(8,128)S(1)}, u32[]{:S(2)}, u32[]{:S(2)}) collective-permute-start(f32[296,128]{1,0:T(8,128)S(1)} %get-tuple-element.54), channel_id=1, source_target_pairs={{0,8},{1,9},{2,10},{3,11},{4,12},{5,13},{6,14},{7,15},{8,0},{9,1},... | collective-permute-start | bytes 454664 | tf_op jit(solution)/shard_map/ppermute | solution.py:418
  9.2 0.0 collective-permute-done.3.rest_0_
  9.2 0.1 y_sweep.1
  9.3 2.6 %collective-permute-start.6 = (f32[40,128]{1,0:T(8,128)S(1)}, f32[40,128]{1,0:T(8,128)S(1)}, u32[]{:S(2)}, u32[]{:S(2)}) collective-permute-start(f32[40,128]{1,0:T(8,128)S(1)} %get-tuple-element.55), channel_id=1, source_target_pairs={{0,24},{1,25},{2,26},{3,27},{4,28},{5,29},{6,30},{7,31},{8,16},{9,... | collective-permute-start | bytes 61448 | tf_op jit(solution)/shard_map/ppermute | solution.py:418
  11.9 0.0 collective-permute-start.7
  11.9 0.1 x_inner.1
  12.0 1.8 %collective-permute-done.6.rest_2_ = f32[40,128]{1,0:T(8,128)S(1)} collective-permute-done((f32[40,128]{1,0:T(8,128)S(1)}, f32[40,128]{1,0:T(8,128)S(1)}, u32[]{:S(2)}, u32[]{:S(2)}) %collective-permute-start.6) | collective-permute-done | bytes 20512 | tf_op jit(solution)/shard_map/ppermute | solution.py:418
  13.8 0.0 collective-permute-done.7.rest_3_
  13.8 0.0 collective-permute-done.4.rest_0_
  13.8 0.0 collective-permute-done.5.rest_1_
  13.8 0.8 %x_sweep.1 = f32[4,64,128]{2,1,0:T(8,128)} custom-call(f32[4,64,128]{2,1,0:T(8,128)S(1)} %get-tuple-element.49.g_ref, f32[4,64,128]{2,1,0:T(8,128)S(1)} %copy-done, f32[4,64,128]{2,1,0:T(8,128)S(1)} %copy-done.1, f32[4,64,128]{2,1,0:T(8,128)S(1)} %get-tuple-element.50.ready, f32[2,64,128]{2,1,0:T(8,128)S(1)} %get-tuple-element.51.own_ref, ...), custom_call_target="tpu_custom_call" | custom-call | bytes 1048576 | tf_op jit(solution)/shard_map/x_sweep/pallas_call | solution.py:399
Async XLA Ops:
  0.0 3.4 %copy-start.2 = (f32[4,64,128]{2,1,0:T(8,128)S(1)}, f32[4,64,128]{2,1,0:T(8,128)}, u32[]{:S(2)}) copy-start(f32[4,64,128]{2,1,0:T(8,128)} %ay.5) | copy-start | bytes 393220
  0.0 3.4 %copy-start.3 = (f32[4,64,128]{2,1,0:T(8,128)S(1)}, f32[4,64,128]{2,1,0:T(8,128)}, u32[]{:S(2)}) copy-start(f32[4,64,128]{2,1,0:T(8,128)} %cy.5) | copy-start | bytes 393220
  1.3 2.7 %collective-permute-start = (f32[16,128]{1,0:T(8,128)S(1)}, f32[16,128]{1,0:T(8,128)S(1)}, u32[]{:S(2)}, u32[]{:S(2)}) collective-permute-start(f32[16,128]{1,0:T(8,128)S(1)} %get-tuple-element.38), channel_id=1, source_target_pairs={{0,1},{1,0},{2,10},{3,11},{4,5},{5,4},{6,14},{7,15},{8,9},{9,8},{1... | collective-permute-start | bytes 24584 | tf_op jit(solution)/shard_map/ppermute | solution.py:418
  2.1 2.5 %collective-permute-start.1 = (f32[16,128]{1,0:T(8,128)S(1)}, f32[16,128]{1,0:T(8,128)S(1)}, u32[]{:S(2)}, u32[]{:S(2)}) collective-permute-start(f32[16,128]{1,0:T(8,128)S(1)} %get-tuple-element.39), channel_id=1, source_target_pairs={{0,8},{1,2},{2,1},{3,11},{4,12},{5,6},{6,5},{7,15},{8,0},{9,10},{1... | collective-permute-start | bytes 24584 | tf_op jit(solution)/shard_map/ppermute | solution.py:418
  2.1 2.5 %collective-permute-start.2 = (f32[16,128]{1,0:T(8,128)S(1)}, f32[16,128]{1,0:T(8,128)S(1)}, u32[]{:S(2)}, u32[]{:S(2)}) collective-permute-start(f32[16,128]{1,0:T(8,128)S(1)} %get-tuple-element.40), channel_id=1, source_target_pairs={{0,8},{1,9},{2,3},{3,2},{4,12},{5,13},{6,7},{7,6},{8,0},{9,1},{10,... | collective-permute-start | bytes 24584 | tf_op jit(solution)/shard_map/ppermute | solution.py:418
  3.5 1.0 %copy-start = (f32[4,64,128]{2,1,0:T(8,128)S(1)}, f32[4,64,128]{2,1,0:T(8,128)}, u32[]{:S(2)}) copy-start(f32[4,64,128]{2,1,0:T(8,128)} %ax.7) | copy-start | bytes 393220
  3.6 1.0 %copy-start.1 = (f32[4,64,128]{2,1,0:T(8,128)S(1)}, f32[4,64,128]{2,1,0:T(8,128)}, u32[]{:S(2)}) copy-start(f32[4,64,128]{2,1,0:T(8,128)} %cx.9) | copy-start | bytes 393220
  4.8 4.4 %collective-permute-start.3 = (f32[4,8,128]{2,1,0:T(8,128)S(1)}, f32[4,8,128]{2,1,0:T(8,128)S(1)}, u32[]{:S(2)}, u32[]{:S(2)}) collective-permute-start(f32[4,8,128]{2,1,0:T(8,128)S(1)} %get-tuple-element.48), channel_id=1, source_target_pairs={{0,4},{1,5},{2,6},{3,7},{4,0},{5,1},{6,2},{7,3},{8,12},{9,13},{10,... | collective-permute-start | bytes 49160 | tf_op jit(solution)/shard_map/ppermute | solution.py:418
  5.3 8.5 %collective-permute-start.4 = (f32[296,128]{1,0:T(8,128)S(1)}, f32[296,128]{1,0:T(8,128)S(1)}, u32[]{:S(2)}, u32[]{:S(2)}) collective-permute-start(f32[296,128]{1,0:T(8,128)S(1)} %get-tuple-element.53), channel_id=1, source_target_pairs={{0,4},{1,5},{2,6},{3,7},{4,0},{5,1},{6,2},{7,3},{8,16},{9,17},{10,... | collective-permute-start | bytes 454664 | tf_op jit(solution)/shard_map/ppermute | solution.py:418
  8.8 5.0 %collective-permute-start.5 = (f32[296,128]{1,0:T(8,128)S(1)}, f32[296,128]{1,0:T(8,128)S(1)}, u32[]{:S(2)}, u32[]{:S(2)}) collective-permute-start(f32[296,128]{1,0:T(8,128)S(1)} %get-tuple-element.54), channel_id=1, source_target_pairs={{0,8},{1,9},{2,10},{3,11},{4,12},{5,13},{6,14},{7,15},{8,0},{9,1},... | collective-permute-start | bytes 454664 | tf_op jit(solution)/shard_map/ppermute | solution.py:418
  9.3 4.5 %collective-permute-start.6 = (f32[40,128]{1,0:T(8,128)S(1)}, f32[40,128]{1,0:T(8,128)S(1)}, u32[]{:S(2)}, u32[]{:S(2)}) collective-permute-start(f32[40,128]{1,0:T(8,128)S(1)} %get-tuple-element.55), channel_id=1, source_target_pairs={{0,24},{1,25},{2,26},{3,27},{4,28},{5,29},{6,30},{7,31},{8,16},{9,... | collective-permute-start | bytes 61448 | tf_op jit(solution)/shard_map/ppermute | solution.py:418
  11.9 1.9 %collective-permute-start.7 = (f32[40,128]{1,0:T(8,128)S(1)}, f32[40,128]{1,0:T(8,128)S(1)}, u32[]{:S(2)}, u32[]{:S(2)}) collective-permute-start(f32[40,128]{1,0:T(8,128)S(1)} %get-tuple-element.56), channel_id=1, source_target_pairs={{0,8},{1,9},{2,10},{3,11},{4,12},{5,13},{6,14},{7,15},{8,0},{9,1},... | collective-permute-start | bytes 61448 | tf_op jit(solution)/shard_map/ppermute | solution.py:418

commit v8 on v7

--- a/solution.py
+++ b/solution.py
@@ -164,32 +164,39 @@
         ref[...] = message
 
 
-def z_inner(g_ref, w_ref, a_ref, c_ref, out):
+def lane(value, at):
+    lanes = value.shape[1]
+    return pltpu.roll(value, lanes - at, 1) if at else value
+
+
+def z_inner(g_ref, w_ref, a_ref, c_ref, edges, out, own):
     for x in range(a_ref.shape[0]):
         out[x] = interior(g_ref[x], w_ref[x], factors(a_ref[x], c_ref[x], 1), 1)
-
-
-def y_factors(ay, cy, *out):
-    for x in range(ay.shape[0]):
+    for n, at in enumerate((2, 3, 6, 7, 0, 1, 4, 5)):
+        own[n] = lane(edges[0], at)
+    for n, at in enumerate((4, 2, 3)):
+        own[8 + n] = lane(edges[1], at)
+
+
+def y_factors(sizes, ay, cy, *out):
+    planes, rows, lanes = ay.shape
+    tile = lax.broadcasted_iota(jnp.int32, (8, lanes), 0)
+    for x in range(planes):
         for ref, part in zip(out, factors(ay[x], cy[x], 0)):
             ref[x] = part
-
-
-def z_ends(edges, low, high, lanes):
-    lane = lambda value, at: pltpu.roll(value, lanes - at, 1) if at else value
-    wa, c = edges
+        a, c = (pltpu.roll(ref[x, rows - 8 :], by, 0) for ref, by in ((ay, 6), (cy, 4)))
+        up = jnp.where(tile >= 4, a, c)
+        a, c = (pltpu.roll(ref[x, :8], by, 0) for ref, by in ((ay, 2), (cy, 4)))
+        down = jnp.where(tile < 4, a, c)
+        for ref, message in zip(out[5:], to_send(sizes, 1, up, down)):
+            ref[x] = message
+
+
+def z_ends(own, low, high):
     w_far, w_low, c_far, c_low, a_far, a_low = (lane(low, at) for at in range(6))
-    first, second = low_end(
-        (w_far, w_low, a_far, a_low, c_far, c_low),
-        *(lane(wa, at) for at in (2, 3, 6, 7)),
-        lane(c, 4),
-    )
+    first, second = low_end((w_far, w_low, a_far, a_low, c_far, c_low), *own[:4], own[8])
     w_high, w_far, c_high, a_high, a_far = (lane(high, at) for at in (2, 3, 4, 6, 7))
-    last, before = high_end(
-        (w_high, w_far, a_high, a_far, c_high),
-        *(lane(wa, at) for at in (0, 1, 4, 5)),
-        *(lane(c, at) for at in (2, 3)),
-    )
+    last, before = high_end((w_high, w_far, a_high, a_far, c_high), *own[4:8], *own[9:])
     return first, second, last, before
 
 
@@ -208,14 +215,15 @@
     return total
 
 
-def z_sweep(sizes, partial, edges, opened, ay, cy, ax, cx, _, *rest):
-    n_in = colours(sizes, 2)
-    messages, (ends_ref, *out) = [m[...] for m in rest[:n_in]], rest[n_in:]
-    planes, rows, lanes = ay.shape
+def z_sweep(sizes, partial, own, opened, ax, cx, *rest):
+    n_in, n_y = colours(sizes, 2), colours(sizes, 1)
+    others, messages = rest[:n_y], [m[...] for m in rest[n_y : n_y + n_in]]
+    ends_ref, *out = rest[n_y + n_in :]
+    planes, rows, lanes = partial.shape
     per = fold(planes, rows, lanes)
     step = rows // per
-    low, high = received(sizes, 2, messages, edges[0])
-    ends = z_ends([edges[0], edges[1]], low, high, lanes)
+    low, high = received(sizes, 2, messages, own[0])
+    ends = z_ends([own[n] for n in range(11)], low, high)
     _, place = edge_lanes((step, lanes), lanes)
     ends_ref[...] = on_columns(
         place, slot, [spread(end, 0, 0, planes, lanes, column) for end, column in zip(ends, columns)]
@@ -232,12 +240,9 @@
             ]
             g = partial[x, rim] + on_columns(at, lanes, added)
             ws.append(opened[x, rim].astype(jnp.float32) * g)
-        a, c = (pltpu.roll(ref[x, rows - 8 :], by, 0) for ref, by in ((ay, 6), (cy, 4)))
-        up = jnp.where(tile >= 6, ws[1], jnp.where(tile >= 4, a, c))
-        a, c = (pltpu.roll(ref[x, :8], by, 0) for ref, by in ((ay, 2), (cy, 4)))
-        down = jnp.where(tile < 2, ws[0], jnp.where(tile < 4, a, c))
-        for ref, message in zip(out, to_send(sizes, 1, up, down)):
-            ref[x] = message
+        row = to_send(sizes, 1, tile, 7 - tile)
+        for other, ref, here, w in zip(others, out, row, to_send(sizes, 1, ws[1], ws[0])):
+            ref[x] = jnp.where(here >= 6, w, other[x])
 
 
 def x_products(w, cx):
@@ -426,12 +431,18 @@
         name="z_pack", scratch=[dma((4, planes))],
     )
     z_in = [swap(m, p) for m, p in zip(z_out, z_rounds)]
-    (partial,) = call(z_inner, [block], cot, w, az, cz, name="z_inner")
-    parts_y = call(y_factors, [block] * 5, ay, cy, name="y_factors")
+    partial, own = call(z_inner, [block, (11, *packed)], cot, w, az, cz, edges, name="z_inner")
+    factors_y = call(
+        functools.partial(y_factors, sizes),
+        [block] * 5 + [(planes, 8, lanes)] * len(y_rounds),
+        ay, cy,
+        name="y_factors",
+    )
+    parts_y, others_y = factors_y[:5], factors_y[5:]
     ends, *y_out = call(
         functools.partial(z_sweep, sizes),
         [packed] + [(planes, 8, lanes)] * len(y_rounds),
-        partial, edges, opened, ay, cy, ax, cx, parts_y[0], *z_in,
+        partial, own, opened, ax, cx, *others_y, *z_in,
         name="z_sweep",
     )
     y_in = [swap(m, p) for m, p in zip(y_out, y_rounds)]

time: 14.7 us -> 14.7 us (level)
  transfers between devices with their start and end apart: 8 -> 8, of which waited for: 2 -> 2; matrix products, arithmetic and copies ran while one was open for 0% -> 0% of each run, Pallas kernels for 6% -> 7%
where the time goes in v8:
time: 14.7 us; the launch traced here: 14.6 us
  starting transfers between devices  8.88 us (60%)
  Pallas kernels  3.34 us (23%)
  waiting for transfers between devices  2.26 us (15%)
    ppermute x8, starting transfers between devices, per_device(): swap = lambda value, perm: lax.ppermute(value, AXES, perm)  8.88 us
    pallas_call x8, Pallas kernels, call(): pl.pallas_call(body, out_shape=shapes, in_specs=[pl.BlockSpec(memory_spac...  3.34 us
    ppermute x8, waiting for transfers between devices, per_device(): swap = lambda value, perm: lax.ppermute(value, AXES, perm)  2.26 us
  transfers between devices with their start and end apart: 8, of which 2 were waited for; matrix products, arithmetic and copies ran while one was open for 0% of the time, Pallas kernels for 7%

profile of v8, /device:TPU:21, one launch (start us, length us, event | category | flops | bytes accessed | tf_op | source)
XLA Modules:
  0.0 14.6 jit_solution(2312232803444388326)
XLA Ops:
  0.0 0.0 copy-start.2
  0.0 0.0 copy-start.3
  0.0 1.3 %z_pack.1 = (f32[4,64,128]{2,1,0:T(8,128)S(1)}, s32[4,64,128]{2,1,0:T(8,128)S(1)}, f32[4,64,128]{2,1,0:T(8,128)S(1)}, f32[4,64,128]{2,1,0:T(8,128)S(1)}, f32[4,6...) custom-call(f32[4,64,128]{2,1,0:T(8,128)} %refs_0_.1, ...), custom_call_target="tpu_custom_call" | custom-call | bytes 1048576 | tf_op jit(solution)/shard_map/z_pack/pallas_call | solution.py:404
  1.3 0.7 %collective-permute-start = (f32[16,128]{1,0:T(8,128)S(1)}, f32[16,128]{1,0:T(8,128)S(1)}, u32[]{:S(2)}, u32[]{:S(2)}) collective-permute-start(f32[16,128]{1,0:T(8,128)S(1)} %get-tuple-element.43), channel_id=1, source_target_pairs={{0,1},{1,0},{2,10},{3,11},{4,5},{5,4},{6,14},{7,15},{8,9},{9,8},{1... | collective-permute-start | bytes 24584 | tf_op jit(solution)/shard_map/ppermute | solution.py:423
  2.1 0.0 collective-permute-start.1
  2.1 1.4 %collective-permute-start.2 = (f32[16,128]{1,0:T(8,128)S(1)}, f32[16,128]{1,0:T(8,128)S(1)}, u32[]{:S(2)}, u32[]{:S(2)}) collective-permute-start(f32[16,128]{1,0:T(8,128)S(1)} %get-tuple-element.45), channel_id=1, source_target_pairs={{0,8},{1,9},{2,3},{3,2},{4,12},{5,13},{6,7},{7,6},{8,0},{9,1},{10,... | collective-permute-start | bytes 24584 | tf_op jit(solution)/shard_map/ppermute | solution.py:423
  3.4 0.0 copy-done.2
  3.4 0.0 copy-done.3
  3.4 0.1 y_factors.1
  3.5 0.0 copy-start
  3.6 0.0 copy-start.1
  3.6 0.6 %z_inner.1 = (f32[4,64,128]{2,1,0:T(8,128)S(1)}, f32[11,16,128]{2,1,0:T(8,128)S(1)}) custom-call(f32[4,64,128]{2,1,0:T(8,128)S(1)} %get-tuple-element.34.g_ref, f32[4,64,128]{2,1,0:T(8,128)S(1)} %get-tuple-element.35.w_ref, f32[4,64,128]{2,1,0:T(8,128)S(1)} %get-tuple-element.36.a_ref, f32[4,64,128]{2,1,0:T(8,128)S(1)} %get-tuple-element.37.c_ref, ...), custom_call_target="tpu_custom_call" | custom-call | bytes 1048576 | tf_op jit(solution)/shard_map/z_inner/pallas_call | solution.py:404
  4.1 0.0 collective-permute-done.rest_1_
  4.1 0.4 %collective-permute-done.1.rest_2_ = f32[16,128]{1,0:T(8,128)S(1)} collective-permute-done((f32[16,128]{1,0:T(8,128)S(1)}, f32[16,128]{1,0:T(8,128)S(1)}, u32[]{:S(2)}, u32[]{:S(2)}) %collective-permute-start.1) | collective-permute-done | bytes 8224 | tf_op jit(solution)/shard_map/ppermute | solution.py:423
  4.6 0.0 collective-permute-done.2.rest_3_
  4.6 0.0 copy-done
  4.6 0.0 copy-done.1
  4.6 0.2 %z_sweep.1 = (f32[16,128]{1,0:T(8,128)S(1)}, f32[4,8,128]{2,1,0:T(8,128)S(1)}) custom-call(f32[4,64,128]{2,1,0:T(8,128)S(1)} %get-tuple-element.39.partial.partial_z, f32[11,16,128]{2,1,0:T(8,128)S(1)} %get-tuple-element.40.own, s32[4,64,128]{2,1,0:T(8,128)S(1)} %get-tuple-element.41.opened, f32[4,64,128]{2,1,0:T(8,128)S(1)} %copy-done, ...), custom_call_target="tpu_custom_call" | custom-call | bytes 1048576 | tf_op jit(solution)/shard_map/z_sweep/pallas_call | solution.py:404
  4.8 0.3 %collective-permute-start.3 = (f32[4,8,128]{2,1,0:T(8,128)S(1)}, f32[4,8,128]{2,1,0:T(8,128)S(1)}, u32[]{:S(2)}, u32[]{:S(2)}) collective-permute-start(f32[4,8,128]{2,1,0:T(8,128)S(1)} %get-tuple-element.54), channel_id=1, source_target_pairs={{0,4},{1,5},{2,6},{3,7},{4,0},{5,1},{6,2},{7,3},{8,12},{9,13},{10,... | collective-permute-start | bytes 49160 | tf_op jit(solution)/shard_map/ppermute | solution.py:423
  5.1 0.2 %y_inner.1 = (f32[4,64,128]{2,1,0:T(8,128)S(1)}, f32[4,8,128]{2,1,0:T(8,128)S(1)}, f32[296,128]{1,0:T(8,128)S(1)}, f32[296,128]{1,0:T(8,128)S(1)}) custom-call(f32[4,64,128]{2,1,0:T(8,128)S(1)} %get-tuple-element.39.partial.partial_z, f32[16,128]{1,0:T(8,128)S(1)} %get-tuple-element.46.ends_ref, s32[4,64,128]{2,1,0:T(8,128)S(1)} %get-tuple-element.41.opened, ...), custom_call_target="tpu_custom_call" | custom-call | bytes 1048576 | tf_op jit(solution)/shard_map/y_inner/pallas_call | solution.py:404
  5.3 3.5 %collective-permute-start.4 = (f32[296,128]{1,0:T(8,128)S(1)}, f32[296,128]{1,0:T(8,128)S(1)}, u32[]{:S(2)}, u32[]{:S(2)}) collective-permute-start(f32[296,128]{1,0:T(8,128)S(1)} %get-tuple-element.59), channel_id=1, source_target_pairs={{0,4},{1,5},{2,6},{3,7},{4,0},{5,1},{6,2},{7,3},{8,16},{9,17},{10,... | collective-permute-start | bytes 454664 | tf_op jit(solution)/shard_map/ppermute | solution.py:423
  8.8 0.4 %collective-permute-start.5 = (f32[296,128]{1,0:T(8,128)S(1)}, f32[296,128]{1,0:T(8,128)S(1)}, u32[]{:S(2)}, u32[]{:S(2)}) collective-permute-start(f32[296,128]{1,0:T(8,128)S(1)} %get-tuple-element.60), channel_id=1, source_target_pairs={{0,8},{1,9},{2,10},{3,11},{4,12},{5,13},{6,14},{7,15},{8,0},{9,1},... | collective-permute-start | bytes 454664 | tf_op jit(solution)/shard_map/ppermute | solution.py:423
  9.2 0.0 collective-permute-done.3.rest_0_
  9.2 0.1 y_sweep.1
  9.3 2.6 %collective-permute-start.6 = (f32[40,128]{1,0:T(8,128)S(1)}, f32[40,128]{1,0:T(8,128)S(1)}, u32[]{:S(2)}, u32[]{:S(2)}) collective-permute-start(f32[40,128]{1,0:T(8,128)S(1)} %get-tuple-element.61), channel_id=1, source_target_pairs={{0,24},{1,25},{2,26},{3,27},{4,28},{5,29},{6,30},{7,31},{8,16},{9,... | collective-permute-start | bytes 61448 | tf_op jit(solution)/shard_map/ppermute | solution.py:423
  11.9 0.0 collective-permute-start.7
  11.9 0.1 x_inner.1
  12.0 1.8 %collective-permute-done.6.rest_2_ = f32[40,128]{1,0:T(8,128)S(1)} collective-permute-done((f32[40,128]{1,0:T(8,128)S(1)}, f32[40,128]{1,0:T(8,128)S(1)}, u32[]{:S(2)}, u32[]{:S(2)}) %collective-permute-start.6) | collective-permute-done | bytes 20512 | tf_op jit(solution)/shard_map/ppermute | solution.py:423
  13.8 0.0 collective-permute-done.7.rest_3_
  13.8 0.0 collective-permute-done.4.rest_0_
  13.8 0.0 collective-permute-done.5.rest_1_
  13.8 0.8 %x_sweep.1 = f32[4,64,128]{2,1,0:T(8,128)} custom-call(f32[4,64,128]{2,1,0:T(8,128)S(1)} %get-tuple-element.55.g_ref, f32[4,64,128]{2,1,0:T(8,128)S(1)} %copy-done, f32[4,64,128]{2,1,0:T(8,128)S(1)} %copy-done.1, f32[4,64,128]{2,1,0:T(8,128)S(1)} %get-tuple-element.56.ready, f32[2,64,128]{2,1,0:T(8,128)S(1)} %get-tuple-element.57.own_ref, ...), custom_call_target="tpu_custom_call" | custom-call | bytes 1048576 | tf_op jit(solution)/shard_map/x_sweep/pallas_call | solution.py:404
Async XLA Ops:
  0.0 3.4 %copy-start.2 = (f32[4,64,128]{2,1,0:T(8,128)S(1)}, f32[4,64,128]{2,1,0:T(8,128)}, u32[]{:S(2)}) copy-start(f32[4,64,128]{2,1,0:T(8,128)} %ay.3) | copy-start | bytes 393220
  0.0 3.4 %copy-start.3 = (f32[4,64,128]{2,1,0:T(8,128)S(1)}, f32[4,64,128]{2,1,0:T(8,128)}, u32[]{:S(2)}) copy-start(f32[4,64,128]{2,1,0:T(8,128)} %cy.3) | copy-start | bytes 393220
  1.3 2.8 %collective-permute-start = (f32[16,128]{1,0:T(8,128)S(1)}, f32[16,128]{1,0:T(8,128)S(1)}, u32[]{:S(2)}, u32[]{:S(2)}) collective-permute-start(f32[16,128]{1,0:T(8,128)S(1)} %get-tuple-element.43), channel_id=1, source_target_pairs={{0,1},{1,0},{2,10},{3,11},{4,5},{5,4},{6,14},{7,15},{8,9},{9,8},{1... | collective-permute-start | bytes 24584 | tf_op jit(solution)/shard_map/ppermute | solution.py:423
  2.1 2.5 %collective-permute-start.1 = (f32[16,128]{1,0:T(8,128)S(1)}, f32[16,128]{1,0:T(8,128)S(1)}, u32[]{:S(2)}, u32[]{:S(2)}) collective-permute-start(f32[16,128]{1,0:T(8,128)S(1)} %get-tuple-element.44), channel_id=1, source_target_pairs={{0,8},{1,2},{2,1},{3,11},{4,12},{5,6},{6,5},{7,15},{8,0},{9,10},{1... | collective-permute-start | bytes 24584 | tf_op jit(solution)/shard_map/ppermute | solution.py:423
  2.1 2.5 %collective-permute-start.2 = (f32[16,128]{1,0:T(8,128)S(1)}, f32[16,128]{1,0:T(8,128)S(1)}, u32[]{:S(2)}, u32[]{:S(2)}) collective-permute-start(f32[16,128]{1,0:T(8,128)S(1)} %get-tuple-element.45), channel_id=1, source_target_pairs={{0,8},{1,9},{2,3},{3,2},{4,12},{5,13},{6,7},{7,6},{8,0},{9,1},{10,... | collective-permute-start | bytes 24584 | tf_op jit(solution)/shard_map/ppermute | solution.py:423
  3.5 1.0 %copy-start = (f32[4,64,128]{2,1,0:T(8,128)S(1)}, f32[4,64,128]{2,1,0:T(8,128)}, u32[]{:S(2)}) copy-start(f32[4,64,128]{2,1,0:T(8,128)} %ax.7) | copy-start | bytes 393220
  3.6 1.0 %copy-start.1 = (f32[4,64,128]{2,1,0:T(8,128)S(1)}, f32[4,64,128]{2,1,0:T(8,128)}, u32[]{:S(2)}) copy-start(f32[4,64,128]{2,1,0:T(8,128)} %cx.9) | copy-start | bytes 393220
  4.8 4.4 %collective-permute-start.3 = (f32[4,8,128]{2,1,0:T(8,128)S(1)}, f32[4,8,128]{2,1,0:T(8,128)S(1)}, u32[]{:S(2)}, u32[]{:S(2)}) collective-permute-start(f32[4,8,128]{2,1,0:T(8,128)S(1)} %get-tuple-element.54), channel_id=1, source_target_pairs={{0,4},{1,5},{2,6},{3,7},{4,0},{5,1},{6,2},{7,3},{8,12},{9,13},{10,... | collective-permute-start | bytes 49160 | tf_op jit(solution)/shard_map/ppermute | solution.py:423
  5.3 8.5 %collective-permute-start.4 = (f32[296,128]{1,0:T(8,128)S(1)}, f32[296,128]{1,0:T(8,128)S(1)}, u32[]{:S(2)}, u32[]{:S(2)}) collective-permute-start(f32[296,128]{1,0:T(8,128)S(1)} %get-tuple-element.59), channel_id=1, source_target_pairs={{0,4},{1,5},{2,6},{3,7},{4,0},{5,1},{6,2},{7,3},{8,16},{9,17},{10,... | collective-permute-start | bytes 454664 | tf_op jit(solution)/shard_map/ppermute | solution.py:423
  8.8 5.0 %collective-permute-start.5 = (f32[296,128]{1,0:T(8,128)S(1)}, f32[296,128]{1,0:T(8,128)S(1)}, u32[]{:S(2)}, u32[]{:S(2)}) collective-permute-start(f32[296,128]{1,0:T(8,128)S(1)} %get-tuple-element.60), channel_id=1, source_target_pairs={{0,8},{1,9},{2,10},{3,11},{4,12},{5,13},{6,14},{7,15},{8,0},{9,1},... | collective-permute-start | bytes 454664 | tf_op jit(solution)/shard_map/ppermute | solution.py:423
  9.3 4.5 %collective-permute-start.6 = (f32[40,128]{1,0:T(8,128)S(1)}, f32[40,128]{1,0:T(8,128)S(1)}, u32[]{:S(2)}, u32[]{:S(2)}) collective-permute-start(f32[40,128]{1,0:T(8,128)S(1)} %get-tuple-element.61), channel_id=1, source_target_pairs={{0,24},{1,25},{2,26},{3,27},{4,28},{5,29},{6,30},{7,31},{8,16},{9,... | collective-permute-start | bytes 61448 | tf_op jit(solution)/shard_map/ppermute | solution.py:423
  11.9 1.9 %collective-permute-start.7 = (f32[40,128]{1,0:T(8,128)S(1)}, f32[40,128]{1,0:T(8,128)S(1)}, u32[]{:S(2)}, u32[]{:S(2)}) collective-permute-start(f32[40,128]{1,0:T(8,128)S(1)} %get-tuple-element.62), channel_id=1, source_target_pairs={{0,8},{1,9},{2,10},{3,11},{4,12},{5,13},{6,14},{7,15},{8,0},{9,1},... | collective-permute-start | bytes 61448 | tf_op jit(solution)/shard_map/ppermute | solution.py:423

commit v9 on v8

--- a/solution.py
+++ b/solution.py
@@ -178,18 +178,19 @@
         own[8 + n] = lane(edges[1], at)
 
 
+def y_base(planes):
+    return (2 * planes + 7) // 8 * 8
+
+
 def y_factors(sizes, ay, cy, *out):
     planes, rows, lanes = ay.shape
-    tile = lax.broadcasted_iota(jnp.int32, (8, lanes), 0)
     for x in range(planes):
         for ref, part in zip(out, factors(ay[x], cy[x], 0)):
             ref[x] = part
-        a, c = (pltpu.roll(ref[x, rows - 8 :], by, 0) for ref, by in ((ay, 6), (cy, 4)))
-        up = jnp.where(tile >= 4, a, c)
-        a, c = (pltpu.roll(ref[x, :8], by, 0) for ref, by in ((ay, 2), (cy, 4)))
-        down = jnp.where(tile < 4, a, c)
-        for ref, message in zip(out[5:], to_send(sizes, 1, up, down)):
-            ref[x] = message
+        for n, field in enumerate((ay, cy)):
+            at = y_base(planes) + 4 * x + 2 * n
+            for ref, pair in zip(out[5:], to_send(sizes, 1, field[x, rows - 2 :], field[x, :2])):
+                ref[at : at + 2] = pair
 
 
 def z_ends(own, low, high):
@@ -231,7 +232,6 @@
     if not out:
         return
     at = lax.broadcasted_iota(jnp.int32, (8, lanes), 1)
-    tile = lax.broadcasted_iota(jnp.int32, (8, lanes), 0)
     for x in range(planes):
         ws = []
         for rim, group, r in ((slice(0, 8), slice(0, 8), 0), (slice(rows - 8, rows), slice(step - 8, step), per - 1)):
@@ -240,9 +240,11 @@
             ]
             g = partial[x, rim] + on_columns(at, lanes, added)
             ws.append(opened[x, rim].astype(jnp.float32) * g)
-        row = to_send(sizes, 1, tile, 7 - tile)
-        for other, ref, here, w in zip(others, out, row, to_send(sizes, 1, ws[1], ws[0])):
-            ref[x] = jnp.where(here >= 6, w, other[x])
+        for ref, pair in zip(out, to_send(sizes, 1, ws[1][6:], ws[0][:2])):
+            ref[2 * x : 2 * x + 2] = pair
+    base = y_base(planes)
+    for other, ref in zip(others, out):
+        ref[base:] = other[base:]
 
 
 def x_products(w, cx):
@@ -293,15 +295,20 @@
     planes, rows, lanes = ay.shape
     tile = lax.broadcasted_iota(jnp.int32, (8, lanes), 0)
     ws = []
-    for x in range(planes):
-        low, high = received(sizes, 1, [m[x] for m in messages], ay[x, :8])
+    base = y_base(planes)
+    all_low, all_high = received(sizes, 1, [m[...] for m in messages], ay[0, : base + 4 * planes])
+    for x in range(planes):
+        low, high = (
+            [value[n : n + 1] for n in (2 * x, 2 * x + 1, *range(base + 4 * x, base + 4 * x + 4))]
+            for value in (all_low, all_high)
+        )
         row = lambda ref, n: ref[x, n : n + 1]
         first, second = low_end(
-            [low[v : v + 1] for v in (6, 7, 4, 5, 2, 3)],
+            low,
             *(row(ref, n) for ref, n in ((w_rims, 0), (w_rims, 1), (ay, 0), (ay, 1), (cy, 0))),
         )
         last, before = high_end(
-            [high[v : v + 1] for v in range(5)],
+            high[:5],
             row(w_rims, 6),
             row(w_rims, 7),
             *(row(ref, n) for ref in (ay, cy) for n in (rows - 2, rows - 1)),
@@ -434,14 +441,14 @@
     partial, own = call(z_inner, [block, (11, *packed)], cot, w, az, cz, edges, name="z_inner")
     factors_y = call(
         functools.partial(y_factors, sizes),
-        [block] * 5 + [(planes, 8, lanes)] * len(y_rounds),
+        [block] * 5 + [(y_base(planes) + 4 * planes, lanes)] * len(y_rounds),
         ay, cy,
         name="y_factors",
     )
     parts_y, others_y = factors_y[:5], factors_y[5:]
     ends, *y_out = call(
         functools.partial(z_sweep, sizes),
-        [packed] + [(planes, 8, lanes)] * len(y_rounds),
+        [packed] + [(y_base(planes) + 4 * planes, lanes)] * len(y_rounds),
         partial, own, opened, ax, cx, *others_y, *z_in,
         name="z_sweep",
     )

time: 14.7 us -> 14.7 us (level)
  no operation moved by 1% of the time
where the time goes in v9:
time: 14.7 us; the launch traced here: 14.5 us
  starting transfers between devices  8.83 us (60%)
  Pallas kernels  3.36 us (23%)
  waiting for transfers between devices  2.25 us (15%)
    ppermute x8, starting transfers between devices, per_device(): swap = lambda value, perm: lax.ppermute(value, AXES, perm)  8.83 us
    pallas_call x8, Pallas kernels, call(): pl.pallas_call(body, out_shape=shapes, in_specs=[pl.BlockSpec(memory_spac...  3.36 us
    ppermute x8, waiting for transfers between devices, per_device(): swap = lambda value, perm: lax.ppermute(value, AXES, perm)  2.25 us
  transfers between devices with their start and end apart: 8, of which 2 were waited for; matrix products, arithmetic and copies ran while one was open for 0% of the time, Pallas kernels for 7%

profile of v9, /device:TPU:21, one launch (start us, length us, event | category | flops | bytes accessed | tf_op | source)
XLA Modules:
  0.0 14.5 jit_solution(4173258685129197209)
XLA Ops:
  0.0 0.0 copy-start.2
  0.0 0.0 copy-start.3
  0.0 1.3 %z_pack.1 = (f32[4,64,128]{2,1,0:T(8,128)S(1)}, s32[4,64,128]{2,1,0:T(8,128)S(1)}, f32[4,64,128]{2,1,0:T(8,128)S(1)}, f32[4,64,128]{2,1,0:T(8,128)S(1)}, f32[4,6...) custom-call(f32[4,64,128]{2,1,0:T(8,128)} %refs_0_.1, ...), custom_call_target="tpu_custom_call" | custom-call | bytes 1048576 | tf_op jit(solution)/shard_map/z_pack/pallas_call | solution.py:411
  1.3 0.7 %collective-permute-start = (f32[16,128]{1,0:T(8,128)S(1)}, f32[16,128]{1,0:T(8,128)S(1)}, u32[]{:S(2)}, u32[]{:S(2)}) collective-permute-start(f32[16,128]{1,0:T(8,128)S(1)} %get-tuple-element.43), channel_id=1, source_target_pairs={{0,1},{1,0},{2,10},{3,11},{4,5},{5,4},{6,14},{7,15},{8,9},{9,8},{1... | collective-permute-start | bytes 24584 | tf_op jit(solution)/shard_map/ppermute | solution.py:430
  2.1 0.0 collective-permute-start.1
  2.1 1.4 %collective-permute-start.2 = (f32[16,128]{1,0:T(8,128)S(1)}, f32[16,128]{1,0:T(8,128)S(1)}, u32[]{:S(2)}, u32[]{:S(2)}) collective-permute-start(f32[16,128]{1,0:T(8,128)S(1)} %get-tuple-element.45), channel_id=1, source_target_pairs={{0,8},{1,9},{2,3},{3,2},{4,12},{5,13},{6,7},{7,6},{8,0},{9,1},{10,... | collective-permute-start | bytes 24584 | tf_op jit(solution)/shard_map/ppermute | solution.py:430
  3.4 0.0 copy-done.2
  3.4 0.0 copy-done.3
  3.4 0.1 y_factors.1
  3.5 0.0 copy-start
  3.6 0.0 copy-start.1
  3.6 0.6 %z_inner.1 = (f32[4,64,128]{2,1,0:T(8,128)S(1)}, f32[11,16,128]{2,1,0:T(8,128)S(1)}) custom-call(f32[4,64,128]{2,1,0:T(8,128)S(1)} %get-tuple-element.34.g_ref, f32[4,64,128]{2,1,0:T(8,128)S(1)} %get-tuple-element.35.w_ref, f32[4,64,128]{2,1,0:T(8,128)S(1)} %get-tuple-element.36.a_ref, f32[4,64,128]{2,1,0:T(8,128)S(1)} %get-tuple-element.37.c_ref, ...), custom_call_target="tpu_custom_call" | custom-call | bytes 1048576 | tf_op jit(solution)/shard_map/z_inner/pallas_call | solution.py:411
  4.1 0.0 collective-permute-done.rest_1_
  4.1 0.4 %collective-permute-done.1.rest_2_ = f32[16,128]{1,0:T(8,128)S(1)} collective-permute-done((f32[16,128]{1,0:T(8,128)S(1)}, f32[16,128]{1,0:T(8,128)S(1)}, u32[]{:S(2)}, u32[]{:S(2)}) %collective-permute-start.1) | collective-permute-done | bytes 8224 | tf_op jit(solution)/shard_map/ppermute | solution.py:430
  4.6 0.0 collective-permute-done.2.rest_3_
  4.6 0.0 copy-done
  4.6 0.0 copy-done.1
  4.6 0.2 %z_sweep.1 = (f32[16,128]{1,0:T(8,128)S(1)}, f32[24,128]{1,0:T(8,128)S(1)}) custom-call(f32[4,64,128]{2,1,0:T(8,128)S(1)} %get-tuple-element.39.partial.partial_z, f32[11,16,128]{2,1,0:T(8,128)S(1)} %get-tuple-element.40.own, s32[4,64,128]{2,1,0:T(8,128)S(1)} %get-tuple-element.41.opened, f32[4,64,128]{2,1,0:T(8,128)S(1)} %copy-done, ...), custom_call_target="tpu_custom_call" | custom-call | bytes 1048576 | tf_op jit(solution)/shard_map/z_sweep/pallas_call | solution.py:411
  4.8 0.3 %collective-permute-start.3 = (f32[24,128]{1,0:T(8,128)S(1)}, f32[24,128]{1,0:T(8,128)S(1)}, u32[]{:S(2)}, u32[]{:S(2)}) collective-permute-start(f32[24,128]{1,0:T(8,128)S(1)} %get-tuple-element.54), channel_id=1, source_target_pairs={{0,4},{1,5},{2,6},{3,7},{4,0},{5,1},{6,2},{7,3},{8,12},{9,13},{10,... | collective-permute-start | bytes 36872 | tf_op jit(solution)/shard_map/ppermute | solution.py:430
  5.1 0.2 %y_inner.1 = (f32[4,64,128]{2,1,0:T(8,128)S(1)}, f32[4,8,128]{2,1,0:T(8,128)S(1)}, f32[296,128]{1,0:T(8,128)S(1)}, f32[296,128]{1,0:T(8,128)S(1)}) custom-call(f32[4,64,128]{2,1,0:T(8,128)S(1)} %get-tuple-element.39.partial.partial_z, f32[16,128]{1,0:T(8,128)S(1)} %get-tuple-element.46.ends_ref, s32[4,64,128]{2,1,0:T(8,128)S(1)} %get-tuple-element.41.opened, ...), custom_call_target="tpu_custom_call" | custom-call | bytes 1048576 | tf_op jit(solution)/shard_map/y_inner/pallas_call | solution.py:411
  5.3 3.5 %collective-permute-start.4 = (f32[296,128]{1,0:T(8,128)S(1)}, f32[296,128]{1,0:T(8,128)S(1)}, u32[]{:S(2)}, u32[]{:S(2)}) collective-permute-start(f32[296,128]{1,0:T(8,128)S(1)} %get-tuple-element.59), channel_id=1, source_target_pairs={{0,4},{1,5},{2,6},{3,7},{4,0},{5,1},{6,2},{7,3},{8,16},{9,17},{10,... | collective-permute-start | bytes 454664 | tf_op jit(solution)/shard_map/ppermute | solution.py:430
  8.8 0.4 %collective-permute-start.5 = (f32[296,128]{1,0:T(8,128)S(1)}, f32[296,128]{1,0:T(8,128)S(1)}, u32[]{:S(2)}, u32[]{:S(2)}) collective-permute-start(f32[296,128]{1,0:T(8,128)S(1)} %get-tuple-element.60), channel_id=1, source_target_pairs={{0,8},{1,9},{2,10},{3,11},{4,12},{5,13},{6,14},{7,15},{8,0},{9,1},... | collective-permute-start | bytes 454664 | tf_op jit(solution)/shard_map/ppermute | solution.py:430
  9.2 0.0 collective-permute-done.3.rest_0_
  9.2 0.1 y_sweep.1
  9.3 2.5 %collective-permute-start.6 = (f32[40,128]{1,0:T(8,128)S(1)}, f32[40,128]{1,0:T(8,128)S(1)}, u32[]{:S(2)}, u32[]{:S(2)}) collective-permute-start(f32[40,128]{1,0:T(8,128)S(1)} %get-tuple-element.61), channel_id=1, source_target_pairs={{0,24},{1,25},{2,26},{3,27},{4,28},{5,29},{6,30},{7,31},{8,16},{9,... | collective-permute-start | bytes 61448 | tf_op jit(solution)/shard_map/ppermute | solution.py:430
  11.8 0.0 collective-permute-start.7
  11.8 0.1 x_inner.1
  11.9 1.8 %collective-permute-done.6.rest_2_ = f32[40,128]{1,0:T(8,128)S(1)} collective-permute-done((f32[40,128]{1,0:T(8,128)S(1)}, f32[40,128]{1,0:T(8,128)S(1)}, u32[]{:S(2)}, u32[]{:S(2)}) %collective-permute-start.6) | collective-permute-done | bytes 20512 | tf_op jit(solution)/shard_map/ppermute | solution.py:430
  13.7 0.0 collective-permute-done.7.rest_3_
  13.7 0.0 collective-permute-done.4.rest_0_
  13.7 0.0 collective-permute-done.5.rest_1_
  13.7 0.8 %x_sweep.1 = f32[4,64,128]{2,1,0:T(8,128)} custom-call(f32[4,64,128]{2,1,0:T(8,128)S(1)} %get-tuple-element.55.g_ref, f32[4,64,128]{2,1,0:T(8,128)S(1)} %copy-done, f32[4,64,128]{2,1,0:T(8,128)S(1)} %copy-done.1, f32[4,64,128]{2,1,0:T(8,128)S(1)} %get-tuple-element.56.ready, f32[2,64,128]{2,1,0:T(8,128)S(1)} %get-tuple-element.57.own_ref, ...), custom_call_target="tpu_custom_call" | custom-call | bytes 1048576 | tf_op jit(solution)/shard_map/x_sweep/pallas_call | solution.py:411
Async XLA Ops:
  0.0 3.4 %copy-start.2 = (f32[4,64,128]{2,1,0:T(8,128)S(1)}, f32[4,64,128]{2,1,0:T(8,128)}, u32[]{:S(2)}) copy-start(f32[4,64,128]{2,1,0:T(8,128)} %ay.3) | copy-start | bytes 393220
  0.0 3.4 %copy-start.3 = (f32[4,64,128]{2,1,0:T(8,128)S(1)}, f32[4,64,128]{2,1,0:T(8,128)}, u32[]{:S(2)}) copy-start(f32[4,64,128]{2,1,0:T(8,128)} %cy.3) | copy-start | bytes 393220
  1.3 2.8 %collective-permute-start = (f32[16,128]{1,0:T(8,128)S(1)}, f32[16,128]{1,0:T(8,128)S(1)}, u32[]{:S(2)}, u32[]{:S(2)}) collective-permute-start(f32[16,128]{1,0:T(8,128)S(1)} %get-tuple-element.43), channel_id=1, source_target_pairs={{0,1},{1,0},{2,10},{3,11},{4,5},{5,4},{6,14},{7,15},{8,9},{9,8},{1... | collective-permute-start | bytes 24584 | tf_op jit(solution)/shard_map/ppermute | solution.py:430
  2.1 2.5 %collective-permute-start.1 = (f32[16,128]{1,0:T(8,128)S(1)}, f32[16,128]{1,0:T(8,128)S(1)}, u32[]{:S(2)}, u32[]{:S(2)}) collective-permute-start(f32[16,128]{1,0:T(8,128)S(1)} %get-tuple-element.44), channel_id=1, source_target_pairs={{0,8},{1,2},{2,1},{3,11},{4,12},{5,6},{6,5},{7,15},{8,0},{9,10},{1... | collective-permute-start | bytes 24584 | tf_op jit(solution)/shard_map/ppermute | solution.py:430
  2.1 2.5 %collective-permute-start.2 = (f32[16,128]{1,0:T(8,128)S(1)}, f32[16,128]{1,0:T(8,128)S(1)}, u32[]{:S(2)}, u32[]{:S(2)}) collective-permute-start(f32[16,128]{1,0:T(8,128)S(1)} %get-tuple-element.45), channel_id=1, source_target_pairs={{0,8},{1,9},{2,3},{3,2},{4,12},{5,13},{6,7},{7,6},{8,0},{9,1},{10,... | collective-permute-start | bytes 24584 | tf_op jit(solution)/shard_map/ppermute | solution.py:430
  3.5 1.0 %copy-start = (f32[4,64,128]{2,1,0:T(8,128)S(1)}, f32[4,64,128]{2,1,0:T(8,128)}, u32[]{:S(2)}) copy-start(f32[4,64,128]{2,1,0:T(8,128)} %ax.7) | copy-start | bytes 393220
  3.6 1.0 %copy-start.1 = (f32[4,64,128]{2,1,0:T(8,128)S(1)}, f32[4,64,128]{2,1,0:T(8,128)}, u32[]{:S(2)}) copy-start(f32[4,64,128]{2,1,0:T(8,128)} %cx.9) | copy-start | bytes 393220
  4.8 4.4 %collective-permute-start.3 = (f32[24,128]{1,0:T(8,128)S(1)}, f32[24,128]{1,0:T(8,128)S(1)}, u32[]{:S(2)}, u32[]{:S(2)}) collective-permute-start(f32[24,128]{1,0:T(8,128)S(1)} %get-tuple-element.54), channel_id=1, source_target_pairs={{0,4},{1,5},{2,6},{3,7},{4,0},{5,1},{6,2},{7,3},{8,12},{9,13},{10,... | collective-permute-start | bytes 36872 | tf_op jit(solution)/shard_map/ppermute | solution.py:430
  5.3 8.4 %collective-permute-start.4 = (f32[296,128]{1,0:T(8,128)S(1)}, f32[296,128]{1,0:T(8,128)S(1)}, u32[]{:S(2)}, u32[]{:S(2)}) collective-permute-start(f32[296,128]{1,0:T(8,128)S(1)} %get-tuple-element.59), channel_id=1, source_target_pairs={{0,4},{1,5},{2,6},{3,7},{4,0},{5,1},{6,2},{7,3},{8,16},{9,17},{10,... | collective-permute-start | bytes 454664 | tf_op jit(solution)/shard_map/ppermute | solution.py:430
  8.8 4.9 %collective-permute-start.5 = (f32[296,128]{1,0:T(8,128)S(1)}, f32[296,128]{1,0:T(8,128)S(1)}, u32[]{:S(2)}, u32[]{:S(2)}) collective-permute-start(f32[296,128]{1,0:T(8,128)S(1)} %get-tuple-element.60), channel_id=1, source_target_pairs={{0,8},{1,9},{2,10},{3,11},{4,12},{5,13},{6,14},{7,15},{8,0},{9,1},... | collective-permute-start | bytes 454664 | tf_op jit(solution)/shard_map/ppermute | solution.py:430
  9.3 4.4 %collective-permute-start.6 = (f32[40,128]{1,0:T(8,128)S(1)}, f32[40,128]{1,0:T(8,128)S(1)}, u32[]{:S(2)}, u32[]{:S(2)}) collective-permute-start(f32[40,128]{1,0:T(8,128)S(1)} %get-tuple-element.61), channel_id=1, source_target_pairs={{0,24},{1,25},{2,26},{3,27},{4,28},{5,29},{6,30},{7,31},{8,16},{9,... | collective-permute-start | bytes 61448 | tf_op jit(solution)/shard_map/ppermute | solution.py:430
  11.8 1.9 %collective-permute-start.7 = (f32[40,128]{1,0:T(8,128)S(1)}, f32[40,128]{1,0:T(8,128)S(1)}, u32[]{:S(2)}, u32[]{:S(2)}) collective-permute-start(f32[40,128]{1,0:T(8,128)S(1)} %get-tuple-element.62), channel_id=1, source_target_pairs={{0,8},{1,9},{2,10},{3,11},{4,12},{5,13},{6,14},{7,15},{8,0},{9,1},... | collective-permute-start | bytes 61448 | tf_op jit(solution)/shard_map/ppermute | solution.py:430

commit v10 on v7

--- a/solution.py
+++ b/solution.py
@@ -164,14 +164,21 @@
         ref[...] = message
 
 
-def z_inner(g_ref, w_ref, a_ref, c_ref, out):
-    for x in range(a_ref.shape[0]):
+def z_inner(g_ref, w_ref, a_ref, c_ref, ay_in, cy_in, out, ay, cy, *rest):
+    parts, sems = rest[:5], rest[5]
+    copies = [
+        pltpu.make_async_copy(src, dst, sems.at[n])
+        for n, (src, dst) in enumerate(((ay_in, ay), (cy_in, cy)))
+    ]
+    for copy in copies:
+        copy.start()
+    planes = a_ref.shape[0]
+    for x in range(planes):
         out[x] = interior(g_ref[x], w_ref[x], factors(a_ref[x], c_ref[x], 1), 1)
-
-
-def y_factors(ay, cy, *out):
-    for x in range(ay.shape[0]):
-        for ref, part in zip(out, factors(ay[x], cy[x], 0)):
+    for copy in copies:
+        copy.wait()
+    for x in range(planes):
+        for ref, part in zip(parts, factors(ay[x], cy[x], 0)):
             ref[x] = part
 
 
@@ -208,7 +215,7 @@
     return total
 
 
-def z_sweep(sizes, partial, edges, opened, ay, cy, ax, cx, _, *rest):
+def z_sweep(sizes, partial, edges, opened, ay, cy, ax, cx, *rest):
     n_in = colours(sizes, 2)
     messages, (ends_ref, *out) = [m[...] for m in rest[:n_in]], rest[n_in:]
     planes, rows, lanes = ay.shape
@@ -426,12 +433,13 @@
         name="z_pack", scratch=[dma((4, planes))],
     )
     z_in = [swap(m, p) for m, p in zip(z_out, z_rounds)]
-    (partial,) = call(z_inner, [block], cot, w, az, cz, name="z_inner")
-    parts_y = call(y_factors, [block] * 5, ay, cy, name="y_factors")
+    partial, ay, cy, *parts_y = call(
+        z_inner, [block] * 8, cot, w, az, cz, loads=(ay, cy), name="z_inner", scratch=[dma((2,))]
+    )
     ends, *y_out = call(
         functools.partial(z_sweep, sizes),
         [packed] + [(planes, 8, lanes)] * len(y_rounds),
-        partial, edges, opened, ay, cy, ax, cx, parts_y[0], *z_in,
+        partial, edges, opened, ay, cy, ax, cx, *z_in,
         name="z_sweep",
     )
     y_in = [swap(m, p) for m, p in zip(y_out, y_rounds)]

time: 14.7 us -> 14.8 us (level)
  waiting for transfers between devices: 2.36 us -> 1.82 us
  Pallas kernels: 3.25 us -> 3.77 us
    ppermute x8, waiting for transfers between devices: 2.36 us -> 1.82 us  [per_device(): swap = lambda value, perm: lax.ppermute(value, AXES, perm)]
    pallas_call x8 -> x7, Pallas kernels: 3.25 us -> 3.77 us  [call(): pl.pallas_call(body, out_shape=shapes, in_specs=[pl.BlockSpec(memory_spac...]
  transfers between devices with their start and end apart: 8 -> 8, of which waited for: 2 -> 1; matrix products, arithmetic and copies ran while one was open for 0% -> 0% of each run, Pallas kernels for 6% -> 10%
where the time goes in v10:
time: 14.8 us; the launch traced here: 14.5 us
  starting transfers between devices  8.85 us (60%)
  Pallas kernels  3.77 us (25%)
  waiting for transfers between devices  1.82 us (12%)
    ppermute x8, starting transfers between devices, per_device(): swap = lambda value, perm: lax.ppermute(value, AXES, perm)  8.85 us
    pallas_call x7, Pallas kernels, call(): pl.pallas_call(body, out_shape=shapes, in_specs=[pl.BlockSpec(memory_spac...  3.77 us
    ppermute x8, waiting for transfers between devices, per_device(): swap = lambda value, perm: lax.ppermute(value, AXES, perm)  1.82 us
  transfers between devices with their start and end apart: 8, of which 1 were waited for; matrix products, arithmetic and copies ran while one was open for 0% of the time, Pallas kernels for 10%

profile of v10, /device:TPU:21, one launch (start us, length us, event | category | flops | bytes accessed | tf_op | source)
XLA Modules:
  0.0 14.5 jit_solution(7936506638756364763)
XLA Ops:
  0.0 1.3 %z_pack.1 = (f32[4,64,128]{2,1,0:T(8,128)S(1)}, s32[4,64,128]{2,1,0:T(8,128)S(1)}, f32[4,64,128]{2,1,0:T(8,128)S(1)}, f32[4,64,128]{2,1,0:T(8,128)S(1)}, f32[4,6...) custom-call(f32[4,64,128]{2,1,0:T(8,128)} %refs_0_.1, ...), custom_call_target="tpu_custom_call" | custom-call | bytes 1048576 | tf_op jit(solution)/shard_map/z_pack/pallas_call | solution.py:406
  1.3 0.7 %collective-permute-start = (f32[16,128]{1,0:T(8,128)S(1)}, f32[16,128]{1,0:T(8,128)S(1)}, u32[]{:S(2)}, u32[]{:S(2)}) collective-permute-start(f32[16,128]{1,0:T(8,128)S(1)} %get-tuple-element.43), channel_id=1, source_target_pairs={{0,1},{1,0},{2,10},{3,11},{4,5},{5,4},{6,14},{7,15},{8,9},{9,8},{1... | collective-permute-start | bytes 24584 | tf_op jit(solution)/shard_map/ppermute | solution.py:425
  2.0 0.0 collective-permute-start.1
  2.0 1.4 %collective-permute-start.2 = (f32[16,128]{1,0:T(8,128)S(1)}, f32[16,128]{1,0:T(8,128)S(1)}, u32[]{:S(2)}, u32[]{:S(2)}) collective-permute-start(f32[16,128]{1,0:T(8,128)S(1)} %get-tuple-element.45), channel_id=1, source_target_pairs={{0,8},{1,9},{2,3},{3,2},{4,12},{5,13},{6,7},{7,6},{8,0},{9,1},{10,... | collective-permute-start | bytes 24584 | tf_op jit(solution)/shard_map/ppermute | solution.py:425
  3.4 0.0 copy-start
  3.4 0.0 copy-start.1
  3.4 1.1 %z_inner.1 = (f32[4,64,128]{2,1,0:T(8,128)S(1)}, f32[4,64,128]{2,1,0:T(8,128)S(1)}, f32[4,64,128]{2,1,0:T(8,128)S(1)}, f32[4,64,128]{2,1,0:T(8,128)S(1)}, f32[4,...) custom-call(f32[4,64,128]{2,1,0:T(8,128)S(1)} %get-tuple-element.34.g_re, ...), custom_call_target="tpu_custom_call" | custom-call | bytes 1048576 | tf_op jit(solution)/shard_map/z_inner/pallas_call | solution.py:406
  4.5 0.0 collective-permute-done.rest_0_
  4.5 0.0 collective-permute-done.1.rest_1_
  4.5 0.0 collective-permute-done.2.rest_2_
  4.6 0.0 copy-done
  4.6 0.0 copy-done.1
  4.6 0.2 %z_sweep.1 = (f32[16,128]{1,0:T(8,128)S(1)}, f32[4,8,128]{2,1,0:T(8,128)S(1)}) custom-call(f32[4,64,128]{2,1,0:T(8,128)S(1)} %get-tuple-element.38.partial.partial_z, f32[2,16,128]{2,1,0:T(8,128)S(1)} %get-tuple-element.39.edges, s32[4,64,128]{2,1,0:T(8,128)S(1)} %get-tuple-element.40.opened, f32[4,64,128]{2,1,0:T(8,128)S(1)} %get-tuple-element.41.ay, ...), custom_call_target="tpu_custom_call" | custom-call | bytes 1048576 | tf_op jit(solution)/shard_map/z_sweep/pallas_call | solution.py:406
  4.8 0.3 %collective-permute-start.3 = (f32[4,8,128]{2,1,0:T(8,128)S(1)}, f32[4,8,128]{2,1,0:T(8,128)S(1)}, u32[]{:S(2)}, u32[]{:S(2)}) collective-permute-start(f32[4,8,128]{2,1,0:T(8,128)S(1)} %get-tuple-element.54), channel_id=1, source_target_pairs={{0,4},{1,5},{2,6},{3,7},{4,0},{5,1},{6,2},{7,3},{8,12},{9,13},{10,... | collective-permute-start | bytes 49160 | tf_op jit(solution)/shard_map/ppermute | solution.py:425
  5.1 0.2 %y_inner.1 = (f32[4,64,128]{2,1,0:T(8,128)S(1)}, f32[4,8,128]{2,1,0:T(8,128)S(1)}, f32[296,128]{1,0:T(8,128)S(1)}, f32[296,128]{1,0:T(8,128)S(1)}) custom-call(f32[4,64,128]{2,1,0:T(8,128)S(1)} %get-tuple-element.38.partial.partial_z, f32[16,128]{1,0:T(8,128)S(1)} %get-tuple-element.46.ends_ref, s32[4,64,128]{2,1,0:T(8,128)S(1)} %get-tuple-element.40.opened, ...), custom_call_target="tpu_custom_call" | custom-call | bytes 1048576 | tf_op jit(solution)/shard_map/y_inner/pallas_call | solution.py:406
  5.3 3.4 %collective-permute-start.4 = (f32[296,128]{1,0:T(8,128)S(1)}, f32[296,128]{1,0:T(8,128)S(1)}, u32[]{:S(2)}, u32[]{:S(2)}) collective-permute-start(f32[296,128]{1,0:T(8,128)S(1)} %get-tuple-element.59), channel_id=1, source_target_pairs={{0,4},{1,5},{2,6},{3,7},{4,0},{5,1},{6,2},{7,3},{8,16},{9,17},{10,... | collective-permute-start | bytes 454664 | tf_op jit(solution)/shard_map/ppermute | solution.py:425
  8.7 0.4 %collective-permute-start.5 = (f32[296,128]{1,0:T(8,128)S(1)}, f32[296,128]{1,0:T(8,128)S(1)}, u32[]{:S(2)}, u32[]{:S(2)}) collective-permute-start(f32[296,128]{1,0:T(8,128)S(1)} %get-tuple-element.60), channel_id=1, source_target_pairs={{0,8},{1,9},{2,10},{3,11},{4,12},{5,13},{6,14},{7,15},{8,0},{9,1},... | collective-permute-start | bytes 454664 | tf_op jit(solution)/shard_map/ppermute | solution.py:425
  9.2 0.0 collective-permute-done.3.rest_0_
  9.2 0.1 y_sweep.1
  9.3 2.6 %collective-permute-start.6 = (f32[40,128]{1,0:T(8,128)S(1)}, f32[40,128]{1,0:T(8,128)S(1)}, u32[]{:S(2)}, u32[]{:S(2)}) collective-permute-start(f32[40,128]{1,0:T(8,128)S(1)} %get-tuple-element.61), channel_id=1, source_target_pairs={{0,24},{1,25},{2,26},{3,27},{4,28},{5,29},{6,30},{7,31},{8,16},{9,... | collective-permute-start | bytes 61448 | tf_op jit(solution)/shard_map/ppermute | solution.py:425
  11.8 0.0 collective-permute-start.7
  11.8 0.1 x_inner.1
  11.9 1.8 %collective-permute-done.6.rest_2_ = f32[40,128]{1,0:T(8,128)S(1)} collective-permute-done((f32[40,128]{1,0:T(8,128)S(1)}, f32[40,128]{1,0:T(8,128)S(1)}, u32[]{:S(2)}, u32[]{:S(2)}) %collective-permute-start.6) | collective-permute-done | bytes 20512 | tf_op jit(solution)/shard_map/ppermute | solution.py:425
  13.7 0.0 collective-permute-done.7.rest_3_
  13.7 0.0 collective-permute-done.4.rest_0_
  13.7 0.0 collective-permute-done.5.rest_1_
  13.7 0.8 %x_sweep.1 = f32[4,64,128]{2,1,0:T(8,128)} custom-call(f32[4,64,128]{2,1,0:T(8,128)S(1)} %get-tuple-element.55.g_ref, f32[4,64,128]{2,1,0:T(8,128)S(1)} %copy-done, f32[4,64,128]{2,1,0:T(8,128)S(1)} %copy-done.1, f32[4,64,128]{2,1,0:T(8,128)S(1)} %get-tuple-element.56.ready, f32[2,64,128]{2,1,0:T(8,128)S(1)} %get-tuple-element.57.own_ref, ...), custom_call_target="tpu_custom_call" | custom-call | bytes 1048576 | tf_op jit(solution)/shard_map/x_sweep/pallas_call | solution.py:406
Async XLA Ops:
  1.3 3.3 %collective-permute-start = (f32[16,128]{1,0:T(8,128)S(1)}, f32[16,128]{1,0:T(8,128)S(1)}, u32[]{:S(2)}, u32[]{:S(2)}) collective-permute-start(f32[16,128]{1,0:T(8,128)S(1)} %get-tuple-element.43), channel_id=1, source_target_pairs={{0,1},{1,0},{2,10},{3,11},{4,5},{5,4},{6,14},{7,15},{8,9},{9,8},{1... | collective-permute-start | bytes 24584 | tf_op jit(solution)/shard_map/ppermute | solution.py:425
  2.0 2.5 %collective-permute-start.1 = (f32[16,128]{1,0:T(8,128)S(1)}, f32[16,128]{1,0:T(8,128)S(1)}, u32[]{:S(2)}, u32[]{:S(2)}) collective-permute-start(f32[16,128]{1,0:T(8,128)S(1)} %get-tuple-element.44), channel_id=1, source_target_pairs={{0,8},{1,2},{2,1},{3,11},{4,12},{5,6},{6,5},{7,15},{8,0},{9,10},{1... | collective-permute-start | bytes 24584 | tf_op jit(solution)/shard_map/ppermute | solution.py:425
  2.0 2.5 %collective-permute-start.2 = (f32[16,128]{1,0:T(8,128)S(1)}, f32[16,128]{1,0:T(8,128)S(1)}, u32[]{:S(2)}, u32[]{:S(2)}) collective-permute-start(f32[16,128]{1,0:T(8,128)S(1)} %get-tuple-element.45), channel_id=1, source_target_pairs={{0,8},{1,9},{2,3},{3,2},{4,12},{5,13},{6,7},{7,6},{8,0},{9,1},{10,... | collective-permute-start | bytes 24584 | tf_op jit(solution)/shard_map/ppermute | solution.py:425
  3.4 1.2 %copy-start = (f32[4,64,128]{2,1,0:T(8,128)S(1)}, f32[4,64,128]{2,1,0:T(8,128)}, u32[]{:S(2)}) copy-start(f32[4,64,128]{2,1,0:T(8,128)} %ax.7) | copy-start | bytes 393220
  3.4 1.2 %copy-start.1 = (f32[4,64,128]{2,1,0:T(8,128)S(1)}, f32[4,64,128]{2,1,0:T(8,128)}, u32[]{:S(2)}) copy-start(f32[4,64,128]{2,1,0:T(8,128)} %cx.9) | copy-start | bytes 393220
  4.8 4.4 %collective-permute-start.3 = (f32[4,8,128]{2,1,0:T(8,128)S(1)}, f32[4,8,128]{2,1,0:T(8,128)S(1)}, u32[]{:S(2)}, u32[]{:S(2)}) collective-permute-start(f32[4,8,128]{2,1,0:T(8,128)S(1)} %get-tuple-element.54), channel_id=1, source_target_pairs={{0,4},{1,5},{2,6},{3,7},{4,0},{5,1},{6,2},{7,3},{8,12},{9,13},{10,... | collective-permute-start | bytes 49160 | tf_op jit(solution)/shard_map/ppermute | solution.py:425
  5.3 8.4 %collective-permute-start.4 = (f32[296,128]{1,0:T(8,128)S(1)}, f32[296,128]{1,0:T(8,128)S(1)}, u32[]{:S(2)}, u32[]{:S(2)}) collective-permute-start(f32[296,128]{1,0:T(8,128)S(1)} %get-tuple-element.59), channel_id=1, source_target_pairs={{0,4},{1,5},{2,6},{3,7},{4,0},{5,1},{6,2},{7,3},{8,16},{9,17},{10,... | collective-permute-start | bytes 454664 | tf_op jit(solution)/shard_map/ppermute | solution.py:425
  8.7 5.0 %collective-permute-start.5 = (f32[296,128]{1,0:T(8,128)S(1)}, f32[296,128]{1,0:T(8,128)S(1)}, u32[]{:S(2)}, u32[]{:S(2)}) collective-permute-start(f32[296,128]{1,0:T(8,128)S(1)} %get-tuple-element.60), channel_id=1, source_target_pairs={{0,8},{1,9},{2,10},{3,11},{4,12},{5,13},{6,14},{7,15},{8,0},{9,1},... | collective-permute-start | bytes 454664 | tf_op jit(solution)/shard_map/ppermute | solution.py:425
  9.3 4.5 %collective-permute-start.6 = (f32[40,128]{1,0:T(8,128)S(1)}, f32[40,128]{1,0:T(8,128)S(1)}, u32[]{:S(2)}, u32[]{:S(2)}) collective-permute-start(f32[40,128]{1,0:T(8,128)S(1)} %get-tuple-element.61), channel_id=1, source_target_pairs={{0,24},{1,25},{2,26},{3,27},{4,28},{5,29},{6,30},{7,31},{8,16},{9,... | collective-permute-start | bytes 61448 | tf_op jit(solution)/shard_map/ppermute | solution.py:425
  11.8 1.9 %collective-permute-start.7 = (f32[40,128]{1,0:T(8,128)S(1)}, f32[40,128]{1,0:T(8,128)S(1)}, u32[]{:S(2)}, u32[]{:S(2)}) collective-permute-start(f32[40,128]{1,0:T(8,128)S(1)} %get-tuple-element.62), channel_id=1, source_target_pairs={{0,8},{1,9},{2,10},{3,11},{4,12},{5,13},{6,14},{7,15},{8,0},{9,1},... | collective-permute-start | bytes 61448 | tf_op jit(solution)/shard_map/ppermute | solution.py:425
